TPU v7x, 32 devices: a whole 2x2x4 slice. The times are simulated.
32 devices in a mesh: fsdp: 32 (over z, y, x, core).
Axes of the slice: x: 2, y: 2, z: 4, core: 2. Of those that a mesh axis runs over, the one named last changes fastest.
Arguments:
- images: bfloat16 [96, 197, 384], P('fsdp'), may hold values from -6 to 6
- live_counts: int32 [96], P('fsdp'), may hold values from 0 to 1, as said below
- qkv_weight: bfloat16 [2, 442368], P(None, 'fsdp'), may hold values from -0.3125 to 0.3125
- out_weight: bfloat16 [2, 147456], P(None, 'fsdp'), may hold values from -2.5 to 2.5
- fc1_weight: bfloat16 [2, 589824], P(None, 'fsdp'), may hold values from -0.3125 to 0.3125
- fc2_weight: bfloat16 [2, 589824], P(None, 'fsdp'), may hold values from -0.21875 to 0.21875
- norm_gains: bfloat16 [2, 768], P(None, 'fsdp'), may hold values from 0.099609375 to 1.8984375
- biases: bfloat16 [2, 3840], P(None, 'fsdp'), may hold values from -3 to 3
- cotangent: bfloat16 [96, 197, 384], P('fsdp'), may hold values from -6 to 6
Outputs:
- activations: bfloat16 [96, 197, 384], P('fsdp')
- input_grad: bfloat16 [96, 197, 384], P('fsdp')
- qkv_grad: float32 [2, 442368], P(None, 'fsdp')
- out_grad: float32 [2, 147456], P(None, 'fsdp')
- fc1_grad: float32 [2, 589824], P(None, 'fsdp')
- fc2_grad: float32 [2, 589824], P(None, 'fsdp')
- gain_grad: float32 [2, 768], P(None, 'fsdp')
- bias_grad: float32 [2, 3840], P(None, 'fsdp')
Inputs may be any that keep to these rules, and one draw needn't show every extreme that they name: Slot s of micro-batch b on device d is live when s < live_counts[d * 3 + b]; dead slots give zero outputs and no gradient. Some micro-batch is full in every draw.
All inputs are finite; a program needn't handle non-finite values.
Results may differ from a plain program's by a relative error of at most 0.015.
Values may be sent and summed in bfloat16 or wider, within the bound.
No kernel may reach another device: no remote copies, remote signals or barrier semaphores. Data moves between devices by JAX's collectives and lax.ppermute only.
A program may use at most 128 MiB of HBM per device.

v0:
```python
import jax
import jax.numpy as jnp
from jax import lax
from jax.sharding import PartitionSpec as P

D = 384
HEADS = 6
FF = 1536
SEQ = 197
HEAD = 64
LAYERS = 2
MB = 3
SLOTS = 1


norm_eps = 1e-06
root_half = 0.7071067811865476
inv_root_tau = 0.3989422804014327


def norm_forward(values, gain_row, shift_row):
    centre = jnp.mean(values, axis=-1, keepdims=True)
    centred = values - centre
    spread = jnp.mean(centred * centred, axis=-1, keepdims=True)
    inv_std = lax.rsqrt(spread + norm_eps)
    normal = centred * inv_std
    return (normal * gain_row + shift_row, normal, inv_std)


def norm_backward(grad_norm, gain_row, normal, inv_std):
    scaled = grad_norm * gain_row
    first_mean = jnp.mean(scaled, axis=-1, keepdims=True)
    cross_mean = jnp.mean(scaled * normal, axis=-1, keepdims=True)
    return inv_std * (scaled - first_mean - normal * cross_mean)


def gelu_value(values):
    return 0.5 * values * (1.0 + lax.erf(values * root_half))


def gelu_slope(values):
    return (
        0.5 * (1.0 + lax.erf(values * root_half))
        + values * jnp.exp(-0.5 * values * values) * inv_root_tau
    )


def column_total(values):
    return jnp.sum(values.astype(jnp.float32), axis=0)


def outer_sum(left_rows, right_rows):
    return jnp.einsum("ri,rj->ij", left_rows, right_rows, preferred_element_type=jnp.float32)


def back_product(grad_rows, matrix):
    return jnp.einsum("rj,ij->ri", grad_rows, matrix, preferred_element_type=jnp.float32)


def unpack(params):
    qkv_flat, out_flat, fc1_flat, fc2_flat, gain_vec, shifts = params
    return (
        qkv_flat.reshape(D, 3 * D),
        out_flat.reshape(D, D),
        fc1_flat.reshape(D, FF),
        fc2_flat.reshape(FF, D),
        gain_vec.astype(jnp.float32),
        shifts.astype(jnp.float32),
    )


def split_heads(qkv_low, image_count):
    shaped = qkv_low.reshape(image_count, SEQ, 3, HEADS, HEAD)
    return (shaped[:, :, 0], shaped[:, :, 1], shaped[:, :, 2])


def attention_scores(queries, keys_part):
    score_scale = HEAD ** (-0.5)
    return (
        jnp.einsum("bqhe,bkhe->bhqk", queries, keys_part, preferred_element_type=jnp.float32)
        * score_scale
    )


def owner_major(stacked, owners):
    return jnp.transpose(stacked.reshape(LAYERS, owners, -1), (1, 0, 2)).reshape(-1)


def layer_forward(stream, params):
    qkv_mat, out_mat, fc1_mat, fc2_mat, gain_vec, shifts = unpack(params)
    image_count = stream.shape[0]
    token_rows = stream.reshape(-1, D)
    normed, normal_a, inv_a = norm_forward(token_rows, gain_vec[:D], shifts[:D])
    normed_low = normed.astype(jnp.bfloat16)
    qkv_bias = jnp.concatenate(
        [shifts[D : 2 * D], jnp.zeros((D,), jnp.float32), shifts[2 * D : 3 * D]]
    )
    qkv_low = (jnp.dot(normed_low, qkv_mat, preferred_element_type=jnp.float32) + qkv_bias).astype(
        jnp.bfloat16
    )
    queries, keys_part, values_part = split_heads(qkv_low, image_count)
    scores = attention_scores(queries, keys_part)
    row_peak = jnp.max(scores, axis=-1, keepdims=True)
    raised = jnp.exp(scores - row_peak)
    totals = jnp.sum(raised, axis=-1, keepdims=True)
    log_total = row_peak + jnp.log(totals)
    probs_low = (raised / totals).astype(jnp.bfloat16)
    mixed_full = jnp.einsum(
        "bhqk,bkhe->bqhe", probs_low, values_part, preferred_element_type=jnp.float32
    )
    mixed_low = mixed_full.reshape(-1, D).astype(jnp.bfloat16)
    middle = token_rows + (
        jnp.dot(mixed_low, out_mat, preferred_element_type=jnp.float32) + shifts[3 * D : 4 * D]
    )
    normed_two, normal_b, inv_b = norm_forward(middle, gain_vec[D:], shifts[4 * D : 5 * D])
    normed_two_low = normed_two.astype(jnp.bfloat16)
    pre_act = jnp.dot(normed_two_low, fc1_mat, preferred_element_type=jnp.float32) + shifts[6 * D :]
    act_low = gelu_value(pre_act).astype(jnp.bfloat16)
    result = middle + (
        jnp.dot(act_low, fc2_mat, preferred_element_type=jnp.float32) + shifts[5 * D : 6 * D]
    )
    kept_state = (
        normal_a,
        inv_a,
        normed_low,
        qkv_low,
        log_total,
        mixed_low,
        normal_b,
        inv_b,
        normed_two_low,
        pre_act,
        act_low,
    )
    return (result.reshape(stream.shape), kept_state)


def layer_backward(grad_rows, params, kept_state, image_count):
    qkv_mat, out_mat, fc1_mat, fc2_mat, gain_vec, shifts = unpack(params)
    (
        normal_a,
        inv_a,
        normed_low,
        qkv_low,
        log_total,
        mixed_low,
        normal_b,
        inv_b,
        normed_two_low,
        pre_act,
        act_low,
    ) = kept_state
    score_scale = HEAD ** (-0.5)
    grad_low = grad_rows.astype(jnp.bfloat16)
    fc2_term = outer_sum(act_low, grad_low)
    bias_fc2 = column_total(grad_low)
    grad_pre = (back_product(grad_low, fc2_mat) * gelu_slope(pre_act)).astype(jnp.bfloat16)
    fc1_term = outer_sum(normed_two_low, grad_pre)
    bias_fc1 = column_total(grad_pre)
    grad_norm_two = back_product(grad_pre, fc1_mat)
    gain_two = jnp.sum(grad_norm_two * normal_b, axis=0)
    shift_two = jnp.sum(grad_norm_two, axis=0)
    grad_middle = grad_rows + norm_backward(grad_norm_two, gain_vec[D:], normal_b, inv_b)
    middle_low = grad_middle.astype(jnp.bfloat16)
    out_term = outer_sum(mixed_low, middle_low)
    bias_out = column_total(middle_low)
    grad_mixed = (
        back_product(middle_low, out_mat)
        .astype(jnp.bfloat16)
        .reshape(image_count, SEQ, HEADS, HEAD)
    )
    queries, keys_part, values_part = split_heads(qkv_low, image_count)
    probs_full = jnp.exp(attention_scores(queries, keys_part) - log_total)
    grad_values = jnp.einsum(
        "bhqk,bqhe->bkhe",
        probs_full.astype(jnp.bfloat16),
        grad_mixed,
        preferred_element_type=jnp.float32,
    )
    grad_probs = jnp.einsum(
        "bqhe,bkhe->bhqk", grad_mixed, values_part, preferred_element_type=jnp.float32
    )
    row_dot = jnp.sum(probs_full * grad_probs, axis=-1, keepdims=True)
    grad_scores = (probs_full * (grad_probs - row_dot)).astype(jnp.bfloat16)
    grad_queries = (
        jnp.einsum("bhqk,bkhe->bqhe", grad_scores, keys_part, preferred_element_type=jnp.float32)
        * score_scale
    )
    grad_keys = (
        jnp.einsum("bhqk,bqhe->bkhe", grad_scores, queries, preferred_element_type=jnp.float32)
        * score_scale
    )
    grad_qkv = (
        jnp.stack([grad_queries, grad_keys, grad_values], axis=2)
        .reshape(-1, 3 * D)
        .astype(jnp.bfloat16)
    )
    qkv_term = outer_sum(normed_low, grad_qkv)
    qkv_bias_sum = column_total(grad_qkv)
    grad_norm_one = back_product(grad_qkv, qkv_mat)
    gain_one = jnp.sum(grad_norm_one * normal_a, axis=0)
    shift_one = jnp.sum(grad_norm_one, axis=0)
    grad_input = grad_middle + norm_backward(grad_norm_one, gain_vec[:D], normal_a, inv_a)
    gain_term = jnp.concatenate([gain_one, gain_two])
    bias_term = jnp.concatenate(
        [
            shift_one,
            qkv_bias_sum[:D],
            qkv_bias_sum[2 * D :],
            bias_out,
            shift_two,
            bias_fc2,
            bias_fc1,
        ]
    )
    grad_terms = (
        qkv_term.reshape(-1),
        out_term.reshape(-1),
        fc1_term.reshape(-1),
        fc2_term.reshape(-1),
        gain_term,
        bias_term,
    )
    return (grad_input, grad_terms)


def local(
    images,
    live_counts,
    qkv_weight,
    out_weight,
    fc1_weight,
    fc2_weight,
    norm_gains,
    biases,
    cotangent,
):
    owners = lax.axis_size("fsdp")
    grad_sums = [None] * LAYERS
    act_parts = []
    input_parts = []
    for batch_idx in range(MB):
        first_slot = batch_idx * SLOTS
        stream = images[first_slot : first_slot + SLOTS].astype(jnp.float32)
        live_rows = (lax.iota(jnp.int32, SLOTS) < live_counts[batch_idx]).astype(jnp.float32)[
            :, None, None
        ]
        layer_states = []
        for layer_idx in range(LAYERS):
            stream, kept_state = layer_forward(
                stream,
                (
                    lax.all_gather(qkv_weight[layer_idx], "fsdp", axis=0, tiled=True),
                    lax.all_gather(out_weight[layer_idx], "fsdp", axis=0, tiled=True),
                    lax.all_gather(fc1_weight[layer_idx], "fsdp", axis=0, tiled=True),
                    lax.all_gather(fc2_weight[layer_idx], "fsdp", axis=0, tiled=True),
                    lax.all_gather(norm_gains[layer_idx], "fsdp", axis=0, tiled=True),
                    lax.all_gather(biases[layer_idx], "fsdp", axis=0, tiled=True),
                ),
            )
            layer_states.append(kept_state)
        act_parts.append((stream * live_rows).astype(jnp.bfloat16))
        grad_rows = (
            cotangent[first_slot : first_slot + SLOTS].astype(jnp.float32) * live_rows
        ).reshape(-1, D)
        for layer_idx in reversed(range(LAYERS)):
            grad_rows, grad_terms = layer_backward(
                grad_rows,
                (
                    lax.all_gather(qkv_weight[layer_idx], "fsdp", axis=0, tiled=True),
                    lax.all_gather(out_weight[layer_idx], "fsdp", axis=0, tiled=True),
                    lax.all_gather(fc1_weight[layer_idx], "fsdp", axis=0, tiled=True),
                    lax.all_gather(fc2_weight[layer_idx], "fsdp", axis=0, tiled=True),
                    lax.all_gather(norm_gains[layer_idx], "fsdp", axis=0, tiled=True),
                    lax.all_gather(biases[layer_idx], "fsdp", axis=0, tiled=True),
                ),
                layer_states[layer_idx],
                SLOTS,
            )
            if grad_sums[layer_idx] is None:
                grad_sums[layer_idx] = grad_terms
            else:
                grad_sums[layer_idx] = jax.tree.map(jnp.add, grad_sums[layer_idx], grad_terms)
        input_parts.append(grad_rows.reshape(SLOTS, SEQ, D).astype(jnp.bfloat16))
    stacked = tuple(
        (
            owner_major(
                jnp.stack([grad_sums[layer_idx][member] for layer_idx in range(LAYERS)]), owners
            )
            for member in range(6)
        )
    )
    summed = (
        lax.psum_scatter(stacked[0], "fsdp", scatter_dimension=0, tiled=True),
        lax.psum_scatter(stacked[1], "fsdp", scatter_dimension=0, tiled=True),
        lax.psum_scatter(stacked[2], "fsdp", scatter_dimension=0, tiled=True),
        lax.psum_scatter(stacked[3], "fsdp", scatter_dimension=0, tiled=True),
        lax.psum_scatter(stacked[4], "fsdp", scatter_dimension=0, tiled=True),
        lax.psum_scatter(stacked[5], "fsdp", scatter_dimension=0, tiled=True),
    )
    results = tuple((member.reshape(LAYERS, -1) for member in summed))
    activations = jnp.concatenate(act_parts, axis=0)
    input_grad = jnp.concatenate(input_parts, axis=0)
    return (
        activations,
        input_grad,
        results[0],
        results[1],
        results[2],
        results[3],
        results[4],
        results[5],
    )


def solution(mesh):
    in_specs = (
        P("fsdp", None, None),
        P("fsdp"),
        P(None, "fsdp"),
        P(None, "fsdp"),
        P(None, "fsdp"),
        P(None, "fsdp"),
        P(None, "fsdp"),
        P(None, "fsdp"),
        P("fsdp", None, None),
    )
    out_specs = (
        P("fsdp", None, None),
        P("fsdp", None, None),
        P(None, "fsdp"),
        P(None, "fsdp"),
        P(None, "fsdp"),
        P(None, "fsdp"),
        P(None, "fsdp"),
        P(None, "fsdp"),
    )
    return jax.shard_map(local, mesh=mesh, in_specs=in_specs, out_specs=out_specs, check_vma=False)
```

profile of v0, /device:TPU:0, one launch (start us, length us, event | category | flops | bytes accessed | tf_op | source)
XLA Modules:
  0.0 902.2 jit_solution(18207908684544974532)
XLA Ops:
  14.5 42.3 %all-reduce.12 = (bf16[3840]{0:T(1024)(128)(2,1)S(1)}, bf16[768]{0:T(1024)(128)(2,1)S(1)}, bf16[3840]{0:T(1024)(128)(2,1)S(1)}, bf16[768]{0:T(1024)(128)(2,1)S(1)}) all-reduce(bf16[3840]{0:T(1024)(128)(2,1)S(1)} %dynamic-update-slice.1, bf16[768]{0:T(1024)(128)(2,1)S(1)} %dynamic-update-slice, ...), channel_id=3, replica_groups=mesh['fsdp'=32] {'fsdp'}, use_global_device_ids=true, to_apply=%add.1 | all-reduce | flops 9216 | bytes 36864
  59.1 46.5 %all-gather.2 = bf16[1,442368]{1,0:T(2,128)(2,1)S(1)} all-gather(bf16[1,13824]{1,0:T(2,128)(2,1)S(1)} %get-tuple-element.136), channel_id=4, replica_groups=mesh['fsdp'=32] {'fsdp'}, dimensions={1}, use_global_device_ids=true | all-gather | bytes 912384 | tf_op jit(solution)/shard_map/all_gather | solution.py:253
  105.6 19.2 %reduce.47 = bf16[442368]{0:T(1024)(128)(2,1)} reduce(bf16[1,442368]{1,0:T(2,128)(2,1)S(1)} %all-gather.2, bf16[]{:T(256)} %constant.113), dimensions={0}, to_apply=%all-gather.2.reduce_sub_computation | reduce | bytes 1769474 | tf_op jit(solution)/shard_map/all_gather | solution.py:253
  135.4 38.8 %all-gather.3 = bf16[1,147456]{1,0:T(2,128)(2,1)S(1)} all-gather(bf16[1,4608]{1,0:T(2,128)(2,1)S(1)} %get-tuple-element.138), channel_id=5, replica_groups=mesh['fsdp'=32] {'fsdp'}, dimensions={1}, use_global_device_ids=true | all-gather | bytes 304128 | tf_op jit(solution)/shard_map/all_gather | solution.py:254
  174.2 6.1 reduce.50
  182.4 46.7 %all-gather.8 = bf16[1,442368]{1,0:T(2,128)(2,1)} all-gather(bf16[1,13824]{1,0:T(2,128)(2,1)S(1)} %get-tuple-element.135), channel_id=10, replica_groups=mesh['fsdp'=32] {'fsdp'}, dimensions={1}, use_global_device_ids=true | all-gather | bytes 912384 | tf_op jit(solution)/shard_map/all_gather | solution.py:253
  229.1 20.3 %reduce.60 = bf16[442368]{0:T(1024)(128)(2,1)} reduce(bf16[1,442368]{1,0:T(2,128)(2,1)} %all-gather.8, bf16[]{:T(256)} %constant.113), dimensions={0}, to_apply=%all-gather.8.reduce_sub_computation | reduce | bytes 1769474 | tf_op jit(solution)/shard_map/all_gather | solution.py:253
  251.5 39.7 %all-gather.9 = bf16[1,147456]{1,0:T(2,128)(2,1)S(1)} all-gather(bf16[1,4608]{1,0:T(2,128)(2,1)S(1)} %get-tuple-element.137), channel_id=11, replica_groups=mesh['fsdp'=32] {'fsdp'}, dimensions={1}, use_global_device_ids=true | all-gather | bytes 304128 | tf_op jit(solution)/shard_map/all_gather | solution.py:254
  291.3 6.8 reduce.63
  306.7 25.5 %reduce.56 = bf16[589824]{0:T(1024)(128)(2,1)S(1)} reduce(bf16[1,589824]{1,0:T(2,128)(2,1)} %all-gather.19.cloned.1.call-done, bf16[]{:T(256)} %constant.113), dimensions={0}, to_apply=%all-gather.5.reduce_sub_computation | reduce | bytes 2359298 | tf_op jit(solution)/shard_map/all_gather | solution.py:256
  333.7 26.7 %reduce.54 = bf16[589824]{0:T(1024)(128)(2,1)} reduce(bf16[1,589824]{1,0:T(2,128)(2,1)} %all-gather.17.cloned.1.call-done, bf16[]{:T(256)} %constant.113), dimensions={0}, to_apply=%all-gather.4.reduce_sub_computation | reduce | bytes 2359298 | tf_op jit(solution)/shard_map/all_gather | solution.py:255
  376.2 26.8 %reduce.67 = bf16[589824]{0:T(1024)(128)(2,1)} reduce(bf16[1,589824]{1,0:T(2,128)(2,1)} %all-gather.21.cloned.1.call-done, bf16[]{:T(256)} %constant.113), dimensions={0}, to_apply=%all-gather.10.reduce_sub_computation | reduce | bytes 2359298 | tf_op jit(solution)/shard_map/all_gather | solution.py:255
  414.6 26.6 %reduce.69 = bf16[589824]{0:T(1024)(128)(2,1)} reduce(bf16[1,589824]{1,0:T(2,128)(2,1)} %all-gather.23.cloned.1.call-done, bf16[]{:T(256)} %constant.113), dimensions={0}, to_apply=%all-gather.11.reduce_sub_computation | reduce | bytes 2359298 | tf_op jit(solution)/shard_map/all_gather | solution.py:256
  441.1 3.5 reshape.2207
  561.8 5.6 maximum_bitcast_fusion.2
  567.4 4.6 reshape.2235
  584.2 5.1 add.969
  594.5 4.9 add.968
  599.4 6.6 maximum_bitcast_fusion
  612.7 4.9 add.971
  622.0 4.9 add.970
  627.0 6.6 maximum_bitcast_fusion.1
  665.3 39.3 %all-reduce.10 = (f32[1536]{0:T(1024)}, f32[7680]{0:T(1024)S(1)}) all-reduce(f32[1536]{0:T(1024)} %reshape.2243, f32[7680]{0:T(1024)S(1)} %reshape.2245), channel_id=18, replica_groups=mesh['fsdp'=32] {'fsdp'}, use_global_device_ids=true, to_apply=%region_82.0.clone | all-reduce | flops 9216 | bytes 73728
  712.5 176.5 %all-reduce.15.cloned.1.call-done = (f32[884736]{0:T(1024)}, f32[294912]{0:T(1024)}, f32[1179648]{0:T(1024)}, f32[1179648]{0:T(1024)}) async-done(((f32[884736]{0:T(1024)}, f32[294912]{0:T(1024)}, f32[1179648]{0:T(1024)}, f32[1179648]{0:T(1024)}), (f32[884736]{0:T(1024)}, f32[294912]{0:T(1024)}, f32[1179648]{0:T(1024)}, f32[1179648]{0:T(1024)})) %all-reduce.15.cloned.1.call-update) | async-done | bytes 14155792
  (916 shorter events, 248.1 us)
Async XLA Ops:
  7.2 299.5 %all-gather.19.cloned.1.call-start = ((), (), s32[]{:S(2)}) async-start(), calls=%async_computation.1 | async-start | bytes 2433024 | tf_op jit(solution)/shard_map/all_gather | solution.py:256
  9.0 324.7 %all-gather.17.cloned.1.call-start = ((), (), s32[]{:S(2)}) async-start(), calls=%async_computation | async-start | bytes 2433024 | tf_op jit(solution)/shard_map/all_gather | solution.py:255
  10.8 365.4 %all-gather.21.cloned.1.call-start = ((), (), s32[]{:S(2)}) async-start(), calls=%async_computation.2 | async-start | bytes 2433024 | tf_op jit(solution)/shard_map/all_gather | solution.py:255
  11.5 403.0 %all-gather.23.cloned.1.call-start = ((), (), s32[]{:S(2)}) async-start(), calls=%async_computation.3 | async-start | bytes 2433024 | tf_op jit(solution)/shard_map/all_gather | solution.py:256
  12.1 876.9 %all-reduce.15.cloned.1.call-start = ((), (), s32[]{:S(2)}) async-start(), calls=%async_computation.4 | async-start | bytes 28311552
  58.1 74.5 %copy-start.159 = (f32[384]{0:T(512)}, f32[384]{0:T(512)S(1)}, u32[]{:S(2)}) copy-start(f32[384]{0:T(512)S(1)} %get-tuple-element.259) | copy-start | bytes 4612
  58.1 74.5 %copy-start.178 = (f32[384]{0:T(512)}, f32[384]{0:T(512)S(1)}, u32[]{:S(2)}) copy-start(f32[384]{0:T(512)S(1)} %get-tuple-element.79) | copy-start | bytes 4612
  58.1 122.3 %copy-start.182 = (f32[384]{0:T(512)}, f32[384]{0:T(512)S(1)}, u32[]{:S(2)}) copy-start(f32[384]{0:T(512)S(1)} %get-tuple-element.76) | copy-start | bytes 4612
  58.1 313.5 %copy-start.180 = (f32[384]{0:T(512)}, f32[384]{0:T(512)S(1)}, u32[]{:S(2)}) copy-start(f32[384]{0:T(512)S(1)} %get-tuple-element.80) | copy-start | bytes 4612
  127.7 245.2 %copy-start.157 = (f32[1152]{0:T(1024)}, f32[1152]{0:T(1024)S(1)}, u32[]{:S(2)}) copy-start(f32[1152]{0:T(1024)S(1)} %get-tuple-element.179) | copy-start | bytes 13828
  130.0 50.5 %copy-start.134 = (bf16[6,64,197]{2,1,0:T(8,128)(2,1)}, bf16[6,64,197]{2,1,0:T(8,128)(2,1)S(1)}, u32[]{:S(2)}) copy-start(bf16[6,64,197]{2,1,0:T(8,128)(2,1)S(1)} %convolution_convert_fusion.4) | copy-start | bytes 453892
  180.5 123.6 %copy-start.38 = (bf16[384,384]{1,0:T(8,128)(2,1)}, bf16[384,384]{1,0:T(8,128)(2,1)S(1)}, u32[]{:S(2)}) copy-start(bf16[384,384]{1,0:T(8,128)(2,1)S(1)} %reshape.2197) | copy-start | bytes 884740
  180.9 182.2 %copy-start.164 = (f32[197]{0:T(256)}, f32[197]{0:T(256)S(1)}, u32[]{:S(2)}) copy-start(f32[197]{0:T(256)S(1)} %broadcast_multiply_fusion.26) | copy-start | bytes 2368
  291.3 12.8 %copy-start.183 = (f32[384]{0:T(512)S(1)}, f32[384]{0:T(512)}, u32[]{:S(2)}) copy-start(f32[384]{0:T(512)} %copy-done.182) | copy-start | bytes 4612
  303.3 66.6 %copy-start.200 = (f32[197]{0:T(256)}, f32[197]{0:T(256)S(1)}, u32[]{:S(2)}) copy-start(f32[197]{0:T(256)S(1)} %broadcast_multiply_fusion.30) | copy-start | bytes 2368
  303.5 66.4 %copy-start.233 = (f32[197]{0:T(256)}, f32[197]{0:T(256)S(1)}, u32[]{:S(2)}) copy-start(f32[197]{0:T(256)S(1)} %add_rsqrt_fusion.6) | copy-start | bytes 2368
  304.5 27.7 %copy-start.166 = (f32[197]{0:T(256)}, f32[197]{0:T(256)S(1)}, u32[]{:S(2)}) copy-start(f32[197]{0:T(256)S(1)} %broadcast_multiply_fusion.34) | copy-start | bytes 2368
  376.1 34.0 %copy-start.161 = (f32[6,197]{1,0:T(8,128)}, f32[6,197]{1,0:T(8,128)S(1)}, u32[]{:S(2)}) copy-start(f32[6,197]{1,0:T(8,128)S(1)} %get-tuple-element.194) | copy-start | bytes 14188
  414.5 30.2 %copy-start.130 = (bf16[6,64,197]{2,1,0:T(8,128)(2,1)}, bf16[6,64,197]{2,1,0:T(8,128)(2,1)S(1)}, u32[]{:S(2)}) copy-start(bf16[6,64,197]{2,1,0:T(8,128)(2,1)S(1)} %convolution_convert_fusion.5) | copy-start | bytes 453892
  446.2 28.3 %copy-start.195 = (f32[197]{0:T(256)}, f32[197]{0:T(256)S(1)}, u32[]{:S(2)}) copy-start(f32[197]{0:T(256)S(1)} %broadcast_multiply_fusion.28) | copy-start | bytes 2368
  446.5 28.1 %copy-start.221 = (f32[197]{0:T(256)}, f32[197]{0:T(256)S(1)}, u32[]{:S(2)}) copy-start(f32[197]{0:T(256)S(1)} %add_rsqrt_fusion.4) | copy-start | bytes 2368
  462.7 9.9 %copy-start.65 = (f32[197,384]{1,0:T(8,128)}, f32[197,384]{1,0:T(8,128)S(1)}, u32[]{:S(2)}) copy-start(f32[197,384]{1,0:T(8,128)S(1)} %get-tuple-element.223) | copy-start | bytes 907780
  519.8 16.3 %copy-start.89 = (f32[197,384]{1,0:T(8,128)}, f32[197,384]{1,0:T(8,128)S(1)}, u32[]{:S(2)}) copy-start(f32[197,384]{1,0:T(8,128)S(1)} %get-tuple-element.104) | copy-start | bytes 907780
  642.6 64.2 %copy-start.13 = (bf16[1536,384]{1,0:T(8,128)(2,1)S(1)}, bf16[1536,384]{1,0:T(8,128)(2,1)}, u32[]{:S(2)}) copy-start(bf16[1536,384]{1,0:T(8,128)(2,1)} %reshape.2207) | copy-start | bytes 3538948
  (260 other events, 590.8 us)
Sparse Core Ops, SparseCore 0:
  11.5 60.4 all-gather.18
  74.8 56.4 all-gather.16
  134.8 58.1 all-gather.20
  196.3 56.9 all-gather.22
  642.7 246.2 all-reduce.14
where the time goes:
time: 908 us; the launch traced here: 902 us
  blocking collectives  253 us (28%)
  other arithmetic  200 us (22%)
  waiting for transfers between devices  178 us (20%)
  local copies, waits for them, and re-layouts  127 us (14%)
  matrix products  125 us (14%)
  between operations  19.5 us (2%)
    unnamed x6, waiting for transfers between devices  178 us
    all_gather x2, blocking collectives, local(): lax.all_gather(qkv_weight[layer_idx], 'fsdp', axis=0, tiled=True)  93.2 us
    unnamed x2, blocking collectives  81.6 us
    all_gather x2, blocking collectives, local(): lax.all_gather(out_weight[layer_idx], 'fsdp', axis=0, tiled=True)  78.5 us
    all_gather x2, other arithmetic, local(): lax.all_gather(fc1_weight[layer_idx], 'fsdp', axis=0, tiled=True)  53.5 us
    all_gather x2, other arithmetic, local(): lax.all_gather(fc2_weight[layer_idx], 'fsdp', axis=0, tiled=True)  52.1 us
    unnamed x612, local copies, waits for them, and re-layouts  43.1 us
    all_gather x2, other arithmetic, local(): lax.all_gather(qkv_weight[layer_idx], 'fsdp', axis=0, tiled=True)  39.5 us
  transfers between devices with their start and end apart: 5, of which 1 were waited for; matrix products, arithmetic and copies ran while one was open for 24% of the time, Pallas kernels for 0%

commit v1 on v0

v1 whole, which is shorter than its diff:
```python
import jax
import jax.numpy as jnp
from jax import lax
from jax.experimental import pallas as pl
from jax.experimental.pallas import tpu as pltpu
from jax.sharding import PartitionSpec as P

D = 384
FF = 1536
SEQ = 197
HEAD = 64
LAYERS = 2
NORM_EPS = 1e-06
ROOT_HALF = 0.7071067811865476
INV_ROOT_TAU = 0.3989422804014327

IMGS = 3
ROWS = 208
R = IMGS * ROWS
CHUNK = 48
CHUNKS = R // CHUNK
PAIRS = 3

SLABS = 32
SLAB = 448
THIRD = 144
SMALL = 432
BLOCKS = 8
QUAD = 4 * SLAB
SHARD_BIAS = 120
SHARD_GAIN = 24
BIAS = 6 * D + FF
GAIN = 2 * D

F32 = jnp.float32
BF16 = jnp.bfloat16
VMEM_LIMIT = 56 * 1024 * 1024


def dot_nn(a, b):
    return lax.dot_general(a, b, (((1,), (0,)), ((), ())), preferred_element_type=F32)


def dot_nt(a, b):
    return lax.dot_general(a, b, (((1,), (1,)), ((), ())), preferred_element_type=F32)


def dot_tn(a, b):
    return lax.dot_general(a, b, (((0,), (0,)), ((), ())), preferred_element_type=F32)


def chunk_rows(i):
    return pl.ds(pl.multiple_of(i * CHUNK, CHUNK), CHUNK)


def block_rows(j):
    return pl.ds(pl.multiple_of(j * D, D), D)


def image_rows(i):
    return pl.ds(pl.multiple_of(i * ROWS, 16), ROWS)


def pair_lanes(p):
    return pl.ds(pl.multiple_of(p * 128, 128), 128)


def normalize(x):
    centred = x - jnp.mean(x, axis=-1, keepdims=True)
    inv_std = lax.rsqrt(jnp.mean(centred * centred, axis=-1, keepdims=True) + NORM_EPS)
    return centred * inv_std, inv_std


def digits(index, size):
    whole = jnp.floor((index.astype(F32) + 0.5) * (1.0 / size)).astype(jnp.int32)
    return whole, index - whole * size


def order_codes(shape, axis, low):
    index = lax.broadcasted_iota(jnp.int32, shape, axis)
    block, rest = digits(index, 48)
    dev, row = digits(rest, 12)
    return (block * 4 + dev) * 12 + row


def slab_codes(shape, axis, low):
    index = lax.broadcasted_iota(jnp.int32, shape, axis)
    rel, rest = digits(index, 96)
    block, row = digits(rest, 12)
    dev = jnp.bitwise_xor(rel, low)
    return (block * 4 + dev) * 12 + row


def owner_mask(size, per_owner):
    lane = lax.broadcasted_iota(jnp.int32, (1, size), 1)
    owner, place = digits(lane, per_owner)
    rows = lax.broadcasted_iota(jnp.int32, (SLABS, size), 0)
    return rows == owner, place


def place_matrix(place, size):
    rows = lax.broadcasted_iota(jnp.int32, (128, size), 0)
    return jnp.where(rows == place, 1.0, 0.0).astype(BF16)


def assemble(me, pieces, w, w2, bias_row, gain_row, rhs, small):
    low = jnp.bitwise_and(me, 3)
    order = jnp.where(
        order_codes((D, 1), 0, low) == slab_codes((1, D), 1, low), 1.0, 0.0
    ).astype(BF16)

    def group(zr, carry):
        for yr in range(2):
            g = jnp.bitwise_xor(lax.shift_right_logical(me, 2), yr + 2 * zr)
            for xr in range(2):
                for cr in range(2):
                    piece = pieces[cr * 4 + xr + 2 * yr]
                    d = jnp.bitwise_xor(me, cr + 2 * xr + 4 * yr + 8 * zr)
                    base = pl.multiple_of(zr * SLAB, 16)
                    s = xr * 2 + cr
                    for c in range(3):
                        lanes = slice(128 * c, 128 * c + 128)
                        rhs[96 * s : 96 * s + 96, lanes] = piece[pl.ds(base + c * THIRD, 96), :]
                        w2[pl.ds(pl.multiple_of(48 * d, 16), 48), lanes] = piece[
                            pl.ds(base + c * THIRD + 96, 48), :
                        ]
                    tail = piece[pl.ds(base + SMALL, 16), :].astype(F32)
                    small[0, pl.ds(d, 1), :] = tail[0:1, :]
                    small[1, pl.ds(d, 1), :] = tail[1:2, :]
            sorted_rows = dot_nn(order, rhs[...]).astype(BF16)
            for b in range(BLOCKS):
                w[b, pl.ds(pl.multiple_of(48 * g, 16), 48), :] = sorted_rows[48 * b : 48 * b + 48]
        return carry

    lax.fori_loop(0, 4, group, 0)
    for slot, size, per_owner, row in ((0, BIAS, SHARD_BIAS, bias_row), (1, GAIN, SHARD_GAIN, gain_row)):
        mine, place = owner_mask(size, per_owner)
        spread = dot_nn(small[slot].astype(BF16), place_matrix(place, size))
        row[...] = jnp.sum(jnp.where(mine, spread, 0.0), axis=0, keepdims=True)


def disperse(me, dw, dw2, bias_row, gain_row, keep, send, rhs, small):
    low = jnp.bitwise_and(me, 3)
    order = jnp.where(
        slab_codes((D, 1), 0, low) == order_codes((1, D), 1, low), 1.0, 0.0
    ).astype(BF16)
    for slot, size, per_owner, row in ((0, BIAS, SHARD_BIAS, bias_row), (1, GAIN, SHARD_GAIN, gain_row)):
        mine, place = owner_mask(size, per_owner)
        spread = jnp.where(mine, row[...], 0.0).astype(BF16)
        small[slot] = dot_nt(spread, place_matrix(place, size))
    head_row = lax.broadcasted_iota(jnp.int32, (16, 128), 0)

    def group(zr, carry):
        for yr in range(2):
            g = jnp.bitwise_xor(lax.shift_right_logical(me, 2), yr + 2 * zr)
            for b in range(BLOCKS):
                rhs[48 * b : 48 * b + 48, :] = dw[b, pl.ds(pl.multiple_of(48 * g, 16), 48), :]
            slabs = dot_nn(order, rhs[...]).astype(BF16)
            for xr in range(2):
                for cr in range(2):
                    out = send if cr else keep
                    d = jnp.bitwise_xor(me, cr + 2 * xr + 4 * yr + 8 * zr)
                    base = pl.multiple_of((xr + 2 * yr) * QUAD + zr * SLAB, 16)
                    s = xr * 2 + cr
                    for c in range(3):
                        lanes = slice(128 * c, 128 * c + 128)
                        out[pl.ds(base + c * THIRD, 96), :] = slabs[96 * s : 96 * s + 96, lanes]
                        out[pl.ds(base + c * THIRD + 96, 48), :] = dw2[
                            pl.ds(pl.multiple_of(48 * d, 16), 48), lanes
                        ]
                    tail = jnp.where(
                        head_row == 0,
                        small[0, pl.ds(d, 1), :],
                        jnp.where(head_row == 1, small[1, pl.ds(d, 1), :], 0.0),
                    )
                    out[pl.ds(base + SMALL, 16), :] = tail.astype(BF16)
        return carry

    lax.fori_loop(0, 4, group, 0)


def forward(x, w, w2, bias_row, gain_row, xna, qkv, probs, mixed, middle, xnb, act, slope, tmp):
    def norm_a(i, carry):
        rows = chunk_rows(i)
        normal, _ = normalize(x[rows, :])
        xna[rows, :] = (normal * gain_row[:, :D] + bias_row[:, :D]).astype(BF16)
        return carry

    lax.fori_loop(0, CHUNKS, norm_a, 0)
    for b in range(3):
        part = dot_nn(xna[...], w[b])
        if b == 0:
            part = part + bias_row[:, D : 2 * D]
        if b == 2:
            part = part + bias_row[:, 2 * D : 3 * D]
        qkv[b] = part.astype(BF16)

    lane = lax.broadcasted_iota(jnp.int32, (1, 128), 1)
    first = lane < HEAD
    halves = (first.astype(F32).astype(BF16), 1 - first.astype(F32).astype(BF16))
    real_key = lax.broadcasted_iota(jnp.int32, (1, ROWS), 1) < SEQ

    def image_attention(img, carry):
        rows = image_rows(img)

        def pair_attention(pair, inner):
            lanes = pair_lanes(pair)
            q, k, v = qkv[0, rows, lanes], qkv[1, rows, lanes], qkv[2, rows, lanes]
            outs = []
            for h in range(2):
                scores = dot_nt(q * halves[h], k) * (HEAD**-0.5)
                scores = jnp.where(real_key, scores, -1e30)
                raised = jnp.exp(scores - jnp.max(scores, axis=-1, keepdims=True))
                share = raised * (1.0 / jnp.sum(raised, axis=-1, keepdims=True))
                share = share.astype(BF16)
                probs[(img * PAIRS + pair) * 2 + h] = share
                outs.append(dot_nn(share, v))
            mixed[rows, lanes] = jnp.where(first, outs[0], outs[1]).astype(BF16)
            return inner

        return lax.fori_loop(0, PAIRS, pair_attention, carry)

    lax.fori_loop(0, IMGS, image_attention, 0)
    middle[...] = x[...] + (dot_nn(mixed[...], w[3]) + bias_row[:, 3 * D : 4 * D])

    def norm_b(i, carry):
        rows = chunk_rows(i)
        normal, _ = normalize(middle[rows, :])
        xnb[rows, :] = (normal * gain_row[:, D:] + bias_row[:, 4 * D : 5 * D]).astype(BF16)
        return carry

    lax.fori_loop(0, CHUNKS, norm_b, 0)

    def hidden(j, carry):
        tmp[...] = dot_nn(xnb[...], w[4 + j])
        shift = bias_row[:, pl.ds(pl.multiple_of(6 * D + j * D, 128), D)]

        def gelu(i, inner):
            rows = chunk_rows(i)
            pre = tmp[rows, :] + shift
            half = 0.5 * (1.0 + lax.erf(pre * ROOT_HALF))
            act[j, rows, :] = (pre * half).astype(BF16)
            slope[j, rows, :] = (half + pre * jnp.exp(-0.5 * pre * pre) * INV_ROOT_TAU).astype(BF16)
            return inner

        return lax.fori_loop(0, CHUNKS, gelu, carry)

    lax.fori_loop(0, 4, hidden, 0)
    tmp[...] = middle[...] + bias_row[:, 5 * D : 6 * D]
    for j in range(4):
        tmp[...] += dot_nn(act[j], w2[D * j : D * j + D, :])


def column_total(values):
    return jnp.sum(values.astype(F32), axis=0, keepdims=True)


def backward(
    x, w, w2, gain_row, xna, qkv, probs, mixed, middle, xnb, act, slope, grad, low, gpre, gqkv, gmix, tmp, dw, dw2, dbias, dgain
):
    low[...] = grad[...].astype(BF16)
    dbias[:, 5 * D : 6 * D] = column_total(low[...])

    def hidden(j, carry):
        dw2[block_rows(j), :] = dot_tn(act[j], low[...]).astype(BF16)
        pre = (dot_nt(low[...], w2[block_rows(j), :]) * slope[j].astype(F32)).astype(BF16)
        gpre[...] = pre
        dbias[:, pl.ds(pl.multiple_of(6 * D + j * D, 128), D)] = column_total(gpre[...])
        dw[4 + j] = dot_tn(xnb[...], gpre[...]).astype(BF16)
        part = dot_nt(gpre[...], w[4 + j])
        tmp[...] = jnp.where(j == 0, part, tmp[...] + part)
        return carry

    lax.fori_loop(0, 4, hidden, 0)

    def norm_back(source, gain, also_low):
        def step(i, totals):
            rows = chunk_rows(i)
            back = tmp[rows, :]
            normal, inv_std = normalize(source[rows, :])
            scaled = back * gain
            first_mean = jnp.mean(scaled, axis=-1, keepdims=True)
            cross_mean = jnp.mean(scaled * normal, axis=-1, keepdims=True)
            result = grad[rows, :] + inv_std * (scaled - first_mean - normal * cross_mean)
            grad[rows, :] = result
            result_low = result.astype(BF16)
            if also_low:
                low[rows, :] = result_low
            return (
                totals[0] + jnp.sum(back * normal, axis=0, keepdims=True),
                totals[1] + jnp.sum(back, axis=0, keepdims=True),
                totals[2] + jnp.sum(result_low.astype(F32), axis=0, keepdims=True),
            )

        zero = jnp.zeros((1, D), F32)
        return lax.fori_loop(0, CHUNKS, step, (zero, zero, zero))

    gain_two, shift_two, bias_out = norm_back(middle, gain_row[:, D:], True)
    dgain[:, D:] = gain_two
    dbias[:, 4 * D : 5 * D] = shift_two
    dbias[:, 3 * D : 4 * D] = bias_out
    dw[3] = dot_tn(mixed[...], low[...]).astype(BF16)
    gmix[...] = dot_nt(low[...], w[3]).astype(BF16)

    lane = lax.broadcasted_iota(jnp.int32, (1, 128), 1)
    first = lane < HEAD
    halves = (first.astype(F32).astype(BF16), 1 - first.astype(F32).astype(BF16))

    def image_attention(img, carry):
        rows = image_rows(img)

        def pair_attention(pair, inner):
            lanes = pair_lanes(pair)
            q, k, v = qkv[0, rows, lanes], qkv[1, rows, lanes], qkv[2, rows, lanes]
            gm = gmix[rows, lanes]
            grads = ([], [], [])
            for h in range(2):
                share = probs[(img * PAIRS + pair) * 2 + h]
                grad_share = dot_nt(gm * halves[h], v)
                full = share.astype(F32)
                row_dot = jnp.sum(full * grad_share, axis=-1, keepdims=True)
                grad_scores = (full * (grad_share - row_dot)).astype(BF16)
                grads[0].append(dot_nn(grad_scores, k) * (HEAD**-0.5))
                grads[1].append(dot_tn(grad_scores, q) * (HEAD**-0.5))
                grads[2].append(dot_tn(share, gm))
            for b in range(3):
                gqkv[b, rows, lanes] = jnp.where(first, grads[b][0], grads[b][1]).astype(BF16)
            return inner

        return lax.fori_loop(0, PAIRS, pair_attention, carry)

    lax.fori_loop(0, IMGS, image_attention, 0)
    for b in range(3):
        dw[b] = dot_tn(xna[...], gqkv[b]).astype(BF16)
        part = dot_nt(gqkv[b], w[b])
        tmp[...] = part if b == 0 else tmp[...] + part
    dbias[:, D : 2 * D] = column_total(gqkv[0])
    dbias[:, 2 * D : 3 * D] = column_total(gqkv[2])
    gain_one, shift_one, _ = norm_back(x, gain_row[:, :D], False)
    dgain[:, :D] = gain_one
    dbias[:, :D] = shift_one


def load_images(images, x):
    x[...] = jnp.zeros_like(x)
    for i in range(IMGS):
        x[ROWS * i : ROWS * i + SEQ, :] = images[i].astype(F32)


STATE = (
    ((R, D), BF16),
    ((3, R, D), BF16),
    ((IMGS * PAIRS * 2, ROWS, ROWS), BF16),
    ((R, D), BF16),
    ((R, D), F32),
    ((R, D), BF16),
    ((4, R, D), BF16),
    ((4, R, D), BF16),
)
WEIGHTS = (
    ((BLOCKS, D, D), BF16),
    ((FF, D), BF16),
    ((1, BIAS), F32),
    ((1, GAIN), F32),
)
GRAD_SCRATCH = (
    ((R, D), BF16),
    ((R, D), BF16),
    ((3, R, D), BF16),
    ((R, D), BF16),
    ((R, D), F32),
    ((BLOCKS, D, D), BF16),
    ((FF, D), BF16),
    ((1, BIAS), F32),
    ((1, GAIN), F32),
)
MOVE_SCRATCH = (((D, D), BF16), ((2, SLABS, 128), F32))
WIRE = jax.ShapeDtypeStruct((4 * QUAD, 128), BF16)


def shapes(specs):
    return [jax.ShapeDtypeStruct(*spec) for spec in specs]


def scratch(specs):
    return [pltpu.VMEM(*spec) for spec in specs]


def first_forward_kernel(*refs):
    me, images, pieces, refs = refs[0][0], refs[1], refs[2:10], refs[10:]
    stream, weights, state = refs[0], refs[1:5], refs[5:13]
    x, rhs, small = refs[13:]
    assemble(me, pieces, *weights, rhs, small)
    load_images(images, x)
    forward(x, *weights, *state, stream)


def second_layer_kernel(*refs):
    me, live, stream, cotangent, pieces, refs = refs[0][0], refs[1], refs[2], refs[3], refs[4:12], refs[12:]
    activations, grad, keep, send = refs[:4]
    weights, state, back, (rhs, small) = refs[4:8], refs[8:16], refs[16:25], refs[25:]
    assemble(me, pieces, *weights, rhs, small)
    forward(stream, *weights, *state, grad)
    for i in range(IMGS):
        alive = jnp.where(live[i] > 0, 1.0, 0.0)
        activations[i] = (grad[ROWS * i : ROWS * i + SEQ, :] * alive).astype(BF16)
    load_images(cotangent, grad)
    for i in range(IMGS):
        alive = jnp.where(live[i] > 0, 1.0, 0.0)
        grad[ROWS * i : ROWS * i + ROWS, :] = grad[ROWS * i : ROWS * i + ROWS, :] * alive
    w, w2, _, gain_row = weights
    backward(stream, w, w2, gain_row, *state, grad, *back)
    disperse(me, *back[5:], keep, send, rhs, small)


def first_backward_kernel(*refs):
    me, images, grad_in, refs = refs[0][0], refs[1], refs[2], refs[3:]
    weights, state, refs = refs[:3], refs[3:11], refs[11:]
    input_grad, keep, send = refs[:3]
    x, grad, back, (rhs, small) = refs[3], refs[4], refs[5:14], refs[14:]
    load_images(images, x)
    grad[...] = grad_in[...]
    backward(x, *weights, *state, grad, *back)
    for i in range(IMGS):
        input_grad[i] = grad[ROWS * i : ROWS * i + SEQ, :].astype(BF16)
    disperse(me, *back[5:], keep, send, rhs, small)


def whole(count):
    return [pl.BlockSpec(memory_space=pltpu.VMEM)] * count


def scalar(count):
    return [pl.BlockSpec(memory_space=pltpu.SMEM)] * count


def params():
    return pltpu.CompilerParams(vmem_limit_bytes=VMEM_LIMIT)


def cost(flops):
    return pl.CostEstimate(flops=flops, bytes_accessed=20_000_000, transcendentals=0)


def run_first_forward(me, images, pieces):
    outs = [jax.ShapeDtypeStruct((R, D), F32)] + shapes(WEIGHTS) + shapes(STATE)
    out = pl.pallas_call(
        first_forward_kernel,
        out_shape=outs,
        in_specs=scalar(1) + whole(9),
        out_specs=whole(len(outs)),
        scratch_shapes=scratch((((R, D), F32),) + MOVE_SCRATCH),
        compiler_params=params(),
        cost_estimate=cost(8_000_000_000),
        name="first_forward",
    )(me, images, *pieces)
    return out[0], out[1:5], out[5:]


def run_second_layer(me, live, stream, cotangent, pieces):
    outs = [jax.ShapeDtypeStruct(cotangent.shape, BF16), jax.ShapeDtypeStruct((R, D), F32), WIRE, WIRE]
    return pl.pallas_call(
        second_layer_kernel,
        out_shape=outs,
        in_specs=scalar(2) + whole(10),
        out_specs=whole(len(outs)),
        scratch_shapes=scratch(WEIGHTS + STATE + GRAD_SCRATCH + MOVE_SCRATCH),
        compiler_params=params(),
        cost_estimate=cost(24_000_000_000),
        name="second_layer",
    )(me, live, stream, cotangent, *pieces)


def run_first_backward(me, images, grad, weights, state):
    w, w2, _, gain_row = weights
    outs = [jax.ShapeDtypeStruct(images.shape, BF16), WIRE, WIRE]
    return pl.pallas_call(
        first_backward_kernel,
        out_shape=outs,
        in_specs=scalar(1) + whole(13),
        out_specs=whole(len(outs)),
        scratch_shapes=scratch((((R, D), F32), ((R, D), F32)) + GRAD_SCRATCH + MOVE_SCRATCH),
        compiler_params=params(),
        cost_estimate=cost(16_000_000_000),
        name="first_backward",
    )(me, images, grad, w, w2, gain_row, *state)


def chunk_table():
    table = []
    for c in range(3):
        for i in range(12):
            for b in range(3):
                table.append((0, i * 9 + b * 3 + c, c * THIRD + b * 12 + i))
            table.append((1, i * 3 + c, c * THIRD + 36 + i))
            for b in range(4):
                table.append((2, i * 12 + b * 3 + c, c * THIRD + 48 + b * 12 + i))
        for i in range(48):
            table.append((3, i * 3 + c, c * THIRD + 96 + i))
    return table


def pack_kernel(qkv, out, fc1, fc2, gains, biases, slab_a, slab_b, stage):
    flats = (qkv, out, fc1, fc2)
    stage[...] = jnp.zeros_like(stage)
    for which, piece, row in chunk_table():
        both = flats[which][:, 128 * piece : 128 * piece + 128].astype(F32)
        stage[0, row : row + 1, :] = both[0:1]
        stage[1, row : row + 1, :] = both[1:2]
    for layer in range(LAYERS):
        stage[layer, SMALL : SMALL + 1, 0:SHARD_BIAS] = biases[...].astype(F32)[layer : layer + 1]
        stage[layer, SMALL + 1 : SMALL + 2, 0:SHARD_GAIN] = gains[...].astype(F32)[layer : layer + 1]
    slab_a[...] = stage[0].astype(BF16)
    slab_b[...] = stage[1].astype(BF16)


def run_pack(qkv, out, fc1, fc2, gains, biases):
    return pl.pallas_call(
        pack_kernel,
        out_shape=[jax.ShapeDtypeStruct((SLAB, 128), BF16)] * 2,
        in_specs=whole(6),
        out_specs=whole(2),
        scratch_shapes=[pltpu.VMEM((2, SLAB, 128), F32)],
        name="pack",
    )(qkv, out, fc1, fc2, gains, biases)


def unpack_kernel(slab_a, slab_b, qkv, out, fc1, fc2, gains, biases):
    flats = (qkv, out, fc1, fc2)
    for which, piece, row in chunk_table():
        lanes = slice(128 * piece, 128 * piece + 128)
        flats[which][0:1, lanes] = slab_a[row : row + 1, :]
        flats[which][1:2, lanes] = slab_b[row : row + 1, :]
    for layer, slab in enumerate((slab_a, slab_b)):
        biases[layer : layer + 1, :] = slab[SMALL : SMALL + 1, 0:SHARD_BIAS]
        gains[layer : layer + 1, :] = slab[SMALL + 1 : SMALL + 2, 0:SHARD_GAIN]


def run_unpack(slab_a, slab_b, widths):
    return pl.pallas_call(
        unpack_kernel,
        out_shape=[jax.ShapeDtypeStruct((LAYERS, width), F32) for width in widths],
        in_specs=whole(2),
        out_specs=whole(6),
        name="unpack",
    )(slab_a, slab_b)


def swap(value, bits):
    return lax.ppermute(value, "fsdp", [(i, i ^ bits) for i in range(SLABS)])


def gather_tree(slab):
    quad = jnp.concatenate([slab] + [swap(slab, 8 * z) for z in (1, 2, 3)], axis=0)
    near = [quad] + [swap(quad, 2 * xy) for xy in (1, 2, 3)]
    return near + [swap(part, 1) for part in near]


def scatter_tree(keep, send):
    got = swap(send, 1)
    total = keep.astype(F32) + got.astype(F32)
    parts = [total[QUAD * xy : QUAD * xy + QUAD] for xy in range(4)]
    mine = parts[0]
    for xy in (1, 2, 3):
        mine = mine + swap(parts[xy].astype(BF16), 2 * xy).astype(F32)
    slabs = [mine[SLAB * z : SLAB * z + SLAB] for z in range(4)]
    total = slabs[0]
    for z in (1, 2, 3):
        total = total + swap(slabs[z].astype(BF16), 8 * z).astype(F32)
    return total


def to_slabs(qkv, out, fc1, fc2, gains, biases):
    blocks = jnp.concatenate(
        [
            qkv.reshape(SLABS, 12, 3, D).transpose(0, 2, 1, 3).reshape(SLABS, 36, D),
            out.reshape(SLABS, 12, D),
            fc1.reshape(SLABS, 12, 4, D).transpose(0, 2, 1, 3).reshape(SLABS, 48, D),
            fc2.reshape(SLABS, 48, D),
        ],
        axis=1,
    )
    thirds = blocks.reshape(SLABS, THIRD, 3, 128).transpose(0, 2, 1, 3).reshape(SLABS, SMALL, 128)
    tail = jnp.zeros((SLABS, SLAB - SMALL, 128), blocks.dtype)
    tail = tail.at[:, 0, :SHARD_BIAS].set(biases.reshape(SLABS, SHARD_BIAS))
    tail = tail.at[:, 1, :SHARD_GAIN].set(gains.reshape(SLABS, SHARD_GAIN))
    return jnp.concatenate([thirds, tail], axis=1)


def from_slabs(slabs):
    blocks = slabs[:, :SMALL].reshape(SLABS, 3, THIRD, 128).transpose(0, 2, 1, 3).reshape(SLABS, THIRD, D)
    return (
        blocks[:, :36].reshape(SLABS, 3, 12, D).transpose(0, 2, 1, 3).reshape(-1),
        blocks[:, 36:48].reshape(-1),
        blocks[:, 48:96].reshape(SLABS, 4, 12, D).transpose(0, 2, 1, 3).reshape(-1),
        blocks[:, 96:].reshape(-1),
        slabs[:, SMALL + 1, :SHARD_GAIN].reshape(-1),
        slabs[:, SMALL, :SHARD_BIAS].reshape(-1),
    )


def slab_number(core, xy, z):
    return core + 2 * xy + 8 * z


def plain_pieces(flats, layer):
    slabs = to_slabs(*(lax.all_gather(flat[layer], "fsdp", axis=0, tiled=True) for flat in flats))
    return [
        jnp.concatenate([slabs[slab_number(core, xy, z)] for z in range(4)], axis=0)
        for core in range(2)
        for xy in range(4)
    ]


def plain_totals(keep, send):
    halves = [half.reshape(4, 4, SLAB, 128).astype(F32) for half in (keep, send)]
    slabs = jnp.stack([halves[d & 1][(d >> 1) & 3, d >> 3] for d in range(SLABS)])
    return [lax.psum_scatter(flat, "fsdp", scatter_dimension=0, tiled=True) for flat in from_slabs(slabs)]


def local(images, live_counts, qkv_weight, out_weight, fc1_weight, fc2_weight, norm_gains, biases, cotangent):
    flats = (qkv_weight, out_weight, fc1_weight, fc2_weight, norm_gains, biases)
    tree = lax.axis_size("fsdp") == SLABS
    if tree:
        me = lax.axis_index("fsdp").astype(jnp.int32).reshape(1)
        slab_a, slab_b = run_pack(*flats)
        pieces_a, pieces_b = gather_tree(slab_a), gather_tree(slab_b)
    else:
        me = jnp.zeros((1,), jnp.int32)
        pieces_a, pieces_b = plain_pieces(flats, 0), plain_pieces(flats, 1)
    stream, weights, state = run_first_forward(me, images, pieces_a)
    activations, grad, keep_b, send_b = run_second_layer(me, live_counts, stream, cotangent, pieces_b)
    input_grad, keep_a, send_a = run_first_backward(me, images, grad, weights, state)
    if tree:
        total_b, total_a = scatter_tree(keep_b, send_b), scatter_tree(keep_a, send_a)
        results = run_unpack(total_a, total_b, [flat.shape[1] for flat in flats])
    else:
        results = [jnp.stack(both) for both in zip(plain_totals(keep_a, send_a), plain_totals(keep_b, send_b))]
    return (activations, input_grad, *results)


def solution(mesh):
    flat = P(None, "fsdp")
    image = P("fsdp", None, None)
    return jax.shard_map(
        local,
        mesh=mesh,
        in_specs=(image, P("fsdp")) + (flat,) * 6 + (image,),
        out_specs=(image, image) + (flat,) * 6,
        check_vma=False,
    )
```

time: 908 us -> 265 us (0.29)
  blocking collectives: 253 us -> 0 us
  other arithmetic: 200 us -> 4.38 us
  matrix products: 125 us -> 0 us
  Pallas kernels: 0 us -> 124 us
  local copies, waits for them, and re-layouts: 127 us -> 3.38 us
  waiting for transfers between devices: 178 us -> 84.6 us
  starting transfers between devices: 0.2 us -> 46.9 us
  between operations: 19.5 us -> 0.91 us
    unnamed x6 -> x0, waiting for transfers between devices: 178 us -> none
    all_gather x4 -> x0, blocking collectives: 172 us -> none  [the longest x2 93.2 us: local(): lax.all_gather(qkv_weight[layer_idx], 'fsdp', axis=0, tiled=True)]
    all_gather x8 -> x0, other arithmetic: 158 us -> none  [the longest x2 53.5 us: local(): lax.all_gather(fc1_weight[layer_idx], 'fsdp', axis=0, tiled=True)]
    dot_general x108 -> x0, matrix products: 125 us -> none  [the longest x24 33.5 us: outer_sum(): jnp.einsum('ri,rj->ij', left_rows, right_rows, preferred_element_type=jnp...]
    pallas_call x0 -> x5, Pallas kernels: none -> 124 us  [the longest x1 55.9 us: run_second_layer(): pl.pallas_call(second_layer_kernel, out_shape=outs, in_specs=scalar(2) +...]
    ppermute x0 -> x34, waiting for transfers between devices: none -> 84.6 us  [swap(): return lax.ppermute(value, 'fsdp', [(i, i ^ bits) for i in range(SLABS)])]
    unnamed x2 -> x0, blocking collectives: 81.6 us -> none
    ppermute x0 -> x34, starting transfers between devices: none -> 46.9 us  [swap(): return lax.ppermute(value, 'fsdp', [(i, i ^ bits) for i in range(SLABS)])]
  transfers between devices with their start and end apart: 5 -> 34, of which waited for: 1 -> 15; matrix products, arithmetic and copies ran while one was open for 24% -> 2% of each run, Pallas kernels for 0% -> 11%
where the time goes in v1:
time: 265 us
  Pallas kernels  124 us (47%)
  waiting for transfers between devices  84.6 us (32%)
  starting transfers between devices  46.9 us (18%)
  other arithmetic  4.38 us (2%)
  local copies, waits for them, and re-layouts  3.38 us (1%)
    ppermute x34, waiting for transfers between devices, swap(): return lax.ppermute(value, 'fsdp', [(i, i ^ bits) for i in range(SLABS)])  84.6 us
    pallas_call x1, Pallas kernels, run_second_layer(): pl.pallas_call(second_layer_kernel, out_shape=outs, in_specs=scalar(2) +...  55.9 us
    ppermute x34, starting transfers between devices, swap(): return lax.ppermute(value, 'fsdp', [(i, i ^ bits) for i in range(SLABS)])  46.9 us
    pallas_call x1, Pallas kernels, run_first_backward(): pl.pallas_call(first_backward_kernel, out_shape=outs, in_specs=scalar(1)...  35.1 us
    pallas_call x1, Pallas kernels, run_first_forward(): pl.pallas_call(first_forward_kernel, out_shape=outs, in_specs=scalar(1) +...  29.3 us
  transfers between devices with their start and end apart: 34, of which 15 were waited for; matrix products, arithmetic and copies ran while one was open for 2% of the time, Pallas kernels for 11%

profile of v1, /device:TPU:0, one launch (start us, length us, event | category | flops | bytes accessed | tf_op | source)
XLA Modules:
  0.0 264.6 jit_solution(5119986765351247072)
XLA Ops:
  2.6 5.0 %collective-permute-start.2 = (bf16[448,128]{1,0:T(8,128)(2,1)}, bf16[448,128]{1,0:T(8,128)(2,1)S(1)}, u32[]{:S(2)}, u32[]{:S(2)}) collective-permute-start(bf16[448,128]{1,0:T(8,128)(2,1)} %get-tuple-element.35), channel_id=1, source_target_pairs={{0,24},{1,25},{2,26},{3,27},{4,28},{5,29},{6,30},{7,31},{8,16},{9,... | collective-permute-start | bytes 344072 | tf_op jit(solution)/shard_map/ppermute | solution.py:550
  8.2 3.8 %collective-permute-start.12 = (bf16[448,128]{1,0:T(8,128)(2,1)}, bf16[448,128]{1,0:T(8,128)(2,1)S(1)}, u32[]{:S(2)}, u32[]{:S(2)}) collective-permute-start(bf16[448,128]{1,0:T(8,128)(2,1)} %get-tuple-element.37), channel_id=1, source_target_pairs={{0,24},{1,25},{2,26},{3,27},{4,28},{5,29},{6,30},{7,31},{8,16},{9,... | collective-permute-start | bytes 344072 | tf_op jit(solution)/shard_map/ppermute | solution.py:550
  13.8 7.1 %collective-permute-done.10 = bf16[448,128]{1,0:T(8,128)(2,1)S(1)} collective-permute-done((bf16[448,128]{1,0:T(8,128)(2,1)}, bf16[448,128]{1,0:T(8,128)(2,1)S(1)}, u32[]{:S(2)}, u32[]{:S(2)}) %collective-permute-start.10) | collective-permute-done | bytes 114720 | tf_op jit(solution)/shard_map/ppermute | solution.py:550
  22.3 6.5 %collective-permute-done.11 = bf16[448,128]{1,0:T(8,128)(2,1)S(1)} collective-permute-done((bf16[448,128]{1,0:T(8,128)(2,1)}, bf16[448,128]{1,0:T(8,128)(2,1)S(1)}, u32[]{:S(2)}, u32[]{:S(2)}) %collective-permute-start.11) | collective-permute-done | bytes 114720 | tf_op jit(solution)/shard_map/ppermute | solution.py:550
  28.9 2.5 collective-permute-start.15
  35.6 7.7 %collective-permute-done.15.refs_7_ = bf16[1792,128]{1,0:T(8,128)(2,1)S(1)} collective-permute-done((bf16[1792,128]{1,0:T(8,128)(2,1)S(1)}, bf16[1792,128]{1,0:T(8,128)(2,1)S(1)}, u32[]{:S(2)}, u32[]{:S(2)}) %collective-permute-start.15) | collective-permute-done | bytes 458784 | tf_op jit(solution)/shard_map/ppermute | solution.py:550
  44.8 12.6 %collective-permute-done.14.refs_6_ = bf16[1792,128]{1,0:T(8,128)(2,1)S(1)} collective-permute-done((bf16[1792,128]{1,0:T(8,128)(2,1)S(1)}, bf16[1792,128]{1,0:T(8,128)(2,1)S(1)}, u32[]{:S(2)}, u32[]{:S(2)}) %collective-permute-start.14) | collective-permute-done | bytes 458784 | tf_op jit(solution)/shard_map/ppermute | solution.py:550
  57.9 9.2 %collective-permute-done.4.refs_4_ = bf16[1792,128]{1,0:T(8,128)(2,1)S(1)} collective-permute-done((bf16[1792,128]{1,0:T(8,128)(2,1)S(1)}, bf16[1792,128]{1,0:T(8,128)(2,1)S(1)}, u32[]{:S(2)}, u32[]{:S(2)}) %collective-permute-start.4) | collective-permute-done | bytes 458784 | tf_op jit(solution)/shard_map/ppermute | solution.py:550
  70.6 29.3 %first_forward.1 = (f32[624,384]{1,0:T(8,128)}, bf16[8,384,384]{2,1,0:T(8,128)(2,1)}, bf16[1536,384]{1,0:T(8,128)(2,1)}, f32[1,3840]{1,0:T(1,128)}, f32[1,768]{1...) custom-call(s32[1]{0:T(128)} %bitcast.refs_0_, ...), custom_call_target="tpu_custom_call" | custom-call | flops 8000000000 | bytes 20000000 | tf_op jit(solution)/shard_map/first_forward/pallas_call | solution.py:447
  101.3 55.9 %second_layer.1 = (bf16[3,197,384]{2,1,0:T(8,128)(2,1)}, f32[624,384]{1,0:T(8,128)}, bf16[7168,128]{1,0:T(8,128)(2,1)}, bf16[7168,128]{1,0:T(8,128)(2,1)}) custom-call(s32[1]{0:T(128)} %bitcast.refs_0_, s32[3]{0:T(128)} %refs_1_.4, f32[624,384]{1,0:T(8,128)} %get-tuple-element.36.refs_2_, bf16[3,197,384]{2,1,0:T(8,128)(2,1)} %refs_3_.1, ...), custom_call_target="tpu_custom_call" | custom-call | flops 24000000000 | bytes 20000000 | tf_op jit(solution)/shard_map/second_layer/pallas_call | solution.py:462
  157.2 35.1 %first_backward.1 = (bf16[3,197,384]{2,1,0:T(8,128)(2,1)}, bf16[7168,128]{1,0:T(8,128)(2,1)}, bf16[7168,128]{1,0:T(8,128)(2,1)}) custom-call(s32[1]{0:T(128)} %bitcast.refs_0_, bf16[3,197,384]{2,1,0:T(8,128)(2,1)} %refs_1_.5, f32[624,384]{1,0:T(8,128)} %get-tuple-element.39.refs_2_, bf16[8,384,384]{2,1,0:T(8,128)(2,1)} %get-tuple-element.40.refs_3_, ...), custom_call_target="tpu_custom_call" | custom-call | flops 16000000000 | bytes 20000000 | tf_op jit(solution)/shard_map/first_backward/pallas_call | solution.py:477
  192.9 4.9 %collective-permute-done.20 = bf16[7168,128]{1,0:T(8,128)(2,1)S(1)} collective-permute-done((bf16[7168,128]{1,0:T(8,128)(2,1)}, bf16[7168,128]{1,0:T(8,128)(2,1)S(1)}, u32[]{:S(2)}, u32[]{:S(2)}) %collective-permute-start.20) | collective-permute-done | bytes 1835040 | tf_op jit(solution)/shard_map/ppermute | solution.py:550
  197.8 2.0 convert_add_fusion.1
  206.9 6.4 %collective-permute-done.21 = bf16[1792,128]{1,0:T(8,128)(2,1)S(1)} collective-permute-done((bf16[1792,128]{1,0:T(8,128)(2,1)S(1)}, bf16[1792,128]{1,0:T(8,128)(2,1)S(1)}, u32[]{:S(2)}, u32[]{:S(2)}) %collective-permute-start.21) | collective-permute-done | bytes 458784 | tf_op jit(solution)/shard_map/ppermute | solution.py:550
  214.6 9.3 %collective-permute-done.23 = bf16[1792,128]{1,0:T(8,128)(2,1)S(1)} collective-permute-done((bf16[1792,128]{1,0:T(8,128)(2,1)S(1)}, bf16[1792,128]{1,0:T(8,128)(2,1)S(1)}, u32[]{:S(2)}, u32[]{:S(2)}) %collective-permute-start.23) | collective-permute-done | bytes 458784 | tf_op jit(solution)/shard_map/ppermute | solution.py:550
  226.1 5.1 %collective-permute-start.24 = (bf16[448,128]{1,0:T(8,128)(2,1)S(1)}, bf16[448,128]{1,0:T(8,128)(2,1)S(1)}, u32[]{:S(2)}, u32[]{:S(2)}) collective-permute-start(bf16[448,128]{1,0:T(8,128)(2,1)S(1)} %get-tuple-element.79), channel_id=1, source_target_pairs={{0,8},{1,9},{2,10},{3,11},{4,12},{5,13},{6,14},{7,15},{8,0},{9,1},... | collective-permute-start | bytes 344072 | tf_op jit(solution)/shard_map/ppermute | solution.py:550
  231.2 2.4 collective-permute-start.26
  233.6 2.3 collective-permute-start.25
  236.0 6.9 %collective-permute-done.30 = bf16[1792,128]{1,0:T(8,128)(2,1)S(1)} collective-permute-done((bf16[1792,128]{1,0:T(8,128)(2,1)S(1)}, bf16[1792,128]{1,0:T(8,128)(2,1)S(1)}, u32[]{:S(2)}, u32[]{:S(2)}) %collective-permute-start.30) | collective-permute-done | bytes 458784 | tf_op jit(solution)/shard_map/ppermute | solution.py:550
  244.5 5.0 %collective-permute-start.31 = (bf16[448,128]{1,0:T(8,128)(2,1)S(1)}, bf16[448,128]{1,0:T(8,128)(2,1)S(1)}, u32[]{:S(2)}, u32[]{:S(2)}) collective-permute-start(bf16[448,128]{1,0:T(8,128)(2,1)S(1)} %get-tuple-element.76), channel_id=1, source_target_pairs={{0,8},{1,9},{2,10},{3,11},{4,12},{5,13},{6,14},{7,15},{8,0},{9,1},... | collective-permute-start | bytes 344072 | tf_op jit(solution)/shard_map/ppermute | solution.py:550
  249.5 2.5 collective-permute-start.33
  253.3 4.5 %collective-permute-done.33 = bf16[448,128]{1,0:T(8,128)(2,1)S(1)} collective-permute-done((bf16[448,128]{1,0:T(8,128)(2,1)S(1)}, bf16[448,128]{1,0:T(8,128)(2,1)S(1)}, u32[]{:S(2)}, u32[]{:S(2)}) %collective-permute-start.33) | collective-permute-done | bytes 114720 | tf_op jit(solution)/shard_map/ppermute | solution.py:550
  257.8 4.0 %collective-permute-done.32 = bf16[448,128]{1,0:T(8,128)(2,1)S(1)} collective-permute-done((bf16[448,128]{1,0:T(8,128)(2,1)S(1)}, bf16[448,128]{1,0:T(8,128)(2,1)S(1)}, u32[]{:S(2)}, u32[]{:S(2)}) %collective-permute-start.32) | collective-permute-done | bytes 114720 | tf_op jit(solution)/shard_map/ppermute | solution.py:550
  262.5 2.1 unpack.1
  (93 shorter events, 31.3 us)
Async XLA Ops:
  2.6 29.4 %collective-permute-start.2 = (bf16[448,128]{1,0:T(8,128)(2,1)}, bf16[448,128]{1,0:T(8,128)(2,1)S(1)}, u32[]{:S(2)}, u32[]{:S(2)}) collective-permute-start(bf16[448,128]{1,0:T(8,128)(2,1)} %get-tuple-element.35), channel_id=1, source_target_pairs={{0,24},{1,25},{2,26},{3,27},{4,28},{5,29},{6,30},{7,31},{8,16},{9,... | collective-permute-start | bytes 344072 | tf_op jit(solution)/shard_map/ppermute | solution.py:550
  7.6 24.3 %collective-permute-start.1 = (bf16[448,128]{1,0:T(8,128)(2,1)}, bf16[448,128]{1,0:T(8,128)(2,1)S(1)}, u32[]{:S(2)}, u32[]{:S(2)}) collective-permute-start(bf16[448,128]{1,0:T(8,128)(2,1)} %get-tuple-element.35), channel_id=1, source_target_pairs={{0,16},{1,17},{2,18},{3,19},{4,20},{5,21},{6,22},{7,23},{8,24},{9,... | collective-permute-start | bytes 344072 | tf_op jit(solution)/shard_map/ppermute | solution.py:550
  7.6 24.3 %collective-permute-start = (bf16[448,128]{1,0:T(8,128)(2,1)}, bf16[448,128]{1,0:T(8,128)(2,1)S(1)}, u32[]{:S(2)}, u32[]{:S(2)}) collective-permute-start(bf16[448,128]{1,0:T(8,128)(2,1)} %get-tuple-element.35), channel_id=1, source_target_pairs={{0,8},{1,9},{2,10},{3,11},{4,12},{5,13},{6,14},{7,15},{8,0},{9,1},... | collective-permute-start | bytes 344072 | tf_op jit(solution)/shard_map/ppermute | solution.py:550
  8.2 20.7 %collective-permute-start.12 = (bf16[448,128]{1,0:T(8,128)(2,1)}, bf16[448,128]{1,0:T(8,128)(2,1)S(1)}, u32[]{:S(2)}, u32[]{:S(2)}) collective-permute-start(bf16[448,128]{1,0:T(8,128)(2,1)} %get-tuple-element.37), channel_id=1, source_target_pairs={{0,24},{1,25},{2,26},{3,27},{4,28},{5,29},{6,30},{7,31},{8,16},{9,... | collective-permute-start | bytes 344072 | tf_op jit(solution)/shard_map/ppermute | solution.py:550
  28.9 14.4 %collective-permute-start.15 = (bf16[1792,128]{1,0:T(8,128)(2,1)S(1)}, bf16[1792,128]{1,0:T(8,128)(2,1)S(1)}, u32[]{:S(2)}, u32[]{:S(2)}) collective-permute-start(bf16[1792,128]{1,0:T(8,128)(2,1)S(1)} %constant_dynamic-update-slice_fusion.4.refs_4_), channel_id=1, source_target_pairs={{0,6},{1,7},{2,4},{3,5},{4,2},{5,3},{6,0},{7,1},{8,14},{9,15},{10,... | collective-permute-start | bytes 1376264 | tf_op jit(solution)/shard_map/ppermute | solution.py:550
  31.4 26.0 %collective-permute-start.14 = (bf16[1792,128]{1,0:T(8,128)(2,1)S(1)}, bf16[1792,128]{1,0:T(8,128)(2,1)S(1)}, u32[]{:S(2)}, u32[]{:S(2)}) collective-permute-start(bf16[1792,128]{1,0:T(8,128)(2,1)S(1)} %constant_dynamic-update-slice_fusion.4.refs_4_), channel_id=1, source_target_pairs={{0,4},{1,5},{2,6},{3,7},{4,0},{5,1},{6,2},{7,3},{8,12},{9,13},{10,... | collective-permute-start | bytes 1376264 | tf_op jit(solution)/shard_map/ppermute | solution.py:550
  32.0 25.5 %collective-permute-start.5 = (bf16[1792,128]{1,0:T(8,128)(2,1)S(1)}, bf16[1792,128]{1,0:T(8,128)(2,1)S(1)}, u32[]{:S(2)}, u32[]{:S(2)}) collective-permute-start(bf16[1792,128]{1,0:T(8,128)(2,1)S(1)} %constant_dynamic-update-slice_fusion.refs_2_), channel_id=1, source_target_pairs={{0,6},{1,7},{2,4},{3,5},{4,2},{5,3},{6,0},{7,1},{8,14},{9,15},{10,... | collective-permute-start | bytes 1376264 | tf_op jit(solution)/shard_map/ppermute | solution.py:550
  33.6 33.6 %collective-permute-start.4 = (bf16[1792,128]{1,0:T(8,128)(2,1)S(1)}, bf16[1792,128]{1,0:T(8,128)(2,1)S(1)}, u32[]{:S(2)}, u32[]{:S(2)}) collective-permute-start(bf16[1792,128]{1,0:T(8,128)(2,1)S(1)} %constant_dynamic-update-slice_fusion.refs_2_), channel_id=1, source_target_pairs={{0,4},{1,5},{2,6},{3,7},{4,0},{5,1},{6,2},{7,3},{8,12},{9,13},{10,... | collective-permute-start | bytes 1376264 | tf_op jit(solution)/shard_map/ppermute | solution.py:550
  34.1 33.1 %collective-permute-start.3 = (bf16[1792,128]{1,0:T(8,128)(2,1)S(1)}, bf16[1792,128]{1,0:T(8,128)(2,1)}, u32[]{:S(2)}, u32[]{:S(2)}) collective-permute-start(bf16[1792,128]{1,0:T(8,128)(2,1)S(1)} %constant_dynamic-update-slice_fusion.refs_2_), channel_id=1, source_target_pairs={{0,2},{1,3},{2,0},{3,1},{4,6},{5,7},{6,4},{7,5},{8,10},{9,11},{10,... | collective-permute-start | bytes 1376264 | tf_op jit(solution)/shard_map/ppermute | solution.py:550
  43.3 24.4 %collective-permute-start.13 = (bf16[1792,128]{1,0:T(8,128)(2,1)S(1)}, bf16[1792,128]{1,0:T(8,128)(2,1)S(1)}, u32[]{:S(2)}, u32[]{:S(2)}) collective-permute-start(bf16[1792,128]{1,0:T(8,128)(2,1)S(1)} %constant_dynamic-update-slice_fusion.4.refs_4_), channel_id=1, source_target_pairs={{0,2},{1,3},{2,0},{3,1},{4,6},{5,7},{6,4},{7,5},{8,10},{9,11},{10,... | collective-permute-start | bytes 1376264 | tf_op jit(solution)/shard_map/ppermute | solution.py:550
  67.7 32.3 %collective-permute-start.16 = (bf16[1792,128]{1,0:T(8,128)(2,1)S(1)}, bf16[1792,128]{1,0:T(8,128)(2,1)S(1)}, u32[]{:S(2)}, u32[]{:S(2)}) collective-permute-start(bf16[1792,128]{1,0:T(8,128)(2,1)S(1)} %constant_dynamic-update-slice_fusion.4.refs_4_), channel_id=1, source_target_pairs={{0,1},{1,0},{2,3},{3,2},{4,5},{5,4},{6,7},{7,6},{8,9},{9,8},{10,11... | collective-permute-start | bytes 1376264 | tf_op jit(solution)/shard_map/ppermute | solution.py:550
  67.8 32.3 %collective-permute-start.19 = (bf16[1792,128]{1,0:T(8,128)(2,1)S(1)}, bf16[1792,128]{1,0:T(8,128)(2,1)S(1)}, u32[]{:S(2)}, u32[]{:S(2)}) collective-permute-start(bf16[1792,128]{1,0:T(8,128)(2,1)S(1)} %collective-permute-done.15.refs_7_), channel_id=1, source_target_pairs={{0,1},{1,0},{2,3},{3,2},{4,5},{5,4},{6,7},{7,6},{8,9},{9,8},{10,11... | collective-permute-start | bytes 1376264 | tf_op jit(solution)/shard_map/ppermute | solution.py:550
  68.2 31.8 %collective-permute-start.18 = (bf16[1792,128]{1,0:T(8,128)(2,1)S(1)}, bf16[1792,128]{1,0:T(8,128)(2,1)S(1)}, u32[]{:S(2)}, u32[]{:S(2)}) collective-permute-start(bf16[1792,128]{1,0:T(8,128)(2,1)S(1)} %collective-permute-done.14.refs_6_), channel_id=1, source_target_pairs={{0,1},{1,0},{2,3},{3,2},{4,5},{5,4},{6,7},{7,6},{8,9},{9,8},{10,11... | collective-permute-start | bytes 1376264 | tf_op jit(solution)/shard_map/ppermute | solution.py:550
  69.1 31.0 %collective-permute-start.17 = (bf16[1792,128]{1,0:T(8,128)(2,1)S(1)}, bf16[1792,128]{1,0:T(8,128)(2,1)S(1)}, u32[]{:S(2)}, u32[]{:S(2)}) collective-permute-start(bf16[1792,128]{1,0:T(8,128)(2,1)S(1)} %collective-permute-done.13.refs_5_), channel_id=1, source_target_pairs={{0,1},{1,0},{2,3},{3,2},{4,5},{5,4},{6,7},{7,6},{8,9},{9,8},{10,11... | collective-permute-start | bytes 1376264 | tf_op jit(solution)/shard_map/ppermute | solution.py:550
  192.5 10.9 %collective-permute-start.27 = (bf16[7168,128]{1,0:T(8,128)(2,1)S(1)}, bf16[7168,128]{1,0:T(8,128)(2,1)S(1)}, u32[]{:S(2)}, u32[]{:S(2)}) collective-permute-start(bf16[7168,128]{1,0:T(8,128)(2,1)S(1)} %copy-done.3), channel_id=1, source_target_pairs={{0,1},{1,0},{2,3},{3,2},{4,5},{5,4},{6,7},{7,6},{8,9},{9,8},{10,11... | collective-permute-start | bytes 5505032 | tf_op jit(solution)/shard_map/ppermute | solution.py:550
  199.8 13.4 %collective-permute-start.21 = (bf16[1792,128]{1,0:T(8,128)(2,1)S(1)}, bf16[1792,128]{1,0:T(8,128)(2,1)S(1)}, u32[]{:S(2)}, u32[]{:S(2)}) collective-permute-start(bf16[1792,128]{1,0:T(8,128)(2,1)S(1)} %get-tuple-element.73), channel_id=1, source_target_pairs={{0,2},{1,3},{2,0},{3,1},{4,6},{5,7},{6,4},{7,5},{8,10},{9,11},{10,... | collective-permute-start | bytes 1376264 | tf_op jit(solution)/shard_map/ppermute | solution.py:550
  201.3 22.7 %collective-permute-start.23 = (bf16[1792,128]{1,0:T(8,128)(2,1)S(1)}, bf16[1792,128]{1,0:T(8,128)(2,1)S(1)}, u32[]{:S(2)}, u32[]{:S(2)}) collective-permute-start(bf16[1792,128]{1,0:T(8,128)(2,1)S(1)} %get-tuple-element.74), channel_id=1, source_target_pairs={{0,6},{1,7},{2,4},{3,5},{4,2},{5,3},{6,0},{7,1},{8,14},{9,15},{10,... | collective-permute-start | bytes 1376264 | tf_op jit(solution)/shard_map/ppermute | solution.py:550
  202.7 23.1 %collective-permute-start.22 = (bf16[1792,128]{1,0:T(8,128)(2,1)S(1)}, bf16[1792,128]{1,0:T(8,128)(2,1)S(1)}, u32[]{:S(2)}, u32[]{:S(2)}) collective-permute-start(bf16[1792,128]{1,0:T(8,128)(2,1)S(1)} %get-tuple-element.75), channel_id=1, source_target_pairs={{0,4},{1,5},{2,6},{3,7},{4,0},{5,1},{6,2},{7,3},{8,12},{9,13},{10,... | collective-permute-start | bytes 1376264 | tf_op jit(solution)/shard_map/ppermute | solution.py:550
  204.0 29.7 %collective-permute-start.28 = (bf16[1792,128]{1,0:T(8,128)(2,1)S(1)}, bf16[1792,128]{1,0:T(8,128)(2,1)S(1)}, u32[]{:S(2)}, u32[]{:S(2)}) collective-permute-start(bf16[1792,128]{1,0:T(8,128)(2,1)S(1)} %get-tuple-element.70), channel_id=1, source_target_pairs={{0,2},{1,3},{2,0},{3,1},{4,6},{5,7},{6,4},{7,5},{8,10},{9,11},{10,... | collective-permute-start | bytes 1376264 | tf_op jit(solution)/shard_map/ppermute | solution.py:550
  205.4 37.5 %collective-permute-start.30 = (bf16[1792,128]{1,0:T(8,128)(2,1)S(1)}, bf16[1792,128]{1,0:T(8,128)(2,1)S(1)}, u32[]{:S(2)}, u32[]{:S(2)}) collective-permute-start(bf16[1792,128]{1,0:T(8,128)(2,1)S(1)} %get-tuple-element.71), channel_id=1, source_target_pairs={{0,6},{1,7},{2,4},{3,5},{4,2},{5,3},{6,0},{7,1},{8,14},{9,15},{10,... | collective-permute-start | bytes 1376264 | tf_op jit(solution)/shard_map/ppermute | solution.py:550
  213.3 31.0 %collective-permute-start.29 = (bf16[1792,128]{1,0:T(8,128)(2,1)S(1)}, bf16[1792,128]{1,0:T(8,128)(2,1)S(1)}, u32[]{:S(2)}, u32[]{:S(2)}) collective-permute-start(bf16[1792,128]{1,0:T(8,128)(2,1)S(1)} %get-tuple-element.72), channel_id=1, source_target_pairs={{0,4},{1,5},{2,6},{3,7},{4,0},{5,1},{6,2},{7,3},{8,12},{9,13},{10,... | collective-permute-start | bytes 1376264 | tf_op jit(solution)/shard_map/ppermute | solution.py:550
  226.1 25.9 %collective-permute-start.24 = (bf16[448,128]{1,0:T(8,128)(2,1)S(1)}, bf16[448,128]{1,0:T(8,128)(2,1)S(1)}, u32[]{:S(2)}, u32[]{:S(2)}) collective-permute-start(bf16[448,128]{1,0:T(8,128)(2,1)S(1)} %get-tuple-element.79), channel_id=1, source_target_pairs={{0,8},{1,9},{2,10},{3,11},{4,12},{5,13},{6,14},{7,15},{8,0},{9,1},... | collective-permute-start | bytes 344072 | tf_op jit(solution)/shard_map/ppermute | solution.py:550
  231.2 21.3 %collective-permute-start.26 = (bf16[448,128]{1,0:T(8,128)(2,1)S(1)}, bf16[448,128]{1,0:T(8,128)(2,1)S(1)}, u32[]{:S(2)}, u32[]{:S(2)}) collective-permute-start(bf16[448,128]{1,0:T(8,128)(2,1)S(1)} %get-tuple-element.80), channel_id=1, source_target_pairs={{0,24},{1,25},{2,26},{3,27},{4,28},{5,29},{6,30},{7,31},{8,16},{9,... | collective-permute-start | bytes 344072 | tf_op jit(solution)/shard_map/ppermute | solution.py:550
  233.6 18.9 %collective-permute-start.25 = (bf16[448,128]{1,0:T(8,128)(2,1)S(1)}, bf16[448,128]{1,0:T(8,128)(2,1)S(1)}, u32[]{:S(2)}, u32[]{:S(2)}) collective-permute-start(bf16[448,128]{1,0:T(8,128)(2,1)S(1)} %get-tuple-element.81), channel_id=1, source_target_pairs={{0,16},{1,17},{2,18},{3,19},{4,20},{5,21},{6,22},{7,23},{8,24},{9,... | collective-permute-start | bytes 344072 | tf_op jit(solution)/shard_map/ppermute | solution.py:550
  (23 other events, 376.2 us)

commit v2 on v1

v2 whole, which is shorter than its diff:
```python
import jax
import jax.numpy as jnp
from jax import lax
from jax.experimental import pallas as pl
from jax.experimental.pallas import tpu as pltpu
from jax.sharding import PartitionSpec as P

D = 384
FF = 1536
SEQ = 197
HEAD = 64
LAYERS = 2
NORM_EPS = 1e-06
ROOT_HALF = 0.7071067811865476
INV_ROOT_TAU = 0.3989422804014327

IMGS = 3
ROWS = 208
R = IMGS * ROWS
CHUNK = 48
CHUNKS = R // CHUNK
PAIRS = 3

SLABS = 32
THIRD = 144
SMALL = 2 * THIRD
MAIN = SMALL + 16
SIDE = THIRD
BLOCKS = 8
SHARD_BIAS = 120
SHARD_GAIN = 24
BIAS = 6 * D + FF
GAIN = 2 * D

F32 = jnp.float32
BF16 = jnp.bfloat16
VMEM_LIMIT = 56 * 1024 * 1024


def dot_nn(a, b):
    return lax.dot_general(a, b, (((1,), (0,)), ((), ())), preferred_element_type=F32)


def dot_nt(a, b):
    return lax.dot_general(a, b, (((1,), (1,)), ((), ())), preferred_element_type=F32)


def dot_tn(a, b):
    return lax.dot_general(a, b, (((0,), (0,)), ((), ())), preferred_element_type=F32)


def chunk_rows(i):
    return pl.ds(pl.multiple_of(i * CHUNK, CHUNK), CHUNK)


def block_rows(j):
    return pl.ds(pl.multiple_of(j * D, D), D)


def image_rows(i):
    return pl.ds(pl.multiple_of(i * ROWS, 16), ROWS)


def pair_lanes(p):
    return pl.ds(pl.multiple_of(p * 128, 128), 128)


def normalize(x):
    centred = x - jnp.mean(x, axis=-1, keepdims=True)
    inv_std = lax.rsqrt(jnp.mean(centred * centred, axis=-1, keepdims=True) + NORM_EPS)
    return centred * inv_std, inv_std


def digits(index, size):
    whole = jnp.floor((index.astype(F32) + 0.5) * (1.0 / size)).astype(jnp.int32)
    return whole, index - whole * size


def order_codes(shape, axis):
    index = lax.broadcasted_iota(jnp.int32, shape, axis)
    block, rest = digits(index, 48)
    dev, row = digits(rest, 12)
    return (block * 4 + dev) * 12 + row


def slab_codes(shape, axis, low, blocks):
    index = lax.broadcasted_iota(jnp.int32, shape, axis)
    rel, rest = digits(index, 12 * blocks)
    block, row = digits(rest, 12)
    dev = jnp.bitwise_xor(rel, low)
    return (block * 4 + dev) * 12 + row


def owner_mask(size, per_owner):
    lane = lax.broadcasted_iota(jnp.int32, (1, size), 1)
    owner, place = digits(lane, per_owner)
    rows = lax.broadcasted_iota(jnp.int32, (SLABS, size), 0)
    return rows == owner, place


def place_matrix(place, size):
    rows = lax.broadcasted_iota(jnp.int32, (128, size), 0)
    return jnp.where(rows == place, 1.0, 0.0).astype(BF16)


def assemble(me, pieces, w, w2, bias_row, gain_row, rhs, small):
    low = jnp.bitwise_and(me, 3)
    order = jnp.where(
        order_codes((D, 1), 0) == slab_codes((1, D), 1, low, BLOCKS), 1.0, 0.0
    ).astype(BF16)

    for zr in range(4):
        for yr in range(2):
            g = jnp.bitwise_xor(lax.shift_right_logical(me, 2), yr + 2 * zr)
            for xr in range(2):
                for cr in range(2):
                    xy = xr + 2 * yr
                    main, side = pieces[4 * cr + xy], pieces[8 + 4 * cr + zr]
                    d = jnp.bitwise_xor(me, cr + 2 * xy + 8 * zr)
                    s = xr * 2 + cr
                    for c in range(3):
                        lanes = slice(128 * c, 128 * c + 128)
                        piece = main if c else side
                        base = zr * MAIN + (c - 1) * THIRD if c else xy * SIDE
                        rhs[96 * s : 96 * s + 96, lanes] = piece[base : base + 96, :]
                        w2[pl.ds(pl.multiple_of(48 * d, 16), 48), lanes] = piece[base + 96 : base + THIRD, :]
                    tail = main[zr * MAIN + SMALL : zr * MAIN + MAIN, :].astype(F32)
                    small[0, pl.ds(d, 1), :] = tail[0:1, :]
                    small[1, pl.ds(d, 1), :] = tail[1:2, :]
            sorted_rows = dot_nn(order, rhs[...]).astype(BF16)
            for b in range(BLOCKS):
                w[b, pl.ds(pl.multiple_of(48 * g, 16), 48), :] = sorted_rows[48 * b : 48 * b + 48]
    for slot, size, per_owner, row in ((0, BIAS, SHARD_BIAS, bias_row), (1, GAIN, SHARD_GAIN, gain_row)):
        mine, place = owner_mask(size, per_owner)
        spread = dot_nn(small[slot].astype(BF16), place_matrix(place, size))
        row[...] = jnp.sum(jnp.where(mine, spread, 0.0), axis=0, keepdims=True)


def main_rows(blocks, with_w2, with_small):
    return 2 * side_rows(blocks, with_w2) + 16 * with_small


def side_rows(blocks, with_w2):
    return 12 * blocks + 48 * with_w2


def disperse(me, dw, dw2, bias_row, gain_row, wires, rhs, small):
    blocks = dw.shape[0]
    size = 48 * blocks
    third = side_rows(blocks, dw2 is not None)
    stride = main_rows(blocks, dw2 is not None, bias_row is not None)
    low = jnp.bitwise_and(me, 3)
    order = jnp.where(
        slab_codes((size, 1), 0, low, blocks) == order_codes((1, size), 1), 1.0, 0.0
    ).astype(BF16)
    if bias_row is not None:
        for slot, width, per_owner, row in ((0, BIAS, SHARD_BIAS, bias_row), (1, GAIN, SHARD_GAIN, gain_row)):
            mine, place = owner_mask(width, per_owner)
            spread = jnp.where(mine, row[...], 0.0).astype(BF16)
            small[slot] = dot_nt(spread, place_matrix(place, width))
    head_row = lax.broadcasted_iota(jnp.int32, (16, 128), 0)

    def group(zr, carry):
        for yr in range(2):
            g = jnp.bitwise_xor(lax.shift_right_logical(me, 2), yr + 2 * zr)
            for b in range(blocks):
                rhs[48 * b : 48 * b + 48, :] = dw[b, pl.ds(pl.multiple_of(48 * g, 16), 48), :]
            slabs = dot_nn(order, rhs[0:size, :]).astype(BF16)
            for xr in range(2):
                for cr in range(2):
                    main, side = wires[2 * cr : 2 * cr + 2]
                    xy = xr + 2 * yr
                    d = jnp.bitwise_xor(me, cr + 2 * xy + 8 * zr)
                    s = xr * 2 + cr
                    base = pl.multiple_of(xy * (4 * stride) + zr * stride, 16)
                    for c in range(3):
                        lanes = slice(128 * c, 128 * c + 128)
                        if c:
                            out, start = main, base + (c - 1) * third
                        else:
                            out, start = side, pl.multiple_of(zr * (4 * third) + xy * third, 16)
                        rows = 12 * blocks
                        out[pl.ds(start, rows), :] = slabs[rows * s : rows * s + rows, lanes]
                        if dw2 is not None:
                            out[pl.ds(start + rows, 48), :] = dw2[pl.ds(pl.multiple_of(48 * d, 16), 48), lanes]
                    if bias_row is not None:
                        tail = jnp.where(
                            head_row == 0,
                            small[0, pl.ds(d, 1), :],
                            jnp.where(head_row == 1, small[1, pl.ds(d, 1), :], 0.0),
                        )
                        main[pl.ds(base + 2 * third, 16), :] = tail.astype(BF16)
        return carry

    lax.fori_loop(0, 4, group, 0)


def forward(x, w, w2, bias_row, gain_row, xna, qkv, probs, mixed, middle, xnb, act, slope, tmp):
    def norm_a(i, carry):
        rows = chunk_rows(i)
        normal, _ = normalize(x[rows, :])
        xna[rows, :] = (normal * gain_row[:, :D] + bias_row[:, :D]).astype(BF16)
        return carry

    lax.fori_loop(0, CHUNKS, norm_a, 0)
    for b in range(3):
        part = dot_nn(xna[...], w[b])
        if b == 0:
            part = part + bias_row[:, D : 2 * D]
        if b == 2:
            part = part + bias_row[:, 2 * D : 3 * D]
        qkv[b] = part.astype(BF16)

    lane = lax.broadcasted_iota(jnp.int32, (1, 128), 1)
    first = lane < HEAD
    halves = (first.astype(F32).astype(BF16), 1 - first.astype(F32).astype(BF16))
    real_key = lax.broadcasted_iota(jnp.int32, (1, ROWS), 1) < SEQ

    def image_attention(img, carry):
        rows = image_rows(img)

        def pair_attention(pair, inner):
            lanes = pair_lanes(pair)
            q, k, v = qkv[0, rows, lanes], qkv[1, rows, lanes], qkv[2, rows, lanes]
            outs = []
            for h in range(2):
                scores = dot_nt(q * halves[h], k) * (HEAD**-0.5)
                scores = jnp.where(real_key, scores, -1e30)
                raised = jnp.exp(scores - jnp.max(scores, axis=-1, keepdims=True))
                share = raised * (1.0 / jnp.sum(raised, axis=-1, keepdims=True))
                share = share.astype(BF16)
                probs[(img * PAIRS + pair) * 2 + h] = share
                outs.append(dot_nn(share, v))
            mixed[rows, lanes] = jnp.where(first, outs[0], outs[1]).astype(BF16)
            return inner

        return lax.fori_loop(0, PAIRS, pair_attention, carry)

    lax.fori_loop(0, IMGS, image_attention, 0)
    middle[...] = x[...] + (dot_nn(mixed[...], w[3]) + bias_row[:, 3 * D : 4 * D])

    def norm_b(i, carry):
        rows = chunk_rows(i)
        normal, _ = normalize(middle[rows, :])
        xnb[rows, :] = (normal * gain_row[:, D:] + bias_row[:, 4 * D : 5 * D]).astype(BF16)
        return carry

    lax.fori_loop(0, CHUNKS, norm_b, 0)

    def hidden(j, carry):
        tmp[...] = dot_nn(xnb[...], w[4 + j])
        shift = bias_row[:, pl.ds(pl.multiple_of(6 * D + j * D, 128), D)]

        def gelu(i, inner):
            rows = chunk_rows(i)
            pre = tmp[rows, :] + shift
            half = 0.5 * (1.0 + lax.erf(pre * ROOT_HALF))
            act[j, rows, :] = (pre * half).astype(BF16)
            slope[j, rows, :] = (half + pre * jnp.exp(-0.5 * pre * pre) * INV_ROOT_TAU).astype(BF16)
            return inner

        return lax.fori_loop(0, CHUNKS, gelu, carry)

    lax.fori_loop(0, 4, hidden, 0)
    tmp[...] = middle[...] + bias_row[:, 5 * D : 6 * D]
    for j in range(4):
        tmp[...] += dot_nn(act[j], w2[D * j : D * j + D, :])


def column_total(values):
    return jnp.sum(values.astype(F32), axis=0, keepdims=True)


def norm_back(source, gain, grad, tmp, low):
    def step(i, totals):
        rows = chunk_rows(i)
        back = tmp[rows, :]
        normal, inv_std = normalize(source[rows, :])
        scaled = back * gain
        first_mean = jnp.mean(scaled, axis=-1, keepdims=True)
        cross_mean = jnp.mean(scaled * normal, axis=-1, keepdims=True)
        result = grad[rows, :] + inv_std * (scaled - first_mean - normal * cross_mean)
        grad[rows, :] = result
        result_low = result.astype(BF16)
        if low is not None:
            low[rows, :] = result_low
        return (
            totals[0] + jnp.sum(back * normal, axis=0, keepdims=True),
            totals[1] + jnp.sum(back, axis=0, keepdims=True),
            totals[2] + jnp.sum(result_low.astype(F32), axis=0, keepdims=True),
        )

    zero = jnp.zeros((1, D), F32)
    return lax.fori_loop(0, CHUNKS, step, (zero, zero, zero))


def mlp_backward(w, w2, gain_row, mixed, middle, xnb, act, slope, grad, low, gpre, gmix, tmp, dw, dw_out, dw2, dbias, dgain):
    low[...] = grad[...].astype(BF16)
    dbias[:, 5 * D : 6 * D] = column_total(low[...])

    def hidden(j, carry):
        dw2[block_rows(j), :] = dot_tn(act[j], low[...]).astype(BF16)
        pre = (dot_nt(low[...], w2[block_rows(j), :]) * slope[j].astype(F32)).astype(BF16)
        gpre[...] = pre
        dbias[:, pl.ds(pl.multiple_of(6 * D + j * D, 128), D)] = column_total(gpre[...])
        dw[j] = dot_tn(xnb[...], gpre[...]).astype(BF16)
        part = dot_nt(gpre[...], w[4 + j])
        tmp[...] = jnp.where(j == 0, part, tmp[...] + part)
        return carry

    lax.fori_loop(0, 4, hidden, 0)
    gain_two, shift_two, bias_out = norm_back(middle, gain_row[:, D:], grad, tmp, low)
    dgain[:, D:] = gain_two
    dbias[:, 4 * D : 5 * D] = shift_two
    dbias[:, 3 * D : 4 * D] = bias_out
    dw_out[...] = dot_tn(mixed[...], low[...]).astype(BF16)
    gmix[...] = dot_nt(low[...], w[3]).astype(BF16)


def attention_backward(x, w, gain_row, xna, qkv, probs, grad, gqkv, gmix, tmp, dw, dbias, dgain):
    lane = lax.broadcasted_iota(jnp.int32, (1, 128), 1)
    first = lane < HEAD
    halves = (first.astype(F32).astype(BF16), 1 - first.astype(F32).astype(BF16))

    def image_attention(img, carry):
        rows = image_rows(img)

        def pair_attention(pair, inner):
            lanes = pair_lanes(pair)
            q, k, v = qkv[0, rows, lanes], qkv[1, rows, lanes], qkv[2, rows, lanes]
            gm = gmix[rows, lanes]
            grads = ([], [], [])
            for h in range(2):
                share = probs[(img * PAIRS + pair) * 2 + h]
                grad_share = dot_nt(gm * halves[h], v)
                full = share.astype(F32)
                row_dot = jnp.sum(full * grad_share, axis=-1, keepdims=True)
                grad_scores = (full * (grad_share - row_dot)).astype(BF16)
                grads[0].append(dot_nn(grad_scores, k) * (HEAD**-0.5))
                grads[1].append(dot_tn(grad_scores, q) * (HEAD**-0.5))
                grads[2].append(dot_tn(share, gm))
            for b in range(3):
                gqkv[b, rows, lanes] = jnp.where(first, grads[b][0], grads[b][1]).astype(BF16)
            return inner

        return lax.fori_loop(0, PAIRS, pair_attention, carry)

    lax.fori_loop(0, IMGS, image_attention, 0)
    for b in range(3):
        dw[b] = dot_tn(xna[...], gqkv[b]).astype(BF16)
        part = dot_nt(gqkv[b], w[b])
        tmp[...] = part if b == 0 else tmp[...] + part
    dbias[:, D : 2 * D] = column_total(gqkv[0])
    dbias[:, 2 * D : 3 * D] = column_total(gqkv[2])
    gain_one, shift_one, _ = norm_back(x, gain_row[:, :D], grad, tmp, None)
    dgain[:, :D] = gain_one
    dbias[:, :D] = shift_one


def load_images(images, x):
    x[...] = jnp.zeros_like(x)
    for i in range(IMGS):
        x[ROWS * i : ROWS * i + SEQ, :] = images[i].astype(F32)


STATE = (
    ((R, D), BF16),
    ((3, R, D), BF16),
    ((IMGS * PAIRS * 2, ROWS, ROWS), BF16),
    ((R, D), BF16),
    ((R, D), F32),
    ((R, D), BF16),
    ((4, R, D), BF16),
    ((4, R, D), BF16),
)
WEIGHTS = (
    ((BLOCKS, D, D), BF16),
    ((FF, D), BF16),
    ((1, BIAS), F32),
    ((1, GAIN), F32),
)
BIAS_ROW = ((1, BIAS), F32)
GAIN_ROW = ((1, GAIN), F32)
HALF_BLOCKS = ((BLOCKS // 2, D, D), BF16)
MOVE_SCRATCH = (((D, D), BF16), ((2, SLABS, 128), F32))


def wires(blocks, with_w2, with_small):
    rows = (main_rows(blocks, with_w2, with_small), side_rows(blocks, with_w2))
    return [jax.ShapeDtypeStruct((16 * count, 128), BF16) for count in rows] * 2


def shapes(specs):
    return [jax.ShapeDtypeStruct(*spec) for spec in specs]


def scratch(specs):
    return [pltpu.VMEM(*spec) for spec in specs]


def first_forward_kernel(*refs):
    me, images, pieces, refs = refs[0][0], refs[1], refs[2:18], refs[18:]
    stream, weights, state = refs[0], refs[1:5], refs[5:13]
    x, rhs, small = refs[13:]
    assemble(me, pieces, *weights, rhs, small)
    load_images(images, x)
    forward(x, *weights, *state, stream)


def second_layer_kernel(*refs):
    me, live, stream, cotangent, pieces, refs = refs[0][0], refs[1], refs[2], refs[3], refs[4:20], refs[20:]
    activations, grad, sent, refs = refs[0], refs[1], refs[2:6], refs[6:]
    weights, state, refs = refs[:4], refs[4:12], refs[12:]
    low, gpre, gqkv, gmix, tmp, dw, dw2, dbias, dgain, rhs, small = refs
    assemble(me, pieces, *weights, rhs, small)
    forward(stream, *weights, *state, grad)
    for i in range(IMGS):
        alive = jnp.where(live[i] > 0, 1.0, 0.0)
        activations[i] = (grad[ROWS * i : ROWS * i + SEQ, :] * alive).astype(BF16)
    load_images(cotangent, grad)
    for i in range(IMGS):
        alive = jnp.where(live[i] > 0, 1.0, 0.0)
        grad[ROWS * i : ROWS * i + ROWS, :] = grad[ROWS * i : ROWS * i + ROWS, :] * alive
    w, w2, _, gain_row = weights
    xna, qkv, probs, mixed, middle, xnb, act, slope = state
    mlp_backward(
        w, w2, gain_row, mixed, middle, xnb, act, slope, grad, low, gpre, gmix, tmp, dw.at[4:8], dw.at[3], dw2, dbias, dgain
    )
    attention_backward(stream, w, gain_row, xna, qkv, probs, grad, gqkv, gmix, tmp, dw, dbias, dgain)
    disperse(me, dw, dw2, dbias, dgain, sent, rhs, small)


def first_mlp_backward_kernel(
    me, grad_in, w, w2, gain_row, mixed, middle, xnb, act, slope, grad, gmix, dw_out, dbias, dgain, *refs
):
    sent, (low, gpre, tmp, dw, dw2, rhs) = refs[:4], refs[4:]
    grad[...] = grad_in[...]
    dbias[...] = jnp.zeros_like(dbias)
    dgain[...] = jnp.zeros_like(dgain)
    mlp_backward(
        w, w2, gain_row, mixed, middle, xnb, act, slope, grad, low, gpre, gmix, tmp, dw, dw_out, dw2, dbias, dgain
    )
    disperse(me[0], dw, dw2, None, None, sent, rhs, None)


def first_attention_backward_kernel(
    me, images, grad_in, gmix, dw_out, dbias_in, dgain_in, w, gain_row, xna, qkv, probs, input_grad, *refs
):
    sent, (x, grad, gqkv, tmp, dw, dbias, dgain, rhs, small) = refs[:4], refs[4:]
    load_images(images, x)
    grad[...] = grad_in[...]
    dbias[...] = dbias_in[...]
    dgain[...] = dgain_in[...]
    dw[3] = dw_out[...]
    attention_backward(x, w, gain_row, xna, qkv, probs, grad, gqkv, gmix, tmp, dw, dbias, dgain)
    for i in range(IMGS):
        input_grad[i] = grad[ROWS * i : ROWS * i + SEQ, :].astype(BF16)
    disperse(me[0], dw, None, dbias, dgain, sent, rhs, small)


def whole(count):
    return [pl.BlockSpec(memory_space=pltpu.VMEM)] * count


def scalar(count):
    return [pl.BlockSpec(memory_space=pltpu.SMEM)] * count


def params():
    return pltpu.CompilerParams(vmem_limit_bytes=VMEM_LIMIT)


def cost(flops):
    return pl.CostEstimate(flops=flops, bytes_accessed=20_000_000, transcendentals=0)


def run_first_forward(me, images, pieces):
    outs = [jax.ShapeDtypeStruct((R, D), F32)] + shapes(WEIGHTS) + shapes(STATE)
    out = pl.pallas_call(
        first_forward_kernel,
        out_shape=outs,
        in_specs=scalar(1) + whole(17),
        out_specs=whole(len(outs)),
        scratch_shapes=scratch((((R, D), F32),) + MOVE_SCRATCH),
        compiler_params=params(),
        cost_estimate=cost(33_000_000_000),
        name="first_forward",
    )(me, images, *pieces)
    return out[0], out[1:5], out[5:]


def run_second_layer(me, live, stream, cotangent, pieces):
    outs = [jax.ShapeDtypeStruct(cotangent.shape, BF16), jax.ShapeDtypeStruct((R, D), F32)]
    outs += wires(BLOCKS, True, True)
    low, full = ((R, D), BF16), ((R, D), F32)
    back = (low, low, ((3, R, D), BF16), low, full, ((BLOCKS, D, D), BF16), ((FF, D), BF16), BIAS_ROW, GAIN_ROW)
    return pl.pallas_call(
        second_layer_kernel,
        out_shape=outs,
        in_specs=scalar(2) + whole(18),
        out_specs=whole(len(outs)),
        scratch_shapes=scratch(WEIGHTS + STATE + back + MOVE_SCRATCH),
        compiler_params=params(),
        cost_estimate=cost(65_000_000_000),
        name="second_layer",
    )(me, live, stream, cotangent, *pieces)


def run_first_mlp_backward(me, grad, weights, state):
    w, w2, _, gain_row = weights
    low, full = ((R, D), BF16), ((R, D), F32)
    outs = shapes((full, low, ((D, D), BF16), BIAS_ROW, GAIN_ROW)) + wires(BLOCKS // 2, True, False)
    return pl.pallas_call(
        first_mlp_backward_kernel,
        out_shape=outs,
        in_specs=scalar(1) + whole(9),
        out_specs=whole(len(outs)),
        scratch_shapes=scratch((low, low, full, HALF_BLOCKS, ((FF, D), BF16), MOVE_SCRATCH[0])),
        compiler_params=params(),
        cost_estimate=cost(20_000_000_000),
        name="first_mlp_backward",
    )(me, grad, w, w2, gain_row, *state[3:])


def run_first_attention_backward(me, images, grads, weights, state):
    w, _, _, gain_row = weights
    low, full = ((R, D), BF16), ((R, D), F32)
    outs = [jax.ShapeDtypeStruct(images.shape, BF16)] + wires(BLOCKS // 2, False, True)
    back = (full, full, ((3, R, D), BF16), full, HALF_BLOCKS, BIAS_ROW, GAIN_ROW)
    return pl.pallas_call(
        first_attention_backward_kernel,
        out_shape=outs,
        in_specs=scalar(1) + whole(11),
        out_specs=whole(len(outs)),
        scratch_shapes=scratch(back + MOVE_SCRATCH),
        compiler_params=params(),
        cost_estimate=cost(20_000_000_000),
        name="first_attention_backward",
    )(me, images, *grads, w, gain_row, *state[:3])


def chunk_table():
    table = []
    for c in range(3):
        for i in range(12):
            for b in range(3):
                table.append((0, i * 9 + b * 3 + c, c, b * 12 + i))
            table.append((1, i * 3 + c, c, 36 + i))
            for b in range(4):
                table.append((2, i * 12 + b * 3 + c, c, 48 + b * 12 + i))
        for i in range(48):
            table.append((3, i * 3 + c, c, 96 + i))
    return table


def pack_kernel(qkv, out, fc1, fc2, gains, biases, *refs):
    flats, slabs, stages = (qkv, out, fc1, fc2), refs[:4], refs[4:]
    for stage in stages:
        stage[...] = jnp.zeros_like(stage)
    for which, piece, c, row in chunk_table():
        both = flats[which][:, 128 * piece : 128 * piece + 128].astype(F32)
        row += max(c - 1, 0) * THIRD
        for layer in range(LAYERS):
            stages[2 * layer + (c == 0)][row : row + 1, :] = both[layer : layer + 1]
    for layer in range(LAYERS):
        main = stages[2 * layer]
        main[SMALL : SMALL + 1, 0:SHARD_BIAS] = biases[...].astype(F32)[layer : layer + 1]
        main[SMALL + 1 : SMALL + 2, 0:SHARD_GAIN] = gains[...].astype(F32)[layer : layer + 1]
    for slab, stage in zip(slabs, stages):
        slab[...] = stage[...].astype(BF16)


def run_pack(qkv, out, fc1, fc2, gains, biases):
    sizes = [(MAIN, 128), (SIDE, 128)] * LAYERS
    return pl.pallas_call(
        pack_kernel,
        out_shape=[jax.ShapeDtypeStruct(size, BF16) for size in sizes],
        in_specs=whole(6),
        out_specs=whole(4),
        scratch_shapes=[pltpu.VMEM(size, F32) for size in sizes],
        name="pack",
    )(qkv, out, fc1, fc2, gains, biases)


def unpack_kernel(*refs):
    attention, mlp, second, flats, (gains, biases) = refs[:2], refs[2:4], refs[4:6], refs[6:10], refs[10:]
    for which, piece, c, row in chunk_table():
        lanes = slice(128 * piece, 128 * piece + 128)
        place = max(c - 1, 0)
        source, at = (attention, place * 48 + row) if which < 2 else (mlp, place * 96 + row - 48)
        flats[which][0:1, lanes] = source[c == 0][at : at + 1, :]
        at = place * THIRD + row
        flats[which][1:2, lanes] = second[c == 0][at : at + 1, :]
    for layer, (main, row) in enumerate(((attention[0], 96), (second[0], SMALL))):
        biases[layer : layer + 1, :] = main[row : row + 1, 0:SHARD_BIAS]
        gains[layer : layer + 1, :] = main[row + 1 : row + 2, 0:SHARD_GAIN]


def run_unpack(slabs, widths):
    return pl.pallas_call(
        unpack_kernel,
        out_shape=[jax.ShapeDtypeStruct((LAYERS, width), F32) for width in widths],
        in_specs=whole(6),
        out_specs=whole(6),
        name="unpack",
    )(*slabs)


def swap(value, bits):
    return lax.ppermute(value, "fsdp", [(i, i ^ bits) for i in range(SLABS)])


XY_STEPS = (2, 4, 6)
Z_STEPS = (8, 16, 24)


def spread(value, steps):
    return [value] + [swap(value, bits) for bits in steps]


def gather_first(main, side):
    return (
        jnp.concatenate(spread(main, Z_STEPS), axis=0),
        jnp.concatenate(spread(side, XY_STEPS), axis=0),
    )


def gather_second(main, side):
    return spread(main, XY_STEPS) + spread(side, Z_STEPS)


def gather_cores(near):
    far = [swap(part, 1) for part in near]
    return near[:4] + far[:4] + near[4:] + far[4:]


def collect(total, steps):
    rows = total.shape[0] // 4
    mine = total[:rows]
    for place, bits in enumerate(steps):
        part = total[rows * (place + 1) : rows * (place + 2)]
        mine = mine + swap(part.astype(BF16), bits).astype(F32)
    return mine


def scatter_cores(wires):
    return [keep.astype(F32) + swap(send, 1).astype(F32) for keep, send in zip(wires[:2], wires[2:])]


def scatter_first(main, side):
    return [collect(main, XY_STEPS), collect(side, Z_STEPS)]


def scatter_second(main, side):
    return [collect(main, Z_STEPS), collect(side, XY_STEPS)]


def to_slabs(qkv, out, fc1, fc2, gains, biases):
    blocks = jnp.concatenate(
        [
            qkv.reshape(SLABS, 12, 3, D).transpose(0, 2, 1, 3).reshape(SLABS, 36, D),
            out.reshape(SLABS, 12, D),
            fc1.reshape(SLABS, 12, 4, D).transpose(0, 2, 1, 3).reshape(SLABS, 48, D),
            fc2.reshape(SLABS, 48, D),
        ],
        axis=1,
    )
    thirds = blocks.reshape(SLABS, THIRD, 3, 128).transpose(0, 2, 1, 3).reshape(SLABS, 3 * THIRD, 128)
    tail = jnp.zeros((SLABS, MAIN - SMALL, 128), blocks.dtype)
    tail = tail.at[:, 0, :SHARD_BIAS].set(biases.reshape(SLABS, SHARD_BIAS))
    tail = tail.at[:, 1, :SHARD_GAIN].set(gains.reshape(SLABS, SHARD_GAIN))
    return jnp.concatenate([thirds[:, THIRD:], tail], axis=1), thirds[:, :THIRD]


def from_slabs(main, side):
    blocks = jnp.concatenate([side, main[:, :SMALL]], axis=1).reshape(SLABS, 3, THIRD, 128).transpose(0, 2, 1, 3).reshape(SLABS, THIRD, D)
    return (
        blocks[:, :36].reshape(SLABS, 3, 12, D).transpose(0, 2, 1, 3).reshape(-1),
        blocks[:, 36:48].reshape(-1),
        blocks[:, 48:96].reshape(SLABS, 4, 12, D).transpose(0, 2, 1, 3).reshape(-1),
        blocks[:, 96:].reshape(-1),
        main[:, SMALL + 1, :SHARD_GAIN].reshape(-1),
        main[:, SMALL, :SHARD_BIAS].reshape(-1),
    )


def plain_pieces(flats, layer):
    main, side = to_slabs(*(lax.all_gather(flat[layer], "fsdp", axis=0, tiled=True) for flat in flats))
    mains, sides = [], []
    for core in range(2):
        for xy in range(4):
            mains.append(jnp.concatenate([main[core + 2 * xy + 8 * z] for z in range(4)], axis=0))
        for z in range(4):
            sides.append(jnp.concatenate([side[core + 2 * xy + 8 * z] for xy in range(4)], axis=0))
    return mains + sides


def plain_slabs(sent):
    mains, sides = ([wire.reshape(4, 4, -1, 128).astype(F32) for wire in sent[part::2]] for part in range(2))
    main = jnp.stack([mains[d & 1][(d >> 1) & 3, d >> 3] for d in range(SLABS)])
    side = jnp.stack([sides[d & 1][d >> 3, (d >> 1) & 3] for d in range(SLABS)])
    return main, side


def plain_totals(main, side):
    return [lax.psum_scatter(flat, "fsdp", scatter_dimension=0, tiled=True) for flat in from_slabs(main, side)]


def joined_slabs(attention, mlp):
    (main, side), (mlp_main, mlp_side) = plain_slabs(attention), plain_slabs(mlp)
    parts = [main[:, :48], mlp_main[:, :96], main[:, 48:96], mlp_main[:, 96:], main[:, 96:]]
    return jnp.concatenate(parts, axis=1), jnp.concatenate([side, mlp_side], axis=1)


def local(images, live_counts, qkv_weight, out_weight, fc1_weight, fc2_weight, norm_gains, biases, cotangent):
    flats = (qkv_weight, out_weight, fc1_weight, fc2_weight, norm_gains, biases)
    tree = lax.axis_size("fsdp") == SLABS
    if tree:
        me = lax.axis_index("fsdp").astype(jnp.int32).reshape(1)
        main_a, side_a, main_b, side_b = run_pack(*flats)
        first_a = gather_first(main_a, side_a)
        first_a, main_b, side_b = lax.optimization_barrier((first_a, main_b, side_b))
        second_a = gather_second(*first_a)
        first_b = gather_first(main_b, side_b)
        second_a, first_b = lax.optimization_barrier((second_a, first_b))
        pieces_a = gather_cores(second_a)
    else:
        me = jnp.zeros((1,), jnp.int32)
        pieces_a, pieces_b = plain_pieces(flats, 0), plain_pieces(flats, 1)
    stream, weights, state = run_first_forward(me, images, pieces_a)
    if tree:
        second_b, stream = lax.optimization_barrier((gather_second(*first_b), stream))
        pieces_b = gather_cores(second_b)
    activations, grad, *wires_b = run_second_layer(me, live_counts, stream, cotangent, pieces_b)
    if not tree:
        *grads, m0, m1, m2, m3 = run_first_mlp_backward(me, grad, weights, state)
        input_grad, *wires_a = run_first_attention_backward(me, images, grads, weights, state)
        totals_a = plain_totals(*joined_slabs(wires_a, (m0, m1, m2, m3)))
        results = [jnp.stack(both) for both in zip(totals_a, plain_totals(*plain_slabs(wires_b)))]
    else:
        sums_b = scatter_cores(wires_b)
        *grads, m0, m1, m2, m3 = run_first_mlp_backward(me, grad, weights, state)
        sums_b, grads, wires_m = lax.optimization_barrier((sums_b, grads, (m0, m1, m2, m3)))
        halves_b, sums_m = scatter_first(*sums_b), scatter_cores(wires_m)
        input_grad, *wires_a = run_first_attention_backward(me, images, grads, weights, state)
        halves_b, sums_m, wires_a = lax.optimization_barrier((halves_b, sums_m, wires_a))
        slabs_b, halves_m, sums_a = scatter_second(*halves_b), scatter_first(*sums_m), scatter_cores(wires_a)
        slabs_a, slabs_m = scatter_second(*scatter_first(*sums_a)), scatter_second(*halves_m)
        results = run_unpack(slabs_a + slabs_m + slabs_b, [flat.shape[1] for flat in flats])
    return (activations, input_grad, *results)


def solution(mesh):
    flat = P(None, "fsdp")
    image = P("fsdp", None, None)
    return jax.shard_map(
        local,
        mesh=mesh,
        in_specs=(image, P("fsdp")) + (flat,) * 6 + (image,),
        out_specs=(image, image) + (flat,) * 6,
        check_vma=False,
    )
```

time: 265 us -> 270 us (1.019)
  waiting for transfers between devices: 84.6 us -> 43.8 us
  starting transfers between devices: 46.9 us -> 85.7 us
  other arithmetic: 4.38 us -> 8.81 us
    ppermute x34 -> x82, waiting for transfers between devices: 84.6 us -> 43.8 us  [swap(): return lax.ppermute(value, 'fsdp', [(i, i ^ bits) for i in range(SLABS)])]
    ppermute x34 -> x82, starting transfers between devices: 46.9 us -> 85.7 us  [swap(): return lax.ppermute(value, 'fsdp', [(i, i ^ bits) for i in range(SLABS)])]
    pallas_call x2 -> x3, Pallas kernels: 37.1 us -> 40.5 us  [the longest x1 20.6 us: run_first_attention_backward(): pl.pallas_call(first_attention_backward_kernel, out_shape=outs, in_specs=...]
    concatenate x0 -> x4, other arithmetic: none -> 3.37 us  [the longest x2 1.81 us: gather_first(): jnp.concatenate(spread(main, Z_STEPS), axis=0)]
  transfers between devices with their start and end apart: 34 -> 82, of which waited for: 15 -> 28; matrix products, arithmetic and copies ran while one was open for 2% -> 3% of each run, Pallas kernels for 11% -> 25%
where the time goes in v2:
time: 270 us; the launch traced here: 269 us
  Pallas kernels  126 us (47%)
  starting transfers between devices  85.7 us (32%)
  waiting for transfers between devices  43.8 us (16%)
  other arithmetic  8.81 us (3%)
  local copies, waits for them, and re-layouts  3.25 us (1%)
    ppermute x82, starting transfers between devices, swap(): return lax.ppermute(value, 'fsdp', [(i, i ^ bits) for i in range(SLABS)])  85.7 us
    pallas_call x1, Pallas kernels, run_second_layer(): pl.pallas_call(second_layer_kernel, out_shape=outs, in_specs=scalar(2) +...  55.1 us
    ppermute x82, waiting for transfers between devices, swap(): return lax.ppermute(value, 'fsdp', [(i, i ^ bits) for i in range(SLABS)])  43.8 us
    pallas_call x1, Pallas kernels, run_first_forward(): pl.pallas_call(first_forward_kernel, out_shape=outs, in_specs=scalar(1) +...  28.5 us
    pallas_call x1, Pallas kernels, run_first_attention_backward(): pl.pallas_call(first_attention_backward_kernel, out_shape=outs, in_specs=...  20.6 us
    pallas_call x1, Pallas kernels, run_first_mlp_backward(): pl.pallas_call(first_mlp_backward_kernel, out_shape=outs, in_specs=scalar...  18 us
  transfers between devices with their start and end apart: 82, of which 28 were waited for; matrix products, arithmetic and copies ran while one was open for 3% of the time, Pallas kernels for 25%

profile of v2, /device:TPU:0, one launch (start us, length us, event | category | flops | bytes accessed | tf_op | source)
XLA Modules:
  0.0 269.2 jit_solution(15746147273532686974)
XLA Ops:
  0.6 1.9 pack.1
  2.6 3.9 %collective-permute-start.5 = (bf16[144,128]{1,0:T(8,128)(2,1)}, bf16[144,128]{1,0:T(8,128)(2,1)S(1)}, u32[]{:S(2)}, u32[]{:S(2)}) collective-permute-start(bf16[144,128]{1,0:T(8,128)(2,1)} %get-tuple-element.93), channel_id=1, source_target_pairs={{0,6},{1,7},{2,4},{3,5},{4,2},{5,3},{6,0},{7,1},{8,14},{9,15},{10,... | collective-permute-start | bytes 110600 | tf_op jit(solution)/shard_map/ppermute | solution.py:610
  7.1 4.0 %collective-permute-start.2 = (bf16[304,128]{1,0:T(8,128)(2,1)}, bf16[304,128]{1,0:T(8,128)(2,1)S(1)}, u32[]{:S(2)}, u32[]{:S(2)}) collective-permute-start(bf16[304,128]{1,0:T(8,128)(2,1)} %get-tuple-element.92), channel_id=1, source_target_pairs={{0,24},{1,25},{2,26},{3,27},{4,28},{5,29},{6,30},{7,31},{8,16},{9,... | collective-permute-start | bytes 233480 | tf_op jit(solution)/shard_map/ppermute | solution.py:610
  14.3 3.0 %collective-permute-done.1 = bf16[304,128]{1,0:T(8,128)(2,1)S(1)} collective-permute-done((bf16[304,128]{1,0:T(8,128)(2,1)}, bf16[304,128]{1,0:T(8,128)(2,1)S(1)}, u32[]{:S(2)}, u32[]{:S(2)}) %collective-permute-start.1) | collective-permute-done | bytes 77856 | tf_op jit(solution)/shard_map/ppermute | solution.py:610
  18.2 2.5 collective-permute-start.14
  20.7 2.4 collective-permute-start.17
  25.8 2.0 collective-permute-start.11
  29.3 2.4 collective-permute-start.8
  37.5 4.0 %collective-permute-done.10.refs_12_ = bf16[576,128]{1,0:T(8,128)(2,1)S(1)} collective-permute-done((bf16[576,128]{1,0:T(8,128)(2,1)S(1)}, bf16[576,128]{1,0:T(8,128)(2,1)S(1)}, u32[]{:S(2)}, u32[]{:S(2)}) %collective-permute-start.10) | collective-permute-done | bytes 147488 | tf_op jit(solution)/shard_map/ppermute | solution.py:610
  49.1 6.5 %collective-permute-done.23.refs_15_ = bf16[576,128]{1,0:T(8,128)(2,1)S(1)} collective-permute-done((bf16[576,128]{1,0:T(8,128)(2,1)S(1)}, bf16[576,128]{1,0:T(8,128)(2,1)S(1)}, u32[]{:S(2)}, u32[]{:S(2)}) %collective-permute-start.23) | collective-permute-done | bytes 147488 | tf_op jit(solution)/shard_map/ppermute | solution.py:610
  61.3 28.5 %first_forward.1 = (f32[624,384]{1,0:T(8,128)}, bf16[8,384,384]{2,1,0:T(8,128)(2,1)}, bf16[1536,384]{1,0:T(8,128)(2,1)}, f32[1,3840]{1,0:T(1,128)}, f32[1,768]{1...) custom-call(s32[1]{0:T(128)} %bitcast.refs_0_.me, ...), custom_call_target="tpu_custom_call" | custom-call | flops 32999999488 | bytes 20000000 | tf_op jit(solution)/shard_map/first_forward/pallas_call | solution.py:479
  96.8 55.1 %second_layer.1 = (bf16[3,197,384]{2,1,0:T(8,128)(2,1)}, f32[624,384]{1,0:T(8,128)}, bf16[4864,128]{1,0:T(8,128)(2,1)}, bf16[2304,128]{1,0:T(8,128)(2,1)}, bf16[...) custom-call(s32[1]{0:T(128)} %bitcast.refs_0_.me, s32[3]{0:T(128)} %refs_1_.3, f32[624,384]{1,0:T(8,128)} %get-tuple-element.111.refs_2_, ...), custom_call_target="tpu_custom_call" | custom-call | flops 65000001536 | bytes 20000000 | tf_op jit(solution)/shard_map/second_layer/pallas_call | solution.py:497
  152.4 18.0 %first_mlp_backward.1 = (f32[624,384]{1,0:T(8,128)}, bf16[624,384]{1,0:T(8,128)(2,1)}, bf16[384,384]{1,0:T(8,128)(2,1)}, f32[1,3840]{1,0:T(1,128)}, f32[1,768]{1...) custom-call(s32[1]{0:T(128)} %bitcast.refs_0_.me, ...), custom_call_target="tpu_custom_call" | custom-call | flops 20000000000 | bytes 20000000 | tf_op jit(solution)/shard_map/first_mlp_backward/pallas_call | solution.py:513
  172.0 1.9 collective-permute-start.45
  174.0 2.3 collective-permute-start.47
  180.0 20.6 %first_attention_backward.1 = (bf16[3,197,384]{2,1,0:T(8,128)(2,1)}, bf16[1792,128]{1,0:T(8,128)(2,1)}, bf16[768,128]{1,0:T(8,128)(2,1)}, bf16[1792,128]{1,0:T(8,128)(2,1)}, bf16[768,128]{1,0:T(8,128)(2,1)}) custom-call(s32[1]{0:T(128)} %bitcast.refs_0_.me, bf16[3,197,384]{2,1,0:T(8,128)(2,1)} %images.1, f32[624,384]{1,0:T(8,128)} %get-tuple-element.143.grad_in, ...), custom_call_target="tpu_custom_call" | custom-call | flops 20000000000 | bytes 20000000 | tf_op jit(solution)/shard_map/first_attention_backward/pallas_call | solution.py:530
  207.4 2.2 collective-permute-start.76
  210.0 2.2 collective-permute-start.72
  214.8 2.3 collective-permute-start.78
  217.1 2.2 collective-permute-done.72
  219.3 5.8 %collective-permute-start.77 = (bf16[304,128]{1,0:T(8,128)(2,1)S(1)}, bf16[304,128]{1,0:T(8,128)(2,1)S(1)}, u32[]{:S(2)}, u32[]{:S(2)}) collective-permute-start(bf16[304,128]{1,0:T(8,128)(2,1)S(1)} %get-tuple-element.205), channel_id=1, source_target_pairs={{0,16},{1,17},{2,18},{3,19},{4,20},{5,21},{6,22},{7,23},{8,24},{9,... | collective-permute-start | bytes 233480 | tf_op jit(solution)/shard_map/ppermute | solution.py:610
  235.9 2.8 %collective-permute-done.64 = bf16[768,128]{1,0:T(8,128)(2,1)S(1)} collective-permute-done((bf16[768,128]{1,0:T(8,128)(2,1)S(1)}, bf16[768,128]{1,0:T(8,128)(2,1)S(1)}, u32[]{:S(2)}, u32[]{:S(2)}) %collective-permute-start.64) | collective-permute-done | bytes 196640 | tf_op jit(solution)/shard_map/ppermute | solution.py:610
  262.3 3.0 %collective-permute-done.56 = bf16[112,128]{1,0:T(8,128)(2,1)S(1)} collective-permute-done((bf16[112,128]{1,0:T(8,128)(2,1)S(1)}, bf16[112,128]{1,0:T(8,128)(2,1)S(1)}, u32[]{:S(2)}, u32[]{:S(2)}) %collective-permute-start.56) | collective-permute-done | bytes 28704 | tf_op jit(solution)/shard_map/ppermute | solution.py:610
  267.1 2.2 unpack.1
  (266 shorter events, 86.0 us)
Async XLA Ops:
  18.2 13.5 %collective-permute-start.14 = (bf16[304,128]{1,0:T(8,128)(2,1)}, bf16[304,128]{1,0:T(8,128)(2,1)S(1)}, u32[]{:S(2)}, u32[]{:S(2)}) collective-permute-start(bf16[304,128]{1,0:T(8,128)(2,1)} %get-tuple-element.98), channel_id=1, source_target_pairs={{0,24},{1,25},{2,26},{3,27},{4,28},{5,29},{6,30},{7,31},{8,16},{9,... | collective-permute-start | bytes 233480 | tf_op jit(solution)/shard_map/ppermute | solution.py:610
  29.3 12.7 %collective-permute-start.8 = (bf16[1216,128]{1,0:T(8,128)(2,1)S(1)}, bf16[1216,128]{1,0:T(8,128)(2,1)S(1)}, u32[]{:S(2)}, u32[]{:S(2)}) collective-permute-start(bf16[1216,128]{1,0:T(8,128)(2,1)S(1)} %pad_maximum_fusion.refs_2_), channel_id=1, source_target_pairs={{0,6},{1,7},{2,4},{3,5},{4,2},{5,3},{6,0},{7,1},{8,14},{9,15},{10,... | collective-permute-start | bytes 933896 | tf_op jit(solution)/shard_map/ppermute | solution.py:610
  44.4 13.1 %collective-permute-start.24 = (bf16[1216,128]{1,0:T(8,128)(2,1)S(1)}, bf16[1216,128]{1,0:T(8,128)(2,1)S(1)}, u32[]{:S(2)}, u32[]{:S(2)}) collective-permute-start(bf16[1216,128]{1,0:T(8,128)(2,1)S(1)} %pad_maximum_fusion.refs_2_), channel_id=1, source_target_pairs={{0,1},{1,0},{2,3},{3,2},{4,5},{5,4},{6,7},{7,6},{8,9},{9,8},{10,11... | collective-permute-start | bytes 933896 | tf_op jit(solution)/shard_map/ppermute | solution.py:610
  44.8 12.8 %collective-permute-start.25 = (bf16[1216,128]{1,0:T(8,128)(2,1)S(1)}, bf16[1216,128]{1,0:T(8,128)(2,1)S(1)}, u32[]{:S(2)}, u32[]{:S(2)}) collective-permute-start(bf16[1216,128]{1,0:T(8,128)(2,1)S(1)} %collective-permute-done.6.refs_3_), channel_id=1, source_target_pairs={{0,1},{1,0},{2,3},{3,2},{4,5},{5,4},{6,7},{7,6},{8,9},{9,8},{10,11... | collective-permute-start | bytes 933896 | tf_op jit(solution)/shard_map/ppermute | solution.py:610
  45.3 14.0 %collective-permute-start.26 = (bf16[1216,128]{1,0:T(8,128)(2,1)S(1)}, bf16[1216,128]{1,0:T(8,128)(2,1)S(1)}, u32[]{:S(2)}, u32[]{:S(2)}) collective-permute-start(bf16[1216,128]{1,0:T(8,128)(2,1)S(1)} %collective-permute-done.7.refs_4_), channel_id=1, source_target_pairs={{0,1},{1,0},{2,3},{3,2},{4,5},{5,4},{6,7},{7,6},{8,9},{9,8},{10,11... | collective-permute-start | bytes 933896 | tf_op jit(solution)/shard_map/ppermute | solution.py:610
  45.5 15.1 %collective-permute-start.27 = (bf16[1216,128]{1,0:T(8,128)(2,1)S(1)}, bf16[1216,128]{1,0:T(8,128)(2,1)S(1)}, u32[]{:S(2)}, u32[]{:S(2)}) collective-permute-start(bf16[1216,128]{1,0:T(8,128)(2,1)S(1)} %collective-permute-done.8.refs_5_), channel_id=1, source_target_pairs={{0,1},{1,0},{2,3},{3,2},{4,5},{5,4},{6,7},{7,6},{8,9},{9,8},{10,11... | collective-permute-start | bytes 933896 | tf_op jit(solution)/shard_map/ppermute | solution.py:610
  55.7 34.2 %collective-permute-start.22 = (bf16[576,128]{1,0:T(8,128)(2,1)S(1)}, bf16[576,128]{1,0:T(8,128)(2,1)S(1)}, u32[]{:S(2)}, u32[]{:S(2)}) collective-permute-start(bf16[576,128]{1,0:T(8,128)(2,1)S(1)} %pad_maximum_fusion.3.refs_12_), channel_id=1, source_target_pairs={{0,16},{1,17},{2,18},{3,19},{4,20},{5,21},{6,22},{7,23},{8,24},{9,... | collective-permute-start | bytes 442376 | tf_op jit(solution)/shard_map/ppermute | solution.py:610
  57.5 32.3 %collective-permute-start.21 = (bf16[576,128]{1,0:T(8,128)(2,1)S(1)}, bf16[576,128]{1,0:T(8,128)(2,1)S(1)}, u32[]{:S(2)}, u32[]{:S(2)}) collective-permute-start(bf16[576,128]{1,0:T(8,128)(2,1)S(1)} %pad_maximum_fusion.3.refs_12_), channel_id=1, source_target_pairs={{0,8},{1,9},{2,10},{3,11},{4,12},{5,13},{6,14},{7,15},{8,0},{9,1},... | collective-permute-start | bytes 442376 | tf_op jit(solution)/shard_map/ppermute | solution.py:610
  57.6 32.3 %collective-permute-start.20 = (bf16[1216,128]{1,0:T(8,128)(2,1)S(1)}, bf16[1216,128]{1,0:T(8,128)(2,1)S(1)}, u32[]{:S(2)}, u32[]{:S(2)}) collective-permute-start(bf16[1216,128]{1,0:T(8,128)(2,1)S(1)} %pad_maximum_fusion.1.refs_4_), channel_id=1, source_target_pairs={{0,6},{1,7},{2,4},{3,5},{4,2},{5,3},{6,0},{7,1},{8,14},{9,15},{10,... | collective-permute-start | bytes 933896 | tf_op jit(solution)/shard_map/ppermute | solution.py:610
  59.4 30.6 %collective-permute-start.19 = (bf16[1216,128]{1,0:T(8,128)(2,1)S(1)}, bf16[1216,128]{1,0:T(8,128)(2,1)S(1)}, u32[]{:S(2)}, u32[]{:S(2)}) collective-permute-start(bf16[1216,128]{1,0:T(8,128)(2,1)S(1)} %pad_maximum_fusion.1.refs_4_), channel_id=1, source_target_pairs={{0,4},{1,5},{2,6},{3,7},{4,0},{5,1},{6,2},{7,3},{8,12},{9,13},{10,... | collective-permute-start | bytes 933896 | tf_op jit(solution)/shard_map/ppermute | solution.py:610
  60.6 29.3 %collective-permute-start.18 = (bf16[1216,128]{1,0:T(8,128)(2,1)S(1)}, bf16[1216,128]{1,0:T(8,128)(2,1)S(1)}, u32[]{:S(2)}, u32[]{:S(2)}) collective-permute-start(bf16[1216,128]{1,0:T(8,128)(2,1)S(1)} %pad_maximum_fusion.1.refs_4_), channel_id=1, source_target_pairs={{0,2},{1,3},{2,0},{3,1},{4,6},{5,7},{6,4},{7,5},{8,10},{9,11},{10,... | collective-permute-start | bytes 933896 | tf_op jit(solution)/shard_map/ppermute | solution.py:610
  151.9 18.5 %collective-permute-start.41 = (bf16[2304,128]{1,0:T(8,128)(2,1)}, bf16[2304,128]{1,0:T(8,128)(2,1)S(1)}, u32[]{:S(2)}, u32[]{:S(2)}) collective-permute-start(bf16[2304,128]{1,0:T(8,128)(2,1)} %get-tuple-element.124), channel_id=1, source_target_pairs={{0,1},{1,0},{2,3},{3,2},{4,5},{5,4},{6,7},{7,6},{8,9},{9,8},{10,11... | collective-permute-start | bytes 1769480 | tf_op jit(solution)/shard_map/ppermute | solution.py:610
  152.1 18.4 %collective-permute-start.40 = (bf16[4864,128]{1,0:T(8,128)(2,1)}, bf16[4864,128]{1,0:T(8,128)(2,1)S(1)}, u32[]{:S(2)}, u32[]{:S(2)}) collective-permute-start(bf16[4864,128]{1,0:T(8,128)(2,1)} %get-tuple-element.122), channel_id=1, source_target_pairs={{0,1},{1,0},{2,3},{3,2},{4,5},{5,4},{6,7},{7,6},{8,9},{9,8},{10,11... | collective-permute-start | bytes 3735560 | tf_op jit(solution)/shard_map/ppermute | solution.py:610
  174.0 26.6 %collective-permute-start.47 = (bf16[576,128]{1,0:T(8,128)(2,1)S(1)}, bf16[576,128]{1,0:T(8,128)(2,1)S(1)}, u32[]{:S(2)}, u32[]{:S(2)}) collective-permute-start(bf16[576,128]{1,0:T(8,128)(2,1)S(1)} %get-tuple-element.193), channel_id=1, source_target_pairs={{0,24},{1,25},{2,26},{3,27},{4,28},{5,29},{6,30},{7,31},{8,16},{9,... | collective-permute-start | bytes 442376 | tf_op jit(solution)/shard_map/ppermute | solution.py:610
  176.2 24.5 %collective-permute-start.46 = (bf16[576,128]{1,0:T(8,128)(2,1)S(1)}, bf16[576,128]{1,0:T(8,128)(2,1)S(1)}, u32[]{:S(2)}, u32[]{:S(2)}) collective-permute-start(bf16[576,128]{1,0:T(8,128)(2,1)S(1)} %get-tuple-element.194), channel_id=1, source_target_pairs={{0,16},{1,17},{2,18},{3,19},{4,20},{5,21},{6,22},{7,23},{8,24},{9,... | collective-permute-start | bytes 442376 | tf_op jit(solution)/shard_map/ppermute | solution.py:610
  176.4 24.8 %collective-permute-start.42 = (bf16[1216,128]{1,0:T(8,128)(2,1)S(1)}, bf16[1216,128]{1,0:T(8,128)(2,1)S(1)}, u32[]{:S(2)}, u32[]{:S(2)}) collective-permute-start(bf16[1216,128]{1,0:T(8,128)(2,1)S(1)} %get-tuple-element.184), channel_id=1, source_target_pairs={{0,2},{1,3},{2,0},{3,1},{4,6},{5,7},{6,4},{7,5},{8,10},{9,11},{10,... | collective-permute-start | bytes 933896 | tf_op jit(solution)/shard_map/ppermute | solution.py:610
  177.4 23.9 %collective-permute-start.44 = (bf16[1216,128]{1,0:T(8,128)(2,1)S(1)}, bf16[1216,128]{1,0:T(8,128)(2,1)S(1)}, u32[]{:S(2)}, u32[]{:S(2)}) collective-permute-start(bf16[1216,128]{1,0:T(8,128)(2,1)S(1)} %get-tuple-element.185), channel_id=1, source_target_pairs={{0,6},{1,7},{2,4},{3,5},{4,2},{5,3},{6,0},{7,1},{8,14},{9,15},{10,... | collective-permute-start | bytes 933896 | tf_op jit(solution)/shard_map/ppermute | solution.py:610
  179.1 22.2 %collective-permute-start.43 = (bf16[1216,128]{1,0:T(8,128)(2,1)S(1)}, bf16[1216,128]{1,0:T(8,128)(2,1)S(1)}, u32[]{:S(2)}, u32[]{:S(2)}) collective-permute-start(bf16[1216,128]{1,0:T(8,128)(2,1)S(1)} %get-tuple-element.186), channel_id=1, source_target_pairs={{0,4},{1,5},{2,6},{3,7},{4,0},{5,1},{6,2},{7,3},{8,12},{9,13},{10,... | collective-permute-start | bytes 933896 | tf_op jit(solution)/shard_map/ppermute | solution.py:610
  207.3 27.7 %collective-permute-start.57 = (bf16[768,128]{1,0:T(8,128)(2,1)S(1)}, bf16[768,128]{1,0:T(8,128)(2,1)S(1)}, u32[]{:S(2)}, u32[]{:S(2)}) collective-permute-start(bf16[768,128]{1,0:T(8,128)(2,1)S(1)} %copy-done.27), channel_id=1, source_target_pairs={{0,1},{1,0},{2,3},{3,2},{4,5},{5,4},{6,7},{7,6},{8,9},{9,8},{10,11... | collective-permute-start | bytes 589832 | tf_op jit(solution)/shard_map/ppermute | solution.py:610
  207.4 18.0 %collective-permute-start.76 = (bf16[304,128]{1,0:T(8,128)(2,1)S(1)}, bf16[304,128]{1,0:T(8,128)(2,1)S(1)}, u32[]{:S(2)}, u32[]{:S(2)}) collective-permute-start(bf16[304,128]{1,0:T(8,128)(2,1)S(1)} %get-tuple-element.203), channel_id=1, source_target_pairs={{0,8},{1,9},{2,10},{3,11},{4,12},{5,13},{6,14},{7,15},{8,0},{9,1},... | collective-permute-start | bytes 233480 | tf_op jit(solution)/shard_map/ppermute | solution.py:610
  212.2 13.1 %collective-permute-start.71 = (bf16[384,128]{1,0:T(8,128)(2,1)S(1)}, bf16[384,128]{1,0:T(8,128)(2,1)S(1)}, u32[]{:S(2)}, u32[]{:S(2)}) collective-permute-start(bf16[384,128]{1,0:T(8,128)(2,1)S(1)} %get-tuple-element.200), channel_id=1, source_target_pairs={{0,16},{1,17},{2,18},{3,19},{4,20},{5,21},{6,22},{7,23},{8,24},{9,... | collective-permute-start | bytes 294920 | tf_op jit(solution)/shard_map/ppermute | solution.py:610
  225.3 23.0 %collective-permute-start.50 = (bf16[1792,128]{1,0:T(8,128)(2,1)S(1)}, bf16[1792,128]{1,0:T(8,128)(2,1)S(1)}, u32[]{:S(2)}, u32[]{:S(2)}) collective-permute-start(bf16[1792,128]{1,0:T(8,128)(2,1)S(1)} %copy-done.11), channel_id=1, source_target_pairs={{0,1},{1,0},{2,3},{3,2},{4,5},{5,4},{6,7},{7,6},{8,9},{9,8},{10,11... | collective-permute-start | bytes 1376264 | tf_op jit(solution)/shard_map/ppermute | solution.py:610
  246.8 14.5 %collective-permute-start.61 = (bf16[48,128]{1,0:T(8,128)(2,1)S(1)}, bf16[48,128]{1,0:T(8,128)(2,1)S(1)}, u32[]{:S(2)}, u32[]{:S(2)}) collective-permute-start(bf16[48,128]{1,0:T(8,128)(2,1)S(1)} %get-tuple-element.221), channel_id=1, source_target_pairs={{0,2},{1,3},{2,0},{3,1},{4,6},{5,7},{6,4},{7,5},{8,10},{9,11},{10,... | collective-permute-start | bytes 36872 | tf_op jit(solution)/shard_map/ppermute | solution.py:610
  248.3 13.4 %collective-permute-start.63 = (bf16[48,128]{1,0:T(8,128)(2,1)S(1)}, bf16[48,128]{1,0:T(8,128)(2,1)S(1)}, u32[]{:S(2)}, u32[]{:S(2)}) collective-permute-start(bf16[48,128]{1,0:T(8,128)(2,1)S(1)} %get-tuple-element.222), channel_id=1, source_target_pairs={{0,6},{1,7},{2,4},{3,5},{4,2},{5,3},{6,0},{7,1},{8,14},{9,15},{10,... | collective-permute-start | bytes 36872 | tf_op jit(solution)/shard_map/ppermute | solution.py:610
  (98 other events, 862.7 us)

commit v3 on v2

--- a/solution.py
+++ b/solution.py
@@ -23,9 +23,8 @@
 
 SLABS = 32
 THIRD = 144
-SMALL = 2 * THIRD
-MAIN = SMALL + 16
-SIDE = THIRD
+SMALL = 3 * THIRD
+SLAB = SMALL + 16
 BLOCKS = 8
 SHARD_BIAS = 120
 SHARD_GAIN = 24
@@ -103,7 +102,7 @@
     return jnp.where(rows == place, 1.0, 0.0).astype(BF16)
 
 
-def assemble(me, pieces, w, w2, bias_row, gain_row, rhs, small):
+def assemble(me, place, w, w2, bias_row, gain_row, rhs, small):
     low = jnp.bitwise_and(me, 3)
     order = jnp.where(
         order_codes((D, 1), 0) == slab_codes((1, D), 1, low, BLOCKS), 1.0, 0.0
@@ -115,16 +114,15 @@
             for xr in range(2):
                 for cr in range(2):
                     xy = xr + 2 * yr
-                    main, side = pieces[4 * cr + xy], pieces[8 + 4 * cr + zr]
+                    piece, base = place(cr, xy, zr)
                     d = jnp.bitwise_xor(me, cr + 2 * xy + 8 * zr)
                     s = xr * 2 + cr
                     for c in range(3):
                         lanes = slice(128 * c, 128 * c + 128)
-                        piece = main if c else side
-                        base = zr * MAIN + (c - 1) * THIRD if c else xy * SIDE
-                        rhs[96 * s : 96 * s + 96, lanes] = piece[base : base + 96, :]
-                        w2[pl.ds(pl.multiple_of(48 * d, 16), 48), lanes] = piece[base + 96 : base + THIRD, :]
-                    tail = main[zr * MAIN + SMALL : zr * MAIN + MAIN, :].astype(F32)
+                        start = base + c * THIRD
+                        rhs[96 * s : 96 * s + 96, lanes] = piece[start : start + 96, :]
+                        w2[pl.ds(pl.multiple_of(48 * d, 16), 48), lanes] = piece[start + 96 : start + THIRD, :]
+                    tail = piece[base + SMALL : base + SLAB, :].astype(F32)
                     small[0, pl.ds(d, 1), :] = tail[0:1, :]
                     small[1, pl.ds(d, 1), :] = tail[1:2, :]
             sorted_rows = dot_nn(order, rhs[...]).astype(BF16)
@@ -136,19 +134,15 @@
         row[...] = jnp.sum(jnp.where(mine, spread, 0.0), axis=0, keepdims=True)
 
 
-def main_rows(blocks, with_w2, with_small):
-    return 2 * side_rows(blocks, with_w2) + 16 * with_small
-
-
-def side_rows(blocks, with_w2):
-    return 12 * blocks + 48 * with_w2
+def slab_rows(blocks, with_w2, with_small):
+    return 3 * (12 * blocks + 48 * with_w2) + 16 * with_small
 
 
 def disperse(me, dw, dw2, bias_row, gain_row, wires, rhs, small):
     blocks = dw.shape[0]
     size = 48 * blocks
-    third = side_rows(blocks, dw2 is not None)
-    stride = main_rows(blocks, dw2 is not None, bias_row is not None)
+    third = slab_rows(blocks, dw2 is not None, False) // 3
+    stride = slab_rows(blocks, dw2 is not None, bias_row is not None)
     low = jnp.bitwise_and(me, 3)
     order = jnp.where(
         slab_codes((size, 1), 0, low, blocks) == order_codes((1, size), 1), 1.0, 0.0
@@ -168,17 +162,14 @@
             slabs = dot_nn(order, rhs[0:size, :]).astype(BF16)
             for xr in range(2):
                 for cr in range(2):
-                    main, side = wires[2 * cr : 2 * cr + 2]
+                    out = wires[cr]
                     xy = xr + 2 * yr
                     d = jnp.bitwise_xor(me, cr + 2 * xy + 8 * zr)
                     s = xr * 2 + cr
                     base = pl.multiple_of(xy * (4 * stride) + zr * stride, 16)
                     for c in range(3):
                         lanes = slice(128 * c, 128 * c + 128)
-                        if c:
-                            out, start = main, base + (c - 1) * third
-                        else:
-                            out, start = side, pl.multiple_of(zr * (4 * third) + xy * third, 16)
+                        start = base + c * third
                         rows = 12 * blocks
                         out[pl.ds(start, rows), :] = slabs[rows * s : rows * s + rows, lanes]
                         if dw2 is not None:
@@ -189,7 +180,7 @@
                             small[0, pl.ds(d, 1), :],
                             jnp.where(head_row == 1, small[1, pl.ds(d, 1), :], 0.0),
                         )
-                        main[pl.ds(base + 2 * third, 16), :] = tail.astype(BF16)
+                        out[pl.ds(base + 3 * third, 16), :] = tail.astype(BF16)
         return carry
 
     lax.fori_loop(0, 4, group, 0)
@@ -317,7 +308,7 @@
     gmix[...] = dot_nt(low[...], w[3]).astype(BF16)
 
 
-def attention_backward(x, w, gain_row, xna, qkv, probs, grad, gqkv, gmix, tmp, dw, dbias, dgain):
+def attention_backward(qkv, probs, gmix, gqkv):
     lane = lax.broadcasted_iota(jnp.int32, (1, 128), 1)
     first = lane < HEAD
     halves = (first.astype(F32).astype(BF16), 1 - first.astype(F32).astype(BF16))
@@ -346,6 +337,9 @@
         return lax.fori_loop(0, PAIRS, pair_attention, carry)
 
     lax.fori_loop(0, IMGS, image_attention, 0)
+
+
+def projection_backward(x, w, gain_row, xna, gqkv, grad, tmp, dw, dbias, dgain):
     for b in range(3):
         dw[b] = dot_tn(xna[...], gqkv[b]).astype(BF16)
         part = dot_nt(gqkv[b], w[b])
@@ -385,9 +379,8 @@
 MOVE_SCRATCH = (((D, D), BF16), ((2, SLABS, 128), F32))
 
 
-def wires(blocks, with_w2, with_small):
-    rows = (main_rows(blocks, with_w2, with_small), side_rows(blocks, with_w2))
-    return [jax.ShapeDtypeStruct((16 * count, 128), BF16) for count in rows] * 2
+def wires(*part):
+    return [jax.ShapeDtypeStruct((16 * slab_rows(*part), 128), BF16)] * 2
 
 
 def shapes(specs):
@@ -399,20 +392,20 @@
 
 
 def first_forward_kernel(*refs):
-    me, images, pieces, refs = refs[0][0], refs[1], refs[2:18], refs[18:]
+    me, images, pieces, refs = refs[0][0], refs[1], refs[2:10], refs[10:]
     stream, weights, state = refs[0], refs[1:5], refs[5:13]
     x, rhs, small = refs[13:]
-    assemble(me, pieces, *weights, rhs, small)
+    assemble(me, lambda core, xy, z: (pieces[4 * core + xy], z * SLAB), *weights, rhs, small)
     load_images(images, x)
     forward(x, *weights, *state, stream)
 
 
 def second_layer_kernel(*refs):
-    me, live, stream, cotangent, pieces, refs = refs[0][0], refs[1], refs[2], refs[3], refs[4:20], refs[20:]
-    activations, grad, sent, refs = refs[0], refs[1], refs[2:6], refs[6:]
+    me, live, stream, cotangent, slabs, refs = refs[0][0], refs[1], refs[2], refs[3], refs[4], refs[5:]
+    activations, grad, sent, refs = refs[0], refs[1], refs[2:4], refs[4:]
     weights, state, refs = refs[:4], refs[4:12], refs[12:]
     low, gpre, gqkv, gmix, tmp, dw, dw2, dbias, dgain, rhs, small = refs
-    assemble(me, pieces, *weights, rhs, small)
+    assemble(jnp.int32(0), lambda core, xy, z: (slabs, (core + 2 * xy + 8 * z) * SLAB), *weights, rhs, small)
     forward(stream, *weights, *state, grad)
     for i in range(IMGS):
         alive = jnp.where(live[i] > 0, 1.0, 0.0)
@@ -426,14 +419,15 @@
     mlp_backward(
         w, w2, gain_row, mixed, middle, xnb, act, slope, grad, low, gpre, gmix, tmp, dw.at[4:8], dw.at[3], dw2, dbias, dgain
     )
-    attention_backward(stream, w, gain_row, xna, qkv, probs, grad, gqkv, gmix, tmp, dw, dbias, dgain)
+    attention_backward(qkv, probs, gmix, gqkv)
+    projection_backward(stream, w, gain_row, xna, gqkv, grad, tmp, dw, dbias, dgain)
     disperse(me, dw, dw2, dbias, dgain, sent, rhs, small)
 
 
 def first_mlp_backward_kernel(
     me, grad_in, w, w2, gain_row, mixed, middle, xnb, act, slope, grad, gmix, dw_out, dbias, dgain, *refs
 ):
-    sent, (low, gpre, tmp, dw, dw2, rhs) = refs[:4], refs[4:]
+    sent, (low, gpre, tmp, dw, dw2, rhs) = refs[:2], refs[2:]
     grad[...] = grad_in[...]
     dbias[...] = jnp.zeros_like(dbias)
     dgain[...] = jnp.zeros_like(dgain)
@@ -443,16 +437,20 @@
     disperse(me[0], dw, dw2, None, None, sent, rhs, None)
 
 
-def first_attention_backward_kernel(
-    me, images, grad_in, gmix, dw_out, dbias_in, dgain_in, w, gain_row, xna, qkv, probs, input_grad, *refs
+def first_attention_backward_kernel(qkv, probs, gmix, gqkv):
+    attention_backward(qkv, probs, gmix, gqkv)
+
+
+def first_projection_backward_kernel(
+    me, images, grad_in, gqkv, dw_out, dbias_in, dgain_in, w, gain_row, xna, input_grad, *refs
 ):
-    sent, (x, grad, gqkv, tmp, dw, dbias, dgain, rhs, small) = refs[:4], refs[4:]
+    sent, (x, grad, tmp, dw, dbias, dgain, rhs, small) = refs[:2], refs[2:]
     load_images(images, x)
     grad[...] = grad_in[...]
     dbias[...] = dbias_in[...]
     dgain[...] = dgain_in[...]
     dw[3] = dw_out[...]
-    attention_backward(x, w, gain_row, xna, qkv, probs, grad, gqkv, gmix, tmp, dw, dbias, dgain)
+    projection_backward(x, w, gain_row, xna, gqkv, grad, tmp, dw, dbias, dgain)
     for i in range(IMGS):
         input_grad[i] = grad[ROWS * i : ROWS * i + SEQ, :].astype(BF16)
     disperse(me[0], dw, None, dbias, dgain, sent, rhs, small)
@@ -479,7 +477,7 @@
     out = pl.pallas_call(
         first_forward_kernel,
         out_shape=outs,
-        in_specs=scalar(1) + whole(17),
+        in_specs=scalar(1) + whole(9),
         out_specs=whole(len(outs)),
         scratch_shapes=scratch((((R, D), F32),) + MOVE_SCRATCH),
         compiler_params=params(),
@@ -489,7 +487,7 @@
     return out[0], out[1:5], out[5:]
 
 
-def run_second_layer(me, live, stream, cotangent, pieces):
+def run_second_layer(me, live, stream, cotangent, slabs):
     outs = [jax.ShapeDtypeStruct(cotangent.shape, BF16), jax.ShapeDtypeStruct((R, D), F32)]
     outs += wires(BLOCKS, True, True)
     low, full = ((R, D), BF16), ((R, D), F32)
@@ -497,13 +495,13 @@
     return pl.pallas_call(
         second_layer_kernel,
         out_shape=outs,
-        in_specs=scalar(2) + whole(18),
+        in_specs=scalar(2) + whole(3),
         out_specs=whole(len(outs)),
         scratch_shapes=scratch(WEIGHTS + STATE + back + MOVE_SCRATCH),
         compiler_params=params(),
         cost_estimate=cost(65_000_000_000),
         name="second_layer",
-    )(me, live, stream, cotangent, *pieces)
+    )(me, live, stream, cotangent, slabs)
 
 
 def run_first_mlp_backward(me, grad, weights, state):
@@ -522,21 +520,32 @@
     )(me, grad, w, w2, gain_row, *state[3:])
 
 
-def run_first_attention_backward(me, images, grads, weights, state):
-    w, _, _, gain_row = weights
-    low, full = ((R, D), BF16), ((R, D), F32)
-    outs = [jax.ShapeDtypeStruct(images.shape, BF16)] + wires(BLOCKS // 2, False, True)
-    back = (full, full, ((3, R, D), BF16), full, HALF_BLOCKS, BIAS_ROW, GAIN_ROW)
+def run_first_attention_backward(gmix, state):
     return pl.pallas_call(
         first_attention_backward_kernel,
+        out_shape=jax.ShapeDtypeStruct((3, R, D), BF16),
+        in_specs=whole(3),
+        out_specs=whole(1)[0],
+        compiler_params=params(),
+        cost_estimate=cost(12_000_000_000),
+        name="first_attention_backward",
+    )(state[1], state[2], gmix)
+
+
+def run_first_projection_backward(me, images, grad, gqkv, rest, weights, state):
+    w, _, _, gain_row = weights
+    full = ((R, D), F32)
+    outs = [jax.ShapeDtypeStruct(images.shape, BF16)] + wires(BLOCKS // 2, False, True)
+    return pl.pallas_call(
+        first_projection_backward_kernel,
         out_shape=outs,
-        in_specs=scalar(1) + whole(11),
+        in_specs=scalar(1) + whole(9),
         out_specs=whole(len(outs)),
-        scratch_shapes=scratch(back + MOVE_SCRATCH),
+        scratch_shapes=scratch((full, full, full, HALF_BLOCKS, BIAS_ROW, GAIN_ROW) + MOVE_SCRATCH),
         compiler_params=params(),
-        cost_estimate=cost(20_000_000_000),
-        name="first_attention_backward",
-    )(me, images, *grads, w, gain_row, *state[:3])
+        cost_estimate=cost(10_000_000_000),
+        name="first_projection_backward",
+    )(me, images, grad, gqkv, *rest, w, gain_row, state[0])
 
 
 def chunk_table():
@@ -553,57 +562,55 @@
     return table
 
 
-def pack_kernel(qkv, out, fc1, fc2, gains, biases, *refs):
-    flats, slabs, stages = (qkv, out, fc1, fc2), refs[:4], refs[4:]
+def pack_kernel(qkv, out, fc1, fc2, gains, biases, slab_a, slab_b, stage_a, stage_b):
+    flats, stages = (qkv, out, fc1, fc2), (stage_a, stage_b)
     for stage in stages:
-        stage[...] = jnp.zeros_like(stage)
+        stage[SMALL:SLAB, :] = jnp.zeros((SLAB - SMALL, 128), F32)
     for which, piece, c, row in chunk_table():
         both = flats[which][:, 128 * piece : 128 * piece + 128].astype(F32)
-        row += max(c - 1, 0) * THIRD
+        row += c * THIRD
         for layer in range(LAYERS):
-            stages[2 * layer + (c == 0)][row : row + 1, :] = both[layer : layer + 1]
+            stages[layer][row : row + 1, :] = both[layer : layer + 1]
     for layer in range(LAYERS):
-        main = stages[2 * layer]
-        main[SMALL : SMALL + 1, 0:SHARD_BIAS] = biases[...].astype(F32)[layer : layer + 1]
-        main[SMALL + 1 : SMALL + 2, 0:SHARD_GAIN] = gains[...].astype(F32)[layer : layer + 1]
-    for slab, stage in zip(slabs, stages):
-        slab[...] = stage[...].astype(BF16)
+        stages[layer][SMALL : SMALL + 1, 0:SHARD_BIAS] = biases[...].astype(F32)[layer : layer + 1]
+        stages[layer][SMALL + 1 : SMALL + 2, 0:SHARD_GAIN] = gains[...].astype(F32)[layer : layer + 1]
+    slab_a[...] = stage_a[...].astype(BF16)
+    slab_b[...] = stage_b[...].astype(BF16)
 
 
 def run_pack(qkv, out, fc1, fc2, gains, biases):
-    sizes = [(MAIN, 128), (SIDE, 128)] * LAYERS
     return pl.pallas_call(
         pack_kernel,
-        out_shape=[jax.ShapeDtypeStruct(size, BF16) for size in sizes],
+        out_shape=[jax.ShapeDtypeStruct((SLAB, 128), BF16)] * 2,
         in_specs=whole(6),
-        out_specs=whole(4),
-        scratch_shapes=[pltpu.VMEM(size, F32) for size in sizes],
+        out_specs=whole(2),
+        scratch_shapes=[pltpu.VMEM((SLAB, 128), F32)] * 2,
         name="pack",
     )(qkv, out, fc1, fc2, gains, biases)
 
 
-def unpack_kernel(*refs):
-    attention, mlp, second, flats, (gains, biases) = refs[:2], refs[2:4], refs[4:6], refs[6:10], refs[10:]
+def unpack_kernel(first, second, *refs):
+    flats, (gains, biases) = refs[:4], refs[4:]
+    start = slab_rows(BLOCKS // 2, True, False)
     for which, piece, c, row in chunk_table():
         lanes = slice(128 * piece, 128 * piece + 128)
-        place = max(c - 1, 0)
-        source, at = (attention, place * 48 + row) if which < 2 else (mlp, place * 96 + row - 48)
-        flats[which][0:1, lanes] = source[c == 0][at : at + 1, :]
-        at = place * THIRD + row
-        flats[which][1:2, lanes] = second[c == 0][at : at + 1, :]
-    for layer, (main, row) in enumerate(((attention[0], 96), (second[0], SMALL))):
-        biases[layer : layer + 1, :] = main[row : row + 1, 0:SHARD_BIAS]
-        gains[layer : layer + 1, :] = main[row + 1 : row + 2, 0:SHARD_GAIN]
-
-
-def run_unpack(slabs, widths):
+        at = start + c * 48 + row if which < 2 else c * 96 + row - 48
+        flats[which][0:1, lanes] = first[at : at + 1, :]
+        at = c * THIRD + row
+        flats[which][1:2, lanes] = second[at : at + 1, :]
+    for layer, slab in enumerate((first, second)):
+        biases[layer : layer + 1, :] = slab[SMALL : SMALL + 1, 0:SHARD_BIAS]
+        gains[layer : layer + 1, :] = slab[SMALL + 1 : SMALL + 2, 0:SHARD_GAIN]
+
+
+def run_unpack(first, second, widths):
     return pl.pallas_call(
         unpack_kernel,
         out_shape=[jax.ShapeDtypeStruct((LAYERS, width), F32) for width in widths],
-        in_specs=whole(6),
+        in_specs=whole(2),
         out_specs=whole(6),
         name="unpack",
-    )(*slabs)
+    )(first, second)
 
 
 def swap(value, bits):
@@ -618,20 +625,13 @@
     return [value] + [swap(value, bits) for bits in steps]
 
 
-def gather_first(main, side):
-    return (
-        jnp.concatenate(spread(main, Z_STEPS), axis=0),
-        jnp.concatenate(spread(side, XY_STEPS), axis=0),
-    )
-
-
-def gather_second(main, side):
-    return spread(main, XY_STEPS) + spread(side, Z_STEPS)
-
-
-def gather_cores(near):
-    far = [swap(part, 1) for part in near]
-    return near[:4] + far[:4] + near[4:] + far[4:]
+def gather_tree(slab):
+    near = spread(jnp.concatenate(spread(slab, Z_STEPS), axis=0), XY_STEPS)
+    return near + [swap(part, 1) for part in near]
+
+
+def across_cores(keep, send):
+    return keep.astype(F32) + swap(send, 1).astype(F32)
 
 
 def collect(total, steps):
@@ -643,16 +643,8 @@
     return mine
 
 
-def scatter_cores(wires):
-    return [keep.astype(F32) + swap(send, 1).astype(F32) for keep, send in zip(wires[:2], wires[2:])]
-
-
-def scatter_first(main, side):
-    return [collect(main, XY_STEPS), collect(side, Z_STEPS)]
-
-
-def scatter_second(main, side):
-    return [collect(main, Z_STEPS), collect(side, XY_STEPS)]
+def join(first, second):
+    return jnp.concatenate([first.reshape(4, -1, 128), second.reshape(4, -1, 128)], axis=1).reshape(-1, 128)
 
 
 def to_slabs(qkv, out, fc1, fc2, gains, biases):
@@ -666,87 +658,91 @@
         axis=1,
     )
     thirds = blocks.reshape(SLABS, THIRD, 3, 128).transpose(0, 2, 1, 3).reshape(SLABS, 3 * THIRD, 128)
-    tail = jnp.zeros((SLABS, MAIN - SMALL, 128), blocks.dtype)
+    tail = jnp.zeros((SLABS, SLAB - SMALL, 128), blocks.dtype)
     tail = tail.at[:, 0, :SHARD_BIAS].set(biases.reshape(SLABS, SHARD_BIAS))
     tail = tail.at[:, 1, :SHARD_GAIN].set(gains.reshape(SLABS, SHARD_GAIN))
-    return jnp.concatenate([thirds[:, THIRD:], tail], axis=1), thirds[:, :THIRD]
-
-
-def from_slabs(main, side):
-    blocks = jnp.concatenate([side, main[:, :SMALL]], axis=1).reshape(SLABS, 3, THIRD, 128).transpose(0, 2, 1, 3).reshape(SLABS, THIRD, D)
+    return jnp.concatenate([thirds, tail], axis=1)
+
+
+def from_slabs(slabs):
+    blocks = slabs[:, :SMALL].reshape(SLABS, 3, THIRD, 128).transpose(0, 2, 1, 3).reshape(SLABS, THIRD, D)
     return (
         blocks[:, :36].reshape(SLABS, 3, 12, D).transpose(0, 2, 1, 3).reshape(-1),
         blocks[:, 36:48].reshape(-1),
         blocks[:, 48:96].reshape(SLABS, 4, 12, D).transpose(0, 2, 1, 3).reshape(-1),
         blocks[:, 96:].reshape(-1),
-        main[:, SMALL + 1, :SHARD_GAIN].reshape(-1),
-        main[:, SMALL, :SHARD_BIAS].reshape(-1),
+        slabs[:, SMALL + 1, :SHARD_GAIN].reshape(-1),
+        slabs[:, SMALL, :SHARD_BIAS].reshape(-1),
     )
 
 
-def plain_pieces(flats, layer):
-    main, side = to_slabs(*(lax.all_gather(flat[layer], "fsdp", axis=0, tiled=True) for flat in flats))
-    mains, sides = [], []
-    for core in range(2):
-        for xy in range(4):
-            mains.append(jnp.concatenate([main[core + 2 * xy + 8 * z] for z in range(4)], axis=0))
-        for z in range(4):
-            sides.append(jnp.concatenate([side[core + 2 * xy + 8 * z] for xy in range(4)], axis=0))
-    return mains + sides
-
-
-def plain_slabs(sent):
-    mains, sides = ([wire.reshape(4, 4, -1, 128).astype(F32) for wire in sent[part::2]] for part in range(2))
-    main = jnp.stack([mains[d & 1][(d >> 1) & 3, d >> 3] for d in range(SLABS)])
-    side = jnp.stack([sides[d & 1][d >> 3, (d >> 1) & 3] for d in range(SLABS)])
-    return main, side
-
-
-def plain_totals(main, side):
-    return [lax.psum_scatter(flat, "fsdp", scatter_dimension=0, tiled=True) for flat in from_slabs(main, side)]
-
-
-def joined_slabs(attention, mlp):
-    (main, side), (mlp_main, mlp_side) = plain_slabs(attention), plain_slabs(mlp)
-    parts = [main[:, :48], mlp_main[:, :96], main[:, 48:96], mlp_main[:, 96:], main[:, 96:]]
-    return jnp.concatenate(parts, axis=1), jnp.concatenate([side, mlp_side], axis=1)
+def plain_gather(flats, layer):
+    return to_slabs(*(lax.all_gather(flat[layer], "fsdp", axis=0, tiled=True) for flat in flats))
+
+
+def plain_pieces(slabs):
+    return [
+        jnp.concatenate([slabs[core + 2 * xy + 8 * z] for z in range(4)], axis=0)
+        for core in range(2)
+        for xy in range(4)
+    ]
+
+
+def plain_slabs(keep, send):
+    halves = [half.reshape(4, 4, -1, 128).astype(F32) for half in (keep, send)]
+    return jnp.stack([halves[d & 1][(d >> 1) & 3, d >> 3] for d in range(SLABS)])
+
+
+def plain_totals(slabs):
+    return [lax.psum_scatter(flat, "fsdp", scatter_dimension=0, tiled=True) for flat in from_slabs(slabs)]
+
+
+def joined_slabs(mlp, attention):
+    parts = []
+    for c in range(3):
+        parts += [attention[:, 48 * c : 48 * c + 48], mlp[:, 96 * c : 96 * c + 96]]
+    return jnp.concatenate(parts + [attention[:, THIRD:]], axis=1)
 
 
 def local(images, live_counts, qkv_weight, out_weight, fc1_weight, fc2_weight, norm_gains, biases, cotangent):
     flats = (qkv_weight, out_weight, fc1_weight, fc2_weight, norm_gains, biases)
-    tree = lax.axis_size("fsdp") == SLABS
-    if tree:
-        me = lax.axis_index("fsdp").astype(jnp.int32).reshape(1)
-        main_a, side_a, main_b, side_b = run_pack(*flats)
-        first_a = gather_first(main_a, side_a)
-        first_a, main_b, side_b = lax.optimization_barrier((first_a, main_b, side_b))
-        second_a = gather_second(*first_a)
-        first_b = gather_first(main_b, side_b)
-        second_a, first_b = lax.optimization_barrier((second_a, first_b))
-        pieces_a = gather_cores(second_a)
-    else:
-        me = jnp.zeros((1,), jnp.int32)
-        pieces_a, pieces_b = plain_pieces(flats, 0), plain_pieces(flats, 1)
-    stream, weights, state = run_first_forward(me, images, pieces_a)
-    if tree:
-        second_b, stream = lax.optimization_barrier((gather_second(*first_b), stream))
-        pieces_b = gather_cores(second_b)
-    activations, grad, *wires_b = run_second_layer(me, live_counts, stream, cotangent, pieces_b)
-    if not tree:
-        *grads, m0, m1, m2, m3 = run_first_mlp_backward(me, grad, weights, state)
-        input_grad, *wires_a = run_first_attention_backward(me, images, grads, weights, state)
-        totals_a = plain_totals(*joined_slabs(wires_a, (m0, m1, m2, m3)))
-        results = [jnp.stack(both) for both in zip(totals_a, plain_totals(*plain_slabs(wires_b)))]
-    else:
-        sums_b = scatter_cores(wires_b)
-        *grads, m0, m1, m2, m3 = run_first_mlp_backward(me, grad, weights, state)
-        sums_b, grads, wires_m = lax.optimization_barrier((sums_b, grads, (m0, m1, m2, m3)))
-        halves_b, sums_m = scatter_first(*sums_b), scatter_cores(wires_m)
-        input_grad, *wires_a = run_first_attention_backward(me, images, grads, weights, state)
-        halves_b, sums_m, wires_a = lax.optimization_barrier((halves_b, sums_m, wires_a))
-        slabs_b, halves_m, sums_a = scatter_second(*halves_b), scatter_first(*sums_m), scatter_cores(wires_a)
-        slabs_a, slabs_m = scatter_second(*scatter_first(*sums_a)), scatter_second(*halves_m)
-        results = run_unpack(slabs_a + slabs_m + slabs_b, [flat.shape[1] for flat in flats])
+    if lax.axis_size("fsdp") == SLABS:
+        return local_tree(images, live_counts, flats, cotangent)
+    me = jnp.zeros((1,), jnp.int32)
+    slabs_b = plain_gather(flats, 1).reshape(-1, 128)
+    stream, weights, state = run_first_forward(me, images, plain_pieces(plain_gather(flats, 0)))
+    activations, grad, *second = run_second_layer(me, live_counts, stream, cotangent, slabs_b)
+    grad, gmix, *rest, mlp_keep, mlp_send = run_first_mlp_backward(me, grad, weights, state)
+    gqkv = run_first_attention_backward(gmix, state)
+    input_grad, *attention = run_first_projection_backward(me, images, grad, gqkv, rest, weights, state)
+    first = joined_slabs(plain_slabs(mlp_keep, mlp_send), plain_slabs(*attention))
+    results = [jnp.stack(both) for both in zip(plain_totals(first), plain_totals(plain_slabs(*second)))]
+    return (activations, input_grad, *results)
+
+
+def local_tree(images, live_counts, flats, cotangent):
+    me = lax.axis_index("fsdp").astype(jnp.int32).reshape(1)
+    slab_a, slab_b = run_pack(*flats)
+    slabs_b = lax.all_gather(slab_b, "fsdp", axis=0, tiled=True)
+    stream, weights, state = run_first_forward(me, images, gather_tree(slab_a))
+    slabs_b, stream = lax.optimization_barrier((slabs_b, stream))
+    activations, grad, *second = run_second_layer(me, live_counts, stream, cotangent, slabs_b)
+
+    second = across_cores(*second)
+    grad, gmix, *rest, mlp_keep, mlp_send = run_first_mlp_backward(me, grad, weights, state)
+    second, gmix, mlp_keep, mlp_send = lax.optimization_barrier((second, gmix, mlp_keep, mlp_send))
+
+    second, mlp = collect(second, XY_STEPS), across_cores(mlp_keep, mlp_send)
+    gqkv = run_first_attention_backward(gmix, state)
+    second, mlp, gqkv = lax.optimization_barrier((second, mlp, gqkv))
+
+    second, mlp = collect(second, Z_STEPS), collect(mlp, XY_STEPS)
+    input_grad, *attention = run_first_projection_backward(me, images, grad, gqkv, rest, weights, state)
+    second, mlp, attention = lax.optimization_barrier((second, mlp, attention))
+
+    attention = collect(across_cores(*attention), XY_STEPS)
+    first = collect(join(mlp, attention), Z_STEPS)
+    results = run_unpack(first, second, [flat.shape[1] for flat in flats])
     return (activations, input_grad, *results)
 
 

time: 270 us -> 240 us (0.89)
  starting transfers between devices: 85.7 us -> 27.4 us
  waiting for transfers between devices: 43.8 us -> 65.3 us
  between operations: 1.36 us -> 14.3 us
  other arithmetic: 8.81 us -> 3.11 us
  Pallas kernels: 126 us -> 129 us
    ppermute x82 -> x28, starting transfers between devices: 85.7 us -> 27.3 us  [swap(): return lax.ppermute(value, 'fsdp', [(i, i ^ bits) for i in range(SLABS)])]
    ppermute x82 -> x28, waiting for transfers between devices: 43.8 us -> 59.4 us  [swap(): return lax.ppermute(value, 'fsdp', [(i, i ^ bits) for i in range(SLABS)])]
    all_gather x0 -> x1, waiting for transfers between devices: none -> 5.88 us  [local_tree(): slabs_b = lax.all_gather(slab_b, 'fsdp', axis=0, tiled=True)]
    concatenate x4 -> x0, other arithmetic: 3.37 us -> none  [the longest x2 1.81 us: gather_first(): jnp.concatenate(spread(main, Z_STEPS), axis=0)]
    pallas_call x2 -> x3, Pallas kernels: 22.5 us -> 24.8 us  [the longest x1 11.6 us: run_first_projection_backward(): pl.pallas_call(first_projection_backward_kernel, out_shape=outs, in_specs...]
  transfers between devices with their start and end apart: 82 -> 29, of which waited for: 28 -> 17; matrix products, arithmetic and copies ran while one was open for 3% -> 1% of each run, Pallas kernels for 25% -> 29%
where the time goes in v3:
time: 240 us
  Pallas kernels  129 us (54%)
  waiting for transfers between devices  65.3 us (27%)
  starting transfers between devices  27.4 us (11%)
  between operations  14.3 us (6%)
  other arithmetic  3.11 us (1%)
    ppermute x28, waiting for transfers between devices, swap(): return lax.ppermute(value, 'fsdp', [(i, i ^ bits) for i in range(SLABS)])  59.4 us
    pallas_call x1, Pallas kernels, run_second_layer(): pl.pallas_call(second_layer_kernel, out_shape=outs, in_specs=scalar(2) +...  55.1 us
    pallas_call x1, Pallas kernels, run_first_forward(): pl.pallas_call(first_forward_kernel, out_shape=outs, in_specs=scalar(1) +...  28.6 us
    ppermute x28, starting transfers between devices, swap(): return lax.ppermute(value, 'fsdp', [(i, i ^ bits) for i in range(SLABS)])  27.3 us
    pallas_call x1, Pallas kernels, run_first_mlp_backward(): pl.pallas_call(first_mlp_backward_kernel, out_shape=outs, in_specs=scalar...  18 us
    pallas_call x1, Pallas kernels, run_first_projection_backward(): pl.pallas_call(first_projection_backward_kernel, out_shape=outs, in_specs...  11.6 us
    pallas_call x1, Pallas kernels, run_first_attention_backward(): pl.pallas_call(first_attention_backward_kernel, out_shape=jax.ShapeDtypeS...  11.3 us
    all_gather x1, waiting for transfers between devices, local_tree(): slabs_b = lax.all_gather(slab_b, 'fsdp', axis=0, tiled=True)  5.88 us
  transfers between devices with their start and end apart: 29, of which 17 were waited for; matrix products, arithmetic and copies ran while one was open for 1% of the time, Pallas kernels for 29%

profile of v3, /device:TPU:0, one launch (start us, length us, event | category | flops | bytes accessed | tf_op | source)
XLA Modules:
  0.0 240.2 jit_solution(5773320712664322785)
XLA Ops:
  7.2 1.9 pack.1
  9.1 5.1 %collective-permute-start.2 = (bf16[448,128]{1,0:T(8,128)(2,1)}, bf16[448,128]{1,0:T(8,128)(2,1)S(1)}, u32[]{:S(2)}, u32[]{:S(2)}) collective-permute-start(bf16[448,128]{1,0:T(8,128)(2,1)} %get-tuple-element.56), channel_id=1, source_target_pairs={{0,24},{1,25},{2,26},{3,27},{4,28},{5,29},{6,30},{7,31},{8,16},{9,... | collective-permute-start | bytes 344072 | tf_op jit(solution)/shard_map/ppermute | solution.py:617
  15.8 6.1 %collective-permute-done = bf16[448,128]{1,0:T(8,128)(2,1)S(1)} collective-permute-done((bf16[448,128]{1,0:T(8,128)(2,1)}, bf16[448,128]{1,0:T(8,128)(2,1)S(1)}, u32[]{:S(2)}, u32[]{:S(2)}) %collective-permute-start) | collective-permute-done | bytes 114720 | tf_op jit(solution)/shard_map/ppermute | solution.py:617
  22.0 2.2 collective-permute-done.1
  24.2 2.5 %collective-permute-start.5 = (bf16[1792,128]{1,0:T(8,128)(2,1)S(1)}, bf16[1792,128]{1,0:T(8,128)(2,1)S(1)}, u32[]{:S(2)}, u32[]{:S(2)}) collective-permute-start(bf16[1792,128]{1,0:T(8,128)(2,1)S(1)} %constant_dynamic-update-slice_fusion.refs_2_), channel_id=1, source_target_pairs={{0,6},{1,7},{2,4},{3,5},{4,2},{5,3},{6,0},{7,1},{8,14},{9,15},{10,... | collective-permute-start | bytes 1376264 | tf_op jit(solution)/shard_map/ppermute | solution.py:617
  27.8 10.9 %collective-permute-done.5.refs_5_ = bf16[1792,128]{1,0:T(8,128)(2,1)S(1)} collective-permute-done((bf16[1792,128]{1,0:T(8,128)(2,1)S(1)}, bf16[1792,128]{1,0:T(8,128)(2,1)S(1)}, u32[]{:S(2)}, u32[]{:S(2)}) %collective-permute-start.5) | collective-permute-done | bytes 458784 | tf_op jit(solution)/shard_map/ppermute | solution.py:617
  38.7 8.2 %collective-permute-done.4.refs_4_ = bf16[1792,128]{1,0:T(8,128)(2,1)S(1)} collective-permute-done((bf16[1792,128]{1,0:T(8,128)(2,1)S(1)}, bf16[1792,128]{1,0:T(8,128)(2,1)S(1)}, u32[]{:S(2)}, u32[]{:S(2)}) %collective-permute-start.4) | collective-permute-done | bytes 458784 | tf_op jit(solution)/shard_map/ppermute | solution.py:617
  49.6 28.6 %first_forward.1 = (f32[624,384]{1,0:T(8,128)}, bf16[8,384,384]{2,1,0:T(8,128)(2,1)}, bf16[1536,384]{1,0:T(8,128)(2,1)}, f32[1,3840]{1,0:T(1,128)}, f32[1,768]{1...) custom-call(s32[1]{0:T(128)} %bitcast.refs_0_.me, ...), custom_call_target="tpu_custom_call" | custom-call | flops 32999999488 | bytes 20000000 | tf_op jit(solution)/shard_map/first_forward/pallas_call | solution.py:477
  78.1 5.9 %all-gather.2.cloned.1.call-done.refs_4_ = bf16[14336,128]{1,0:T(8,128)(2,1)} async-done(((bf16[448,128]{1,0:T(8,128)(2,1)}), bf16[14336,128]{1,0:T(8,128)(2,1)}) %all-gather.2.cloned.1.call-update) | async-done | bytes 3670032 | tf_op jit(solution)/shard_map/all_gather | solution.py:726
  84.0 55.1 %second_layer.1 = (bf16[3,197,384]{2,1,0:T(8,128)(2,1)}, f32[624,384]{1,0:T(8,128)}, bf16[7168,128]{1,0:T(8,128)(2,1)}, bf16[7168,128]{1,0:T(8,128)(2,1)}) custom-call(s32[1]{0:T(128)} %bitcast.refs_0_.me, s32[3]{0:T(128)} %refs_1_.3, f32[624,384]{1,0:T(8,128)} %get-tuple-element.58.refs_2_, bf16[3,197,384]{2,1,0:T(8,128)(2,1)} %refs_3_.1, ...), custom_call_target="tpu_custom_call" | custom-call | flops 65000001536 | bytes 20000000 | tf_op jit(solution)/shard_map/second_layer/pallas_call | solution.py:495
  139.4 18.0 %first_mlp_backward.1 = (f32[624,384]{1,0:T(8,128)}, bf16[624,384]{1,0:T(8,128)(2,1)}, bf16[384,384]{1,0:T(8,128)(2,1)}, f32[1,3840]{1,0:T(1,128)}, f32[1,768]{1...) custom-call(s32[1]{0:T(128)} %bitcast.refs_0_.me, f32[624,384]{1,0:T(8,128)} %get-tuple-element.61.grad_in, ...), custom_call_target="tpu_custom_call" | custom-call | flops 20000000000 | bytes 20000000 | tf_op jit(solution)/shard_map/first_mlp_backward/pallas_call | solution.py:511
  159.8 1.5 collective-permute-start.13
  161.9 11.3 %first_attention_backward.1.gqkv = bf16[3,624,384]{2,1,0:T(8,128)(2,1)} custom-call(bf16[3,624,384]{2,1,0:T(8,128)(2,1)} %get-tuple-element.79.qkv, bf16[18,208,208]{2,1,0:T(8,128)(2,1)} %get-tuple-element.80.probs, bf16[624,384]{1,0:T(8,128)(2,1)} %get-tuple-element.81.gmix), custom_call_target="tpu_custom_call" | custom-call | flops 12000000000 | bytes 20000000 | tf_op jit(solution)/shard_map/first_attention_backward/pallas_call | solution.py:524
  173.3 8.7 %collective-permute-done.13 = bf16[1792,128]{1,0:T(8,128)(2,1)S(1)} collective-permute-done((bf16[1792,128]{1,0:T(8,128)(2,1)S(1)}, bf16[1792,128]{1,0:T(8,128)(2,1)S(1)}, u32[]{:S(2)}, u32[]{:S(2)}) %collective-permute-start.13) | collective-permute-done | bytes 458784 | tf_op jit(solution)/shard_map/ppermute | solution.py:617
  185.1 1.6 collective-permute-start.17
  191.2 11.6 %first_projection_backward.1 = (bf16[3,197,384]{2,1,0:T(8,128)(2,1)}, bf16[2560,128]{1,0:T(8,128)(2,1)}, bf16[2560,128]{1,0:T(8,128)(2,1)}) custom-call(s32[1]{0:T(128)} %bitcast.refs_0_.me, bf16[3,197,384]{2,1,0:T(8,128)(2,1)} %images.1, f32[624,384]{1,0:T(8,128)} %get-tuple-element.70.grad_in, bf16[3,624,384]{2,1,0:T(8,128)(2,1)} %first_attention_backward.1.gqkv, ...), custom_call_target="tpu_custom_call" | custom-call | flops 10000000000 | bytes 20000000 | tf_op jit(solution)/shard_map/first_projection_backward/pallas_call | solution.py:539
  204.0 2.1 collective-permute-done.21
  209.9 3.6 %collective-permute-done.22 = bf16[640,128]{1,0:T(8,128)(2,1)S(1)} collective-permute-done((bf16[640,128]{1,0:T(8,128)(2,1)S(1)}, bf16[640,128]{1,0:T(8,128)(2,1)S(1)}, u32[]{:S(2)}, u32[]{:S(2)}) %collective-permute-start.22) | collective-permute-done | bytes 163872 | tf_op jit(solution)/shard_map/ppermute | solution.py:617
  213.4 3.7 %collective-permute-done.24 = bf16[640,128]{1,0:T(8,128)(2,1)S(1)} collective-permute-done((bf16[640,128]{1,0:T(8,128)(2,1)S(1)}, bf16[640,128]{1,0:T(8,128)(2,1)S(1)}, u32[]{:S(2)}, u32[]{:S(2)}) %collective-permute-start.24) | collective-permute-done | bytes 163872 | tf_op jit(solution)/shard_map/ppermute | solution.py:617
  219.9 1.6 collective-permute-start.27
  222.2 2.8 %collective-permute-done.25 = bf16[448,128]{1,0:T(8,128)(2,1)S(1)} collective-permute-done((bf16[448,128]{1,0:T(8,128)(2,1)S(1)}, bf16[448,128]{1,0:T(8,128)(2,1)S(1)}, u32[]{:S(2)}, u32[]{:S(2)}) %collective-permute-start.25) | collective-permute-done | bytes 114720 | tf_op jit(solution)/shard_map/ppermute | solution.py:617
  225.0 1.8 collective-permute-done.27
  226.8 3.7 %collective-permute-done.26 = bf16[448,128]{1,0:T(8,128)(2,1)S(1)} collective-permute-done((bf16[448,128]{1,0:T(8,128)(2,1)S(1)}, bf16[448,128]{1,0:T(8,128)(2,1)S(1)}, u32[]{:S(2)}, u32[]{:S(2)}) %collective-permute-start.26) | collective-permute-done | bytes 114720 | tf_op jit(solution)/shard_map/ppermute | solution.py:617
  231.2 2.1 unpack.1
  (85 shorter events, 25.3 us)
Async XLA Ops:
  7.2 76.8 %all-gather.2.cloned.1.call-start = ((), (), s32[]{:S(2)}) async-start(), calls=%async_computation | async-start | bytes 3784704 | tf_op jit(solution)/shard_map/all_gather | solution.py:726
  9.1 15.0 %collective-permute-start.2 = (bf16[448,128]{1,0:T(8,128)(2,1)}, bf16[448,128]{1,0:T(8,128)(2,1)S(1)}, u32[]{:S(2)}, u32[]{:S(2)}) collective-permute-start(bf16[448,128]{1,0:T(8,128)(2,1)} %get-tuple-element.56), channel_id=1, source_target_pairs={{0,24},{1,25},{2,26},{3,27},{4,28},{5,29},{6,30},{7,31},{8,16},{9,... | collective-permute-start | bytes 344072 | tf_op jit(solution)/shard_map/ppermute | solution.py:617
  14.3 9.9 %collective-permute-start.1 = (bf16[448,128]{1,0:T(8,128)(2,1)}, bf16[448,128]{1,0:T(8,128)(2,1)S(1)}, u32[]{:S(2)}, u32[]{:S(2)}) collective-permute-start(bf16[448,128]{1,0:T(8,128)(2,1)} %get-tuple-element.56), channel_id=1, source_target_pairs={{0,16},{1,17},{2,18},{3,19},{4,20},{5,21},{6,22},{7,23},{8,24},{9,... | collective-permute-start | bytes 344072 | tf_op jit(solution)/shard_map/ppermute | solution.py:617
  14.3 7.7 %collective-permute-start = (bf16[448,128]{1,0:T(8,128)(2,1)}, bf16[448,128]{1,0:T(8,128)(2,1)S(1)}, u32[]{:S(2)}, u32[]{:S(2)}) collective-permute-start(bf16[448,128]{1,0:T(8,128)(2,1)} %get-tuple-element.56), channel_id=1, source_target_pairs={{0,8},{1,9},{2,10},{3,11},{4,12},{5,13},{6,14},{7,15},{8,0},{9,1},... | collective-permute-start | bytes 344072 | tf_op jit(solution)/shard_map/ppermute | solution.py:617
  24.2 14.5 %collective-permute-start.5 = (bf16[1792,128]{1,0:T(8,128)(2,1)S(1)}, bf16[1792,128]{1,0:T(8,128)(2,1)S(1)}, u32[]{:S(2)}, u32[]{:S(2)}) collective-permute-start(bf16[1792,128]{1,0:T(8,128)(2,1)S(1)} %constant_dynamic-update-slice_fusion.refs_2_), channel_id=1, source_target_pairs={{0,6},{1,7},{2,4},{3,5},{4,2},{5,3},{6,0},{7,1},{8,14},{9,15},{10,... | collective-permute-start | bytes 1376264 | tf_op jit(solution)/shard_map/ppermute | solution.py:617
  26.7 20.2 %collective-permute-start.4 = (bf16[1792,128]{1,0:T(8,128)(2,1)S(1)}, bf16[1792,128]{1,0:T(8,128)(2,1)S(1)}, u32[]{:S(2)}, u32[]{:S(2)}) collective-permute-start(bf16[1792,128]{1,0:T(8,128)(2,1)S(1)} %constant_dynamic-update-slice_fusion.refs_2_), channel_id=1, source_target_pairs={{0,4},{1,5},{2,6},{3,7},{4,0},{5,1},{6,2},{7,3},{8,12},{9,13},{10,... | collective-permute-start | bytes 1376264 | tf_op jit(solution)/shard_map/ppermute | solution.py:617
  27.2 19.7 %collective-permute-start.3 = (bf16[1792,128]{1,0:T(8,128)(2,1)S(1)}, bf16[1792,128]{1,0:T(8,128)(2,1)S(1)}, u32[]{:S(2)}, u32[]{:S(2)}) collective-permute-start(bf16[1792,128]{1,0:T(8,128)(2,1)S(1)} %constant_dynamic-update-slice_fusion.refs_2_), channel_id=1, source_target_pairs={{0,2},{1,3},{2,0},{3,1},{4,6},{5,7},{6,4},{7,5},{8,10},{9,11},{10,... | collective-permute-start | bytes 1376264 | tf_op jit(solution)/shard_map/ppermute | solution.py:617
  27.8 19.7 %collective-permute-start.6 = (bf16[1792,128]{1,0:T(8,128)(2,1)S(1)}, bf16[1792,128]{1,0:T(8,128)(2,1)S(1)}, u32[]{:S(2)}, u32[]{:S(2)}) collective-permute-start(bf16[1792,128]{1,0:T(8,128)(2,1)S(1)} %constant_dynamic-update-slice_fusion.refs_2_), channel_id=1, source_target_pairs={{0,1},{1,0},{2,3},{3,2},{4,5},{5,4},{6,7},{7,6},{8,9},{9,8},{10,11... | collective-permute-start | bytes 1376264 | tf_op jit(solution)/shard_map/ppermute | solution.py:617
  38.7 8.8 %collective-permute-start.9 = (bf16[1792,128]{1,0:T(8,128)(2,1)S(1)}, bf16[1792,128]{1,0:T(8,128)(2,1)S(1)}, u32[]{:S(2)}, u32[]{:S(2)}) collective-permute-start(bf16[1792,128]{1,0:T(8,128)(2,1)S(1)} %collective-permute-done.5.refs_5_), channel_id=1, source_target_pairs={{0,1},{1,0},{2,3},{3,2},{4,5},{5,4},{6,7},{7,6},{8,9},{9,8},{10,11... | collective-permute-start | bytes 1376264 | tf_op jit(solution)/shard_map/ppermute | solution.py:617
  139.1 18.3 %collective-permute-start.10 = (bf16[7168,128]{1,0:T(8,128)(2,1)}, bf16[7168,128]{1,0:T(8,128)(2,1)S(1)}, u32[]{:S(2)}, u32[]{:S(2)}) collective-permute-start(bf16[7168,128]{1,0:T(8,128)(2,1)} %get-tuple-element.72), channel_id=1, source_target_pairs={{0,1},{1,0},{2,3},{3,2},{4,5},{5,4},{6,7},{7,6},{8,9},{9,8},{10,11... | collective-permute-start | bytes 5505032 | tf_op jit(solution)/shard_map/ppermute | solution.py:617
  157.8 25.7 %collective-permute-start.14 = (bf16[4608,128]{1,0:T(8,128)(2,1)}, bf16[4608,128]{1,0:T(8,128)(2,1)S(1)}, u32[]{:S(2)}, u32[]{:S(2)}) collective-permute-start(bf16[4608,128]{1,0:T(8,128)(2,1)} %get-tuple-element.78), channel_id=1, source_target_pairs={{0,1},{1,0},{2,3},{3,2},{4,5},{5,4},{6,7},{7,6},{8,9},{9,8},{10,11... | collective-permute-start | bytes 3538952 | tf_op jit(solution)/shard_map/ppermute | solution.py:617
  158.4 14.9 %collective-permute-start.11 = (bf16[1792,128]{1,0:T(8,128)(2,1)S(1)}, bf16[1792,128]{1,0:T(8,128)(2,1)S(1)}, u32[]{:S(2)}, u32[]{:S(2)}) collective-permute-start(bf16[1792,128]{1,0:T(8,128)(2,1)S(1)} %get-tuple-element.102), channel_id=1, source_target_pairs={{0,2},{1,3},{2,0},{3,1},{4,6},{5,7},{6,4},{7,5},{8,10},{9,11},{10,... | collective-permute-start | bytes 1376264 | tf_op jit(solution)/shard_map/ppermute | solution.py:617
  159.8 22.1 %collective-permute-start.13 = (bf16[1792,128]{1,0:T(8,128)(2,1)S(1)}, bf16[1792,128]{1,0:T(8,128)(2,1)S(1)}, u32[]{:S(2)}, u32[]{:S(2)}) collective-permute-start(bf16[1792,128]{1,0:T(8,128)(2,1)S(1)} %get-tuple-element.103), channel_id=1, source_target_pairs={{0,6},{1,7},{2,4},{3,5},{4,2},{5,3},{6,0},{7,1},{8,14},{9,15},{10,... | collective-permute-start | bytes 1376264 | tf_op jit(solution)/shard_map/ppermute | solution.py:617
  161.3 22.0 %collective-permute-start.12 = (bf16[1792,128]{1,0:T(8,128)(2,1)S(1)}, bf16[1792,128]{1,0:T(8,128)(2,1)S(1)}, u32[]{:S(2)}, u32[]{:S(2)}) collective-permute-start(bf16[1792,128]{1,0:T(8,128)(2,1)S(1)} %get-tuple-element.104), channel_id=1, source_target_pairs={{0,4},{1,5},{2,6},{3,7},{4,0},{5,1},{6,2},{7,3},{8,12},{9,13},{10,... | collective-permute-start | bytes 1376264 | tf_op jit(solution)/shard_map/ppermute | solution.py:617
  185.1 17.7 %collective-permute-start.17 = (bf16[448,128]{1,0:T(8,128)(2,1)S(1)}, bf16[448,128]{1,0:T(8,128)(2,1)S(1)}, u32[]{:S(2)}, u32[]{:S(2)}) collective-permute-start(bf16[448,128]{1,0:T(8,128)(2,1)S(1)} %get-tuple-element.117), channel_id=1, source_target_pairs={{0,24},{1,25},{2,26},{3,27},{4,28},{5,29},{6,30},{7,31},{8,16},{9,... | collective-permute-start | bytes 344072 | tf_op jit(solution)/shard_map/ppermute | solution.py:617
  186.8 16.1 %collective-permute-start.16 = (bf16[448,128]{1,0:T(8,128)(2,1)S(1)}, bf16[448,128]{1,0:T(8,128)(2,1)S(1)}, u32[]{:S(2)}, u32[]{:S(2)}) collective-permute-start(bf16[448,128]{1,0:T(8,128)(2,1)S(1)} %get-tuple-element.118), channel_id=1, source_target_pairs={{0,16},{1,17},{2,18},{3,19},{4,20},{5,21},{6,22},{7,23},{8,24},{9,... | collective-permute-start | bytes 344072 | tf_op jit(solution)/shard_map/ppermute | solution.py:617
  187.6 15.9 %collective-permute-start.18 = (bf16[1152,128]{1,0:T(8,128)(2,1)S(1)}, bf16[1152,128]{1,0:T(8,128)(2,1)S(1)}, u32[]{:S(2)}, u32[]{:S(2)}) collective-permute-start(bf16[1152,128]{1,0:T(8,128)(2,1)S(1)} %get-tuple-element.107), channel_id=1, source_target_pairs={{0,2},{1,3},{2,0},{3,1},{4,6},{5,7},{6,4},{7,5},{8,10},{9,11},{10,... | collective-permute-start | bytes 884744 | tf_op jit(solution)/shard_map/ppermute | solution.py:617
  188.3 15.3 %collective-permute-start.20 = (bf16[1152,128]{1,0:T(8,128)(2,1)S(1)}, bf16[1152,128]{1,0:T(8,128)(2,1)S(1)}, u32[]{:S(2)}, u32[]{:S(2)}) collective-permute-start(bf16[1152,128]{1,0:T(8,128)(2,1)S(1)} %get-tuple-element.108), channel_id=1, source_target_pairs={{0,6},{1,7},{2,4},{3,5},{4,2},{5,3},{6,0},{7,1},{8,14},{9,15},{10,... | collective-permute-start | bytes 884744 | tf_op jit(solution)/shard_map/ppermute | solution.py:617
  190.6 13.0 %collective-permute-start.19 = (bf16[1152,128]{1,0:T(8,128)(2,1)S(1)}, bf16[1152,128]{1,0:T(8,128)(2,1)S(1)}, u32[]{:S(2)}, u32[]{:S(2)}) collective-permute-start(bf16[1152,128]{1,0:T(8,128)(2,1)S(1)} %get-tuple-element.109), channel_id=1, source_target_pairs={{0,4},{1,5},{2,6},{3,7},{4,0},{5,1},{6,2},{7,3},{8,12},{9,13},{10,... | collective-permute-start | bytes 884744 | tf_op jit(solution)/shard_map/ppermute | solution.py:617
  206.3 7.1 %collective-permute-start.22 = (bf16[640,128]{1,0:T(8,128)(2,1)S(1)}, bf16[640,128]{1,0:T(8,128)(2,1)S(1)}, u32[]{:S(2)}, u32[]{:S(2)}) collective-permute-start(bf16[640,128]{1,0:T(8,128)(2,1)S(1)} %get-tuple-element.110), channel_id=1, source_target_pairs={{0,2},{1,3},{2,0},{3,1},{4,6},{5,7},{6,4},{7,5},{8,10},{9,11},{10,... | collective-permute-start | bytes 491528 | tf_op jit(solution)/shard_map/ppermute | solution.py:617
  207.7 9.3 %collective-permute-start.24 = (bf16[640,128]{1,0:T(8,128)(2,1)S(1)}, bf16[640,128]{1,0:T(8,128)(2,1)S(1)}, u32[]{:S(2)}, u32[]{:S(2)}) collective-permute-start(bf16[640,128]{1,0:T(8,128)(2,1)S(1)} %get-tuple-element.111), channel_id=1, source_target_pairs={{0,6},{1,7},{2,4},{3,5},{4,2},{5,3},{6,0},{7,1},{8,14},{9,15},{10,... | collective-permute-start | bytes 491528 | tf_op jit(solution)/shard_map/ppermute | solution.py:617
  209.3 9.2 %collective-permute-start.23 = (bf16[640,128]{1,0:T(8,128)(2,1)S(1)}, bf16[640,128]{1,0:T(8,128)(2,1)S(1)}, u32[]{:S(2)}, u32[]{:S(2)}) collective-permute-start(bf16[640,128]{1,0:T(8,128)(2,1)S(1)} %get-tuple-element.112), channel_id=1, source_target_pairs={{0,4},{1,5},{2,6},{3,7},{4,0},{5,1},{6,2},{7,3},{8,12},{9,13},{10,... | collective-permute-start | bytes 491528 | tf_op jit(solution)/shard_map/ppermute | solution.py:617
  219.9 6.9 %collective-permute-start.27 = (bf16[448,128]{1,0:T(8,128)(2,1)S(1)}, bf16[448,128]{1,0:T(8,128)(2,1)S(1)}, u32[]{:S(2)}, u32[]{:S(2)}) collective-permute-start(bf16[448,128]{1,0:T(8,128)(2,1)S(1)} %get-tuple-element.114), channel_id=1, source_target_pairs={{0,24},{1,25},{2,26},{3,27},{4,28},{5,29},{6,30},{7,31},{8,16},{9,... | collective-permute-start | bytes 344072 | tf_op jit(solution)/shard_map/ppermute | solution.py:617
  221.5 9.0 %collective-permute-start.26 = (bf16[448,128]{1,0:T(8,128)(2,1)S(1)}, bf16[448,128]{1,0:T(8,128)(2,1)S(1)}, u32[]{:S(2)}, u32[]{:S(2)}) collective-permute-start(bf16[448,128]{1,0:T(8,128)(2,1)S(1)} %get-tuple-element.115), channel_id=1, source_target_pairs={{0,16},{1,17},{2,18},{3,19},{4,20},{5,21},{6,22},{7,23},{8,24},{9,... | collective-permute-start | bytes 344072 | tf_op jit(solution)/shard_map/ppermute | solution.py:617
  (16 other events, 98.7 us)
Sparse Core Ops, SparseCore 0:
  11.4 72.5 all-gather.1
